TPU v7x, 128 devices: a whole 4x4x4 slice. The times are simulated.
128 devices in a mesh: dp: 64 (over x, y, z), cores: 2 (over core).
Axes of the slice: x: 4, y: 4, z: 4, core: 2. Of those that a mesh axis runs over, the one named last changes fastest.
Arguments:
- queries: bfloat16 [65536, 1024], P(('dp', 'cores')), may hold values from -4 to 4
- passages: bfloat16 [65536, 1024], P(('dp', 'cores')), may hold values from -4 to 4
- positives: int32 [128, 512], P(('dp', 'cores')), may hold values from 0 to 511, each once within a row
- pair_blocks: int32 [128, 8], P(('dp', 'cores')), may hold values from 0 to 127, as said below
- negative_pair_count: int32 [128], P(('dp', 'cores')), may hold values from 1 to 8, as said below
Outputs:
- query_loss: float32 [128, 512], P(('dp', 'cores'))
- passage_loss: float32 [128, 512], P(('dp', 'cores'))
- query_grad: float32 [65536, 1024], P(('dp', 'cores'))
- passage_grad: float32 [65536, 1024], P(('dp', 'cores'))
Inputs may be any that keep to these rules, and one draw needn't show every extreme that they name: `pair_blocks`: row b lists 8 different blocks, each (b + o) mod 128 with 1 <= |o| <= 4, so every block within 4 of b in cyclic order appears once. `negative_pair_count`: some block has 8 hard negatives and some block has 1 in every draw.
All inputs are finite; a program needn't handle non-finite values.
Results may differ from a plain program's by a relative error of at most 0.0022.
Values may be sent and summed in bfloat16 or wider, within the bound.
No kernel may reach another device: no remote copies, remote signals or barrier semaphores. Data moves between devices by JAX's collectives and lax.ppermute only.
A program may use at most 128 MiB of HBM per device.

v0:
```python
import functools

import jax
import jax.numpy as jnp
from jax import lax
from jax.experimental import pallas as pl
from jax.experimental.pallas import tpu as pltpu
from jax.sharding import PartitionSpec as P

AXES = ("dp", "cores")
LOGIT = 20.0
FAR = -1e30
BLK = 512
WIDTH = 1024
MIB = 1 << 20
SLOTS = dict(own=0, s0=1, a=2, sa=-1, sb=3, b=-2, r2=4, s2=-3, r3=-4)
NAMES = tuple(SLOTS)
GROUPS = (("own", "s0"), ("a", "sa"), ("sb", "b"), ("r2", "s2"), ("r3",))
PLACE = {name: i for i, name in enumerate(NAMES)}
SPOT = {name: (g, i) for g, names in enumerate(GROUPS) for i, name in enumerate(names)}
BACK = dict(own="own", s0="s0", a="b", b="a", r2="r3", r3="r2", sa="sa", sb="sb", s2="s2")
MESSAGE = dict(
    own=(0, 0), s0=(0, 1), b=(1, 0), sa=(1, 1), sb=(2, 0), a=(2, 1), r3=(3, 0), s2=(3, 1), r2=(4, 1)
)

VMEM = pl.BlockSpec(memory_space=pltpu.VMEM)
SMEM = pl.BlockSpec(memory_space=pltpu.SMEM)
HBM = pl.BlockSpec(memory_space=pltpu.HBM)
FREE = pl.CostEstimate(flops=0, bytes_accessed=0, transcendentals=0)
LIMIT = pltpu.CompilerParams(vmem_limit_bytes=16 * MIB)


def split(value, by_core0, by_core1):
    n = lax.axis_size(AXES)
    pairs = [(i, (i + 2 * (by_core1 if i % 2 else by_core0)) % n) for i in range(n)]
    return lax.ppermute(value, AXES, pairs)


def swap(value):
    n = lax.axis_size(AXES)
    return lax.ppermute(value, AXES, [(i, i ^ 1) for i in range(n)])


def after(value, *others):
    return lax.optimization_barrier((value,) + others)[0]


def small(*lead):
    return jax.ShapeDtypeStruct(lead + (8, BLK), jnp.float32)


def call(kernel, name, outs, *operands, first=VMEM):
    return pl.pallas_call(
        kernel,
        in_specs=[first] + [VMEM] * (len(operands) - 1),
        out_specs=jax.tree.map(lambda _: VMEM, outs),
        out_shape=outs,
        compiler_params=LIMIT,
        cost_estimate=FREE,
        name=name,
    )(*operands)


def column_of(row):
    return jnp.transpose(jnp.broadcast_to(row, (128, row.shape[1])))[:, 0:1]


def rows_of(*columns):
    lane = lax.broadcasted_iota(jnp.int32, (columns[0].shape[0], 128), 1)
    packed = jnp.zeros(lane.shape, jnp.float32)
    for i, column in enumerate(columns):
        packed = jnp.where(lane == i, column, packed)
    return jnp.transpose(packed)[0:8]


def scores_of(rows, columns):
    return LOGIT * lax.dot_general(
        rows, columns, (((1,), (1,)), ((), ())), preferred_element_type=jnp.float32
    )


def chosen_of(positives):
    return column_of(positives[...].astype(jnp.float32)).astype(jnp.int32)


def pair_kernel(mine, peer, out):
    out[0] = mine[...]
    out[1] = peer[...]


def pair(mine, peer):
    return call(pair_kernel, "pair", jax.ShapeDtypeStruct((2,) + mine.shape, mine.dtype), mine, peer)


def stats_kernel(names, flags, positives, queries, *refs):
    passages, (scores, stats) = refs[:-2], refs[-2:]
    for i, name in enumerate(names):
        s = scores_of(queries[...], passages[i][...])
        scores[i] = s
        row_top = jnp.max(s, axis=1, keepdims=True)
        row_total = jnp.sum(jnp.exp(s - row_top), axis=1, keepdims=True)
        col_top = jnp.max(s, axis=0, keepdims=True)
        col_total = jnp.sum(jnp.exp(s - col_top), axis=0, keepdims=True)
        if name == "own":
            hit = jnp.where(lax.broadcasted_iota(jnp.int32, s.shape, 1) == chosen_of(positives), s, 0.0)
            packed = rows_of(row_top, row_total, jnp.sum(hit, axis=1, keepdims=True))
            stats[i, 0:2] = packed[0:2]
            stats[i, 2:3] = col_top
            stats[i, 3:4] = col_total
            stats[i, 4:5] = packed[2:3]
            stats[i, 5:6] = jnp.sum(hit, axis=0, keepdims=True)
        else:
            here = flags[PLACE[name]] > 0
            packed = rows_of(row_top, row_total)
            stats[i, 0:1] = jnp.where(here, packed[0:1], FAR)
            stats[i, 1:2] = jnp.where(here, packed[1:2], 0.0)
            stats[i, 2:3] = jnp.where(here, col_top, FAR)
            stats[i, 3:4] = jnp.where(here, col_total, 0.0)


def stats_of(g, flags, positives, queries, passages):
    n = len(GROUPS[g])
    outs = [jax.ShapeDtypeStruct((n, BLK, BLK), jnp.float32), small(n)]
    kernel = functools.partial(stats_kernel, GROUPS[g])
    return call(kernel, "stats%d" % g, outs, flags, positives, queries, *passages, first=SMEM)


def merged(parts, at):
    tops, totals = [p[at : at + 1] for p in parts], [p[at + 1 : at + 2] for p in parts]
    top = functools.reduce(jnp.maximum, tops)
    return top, sum(total * jnp.exp(t - top) for t, total in zip(tops, totals))


def merge_into(out, *parts):
    out[2:3], out[3:4] = merged(parts, 2)


def near_kernel(st1, peer1, st2, peer2, st3, peer3, peer4, out):
    merge_into(out.at[0], st1.at[0], peer1.at[1])
    merge_into(out.at[1], st2.at[0], peer2.at[1])
    merge_into(out.at[2], st3.at[0], peer3.at[1])
    out[3] = peer4[0]


def home_kernel(st0, one, two, mine, theirs):
    merge_into(mine, st0.at[0], one.at[0], two.at[2])
    merge_into(theirs, st0.at[1], one.at[1], two.at[3])


def lse_kernel(flags, *refs):
    stats, mine, peer, pay, query_loss, passage_loss = refs[:5], *refs[5:]
    top, total = merged([stats[SPOT[name][0]].at[SPOT[name][1]] for name in NAMES], 0)
    row_lse = top + jnp.log(total)
    top, total = merged([mine, peer], 2)
    col_lse = top + jnp.log(total)
    query_loss[...] = row_lse - stats[0][0, 4:5]
    passage_loss[...] = col_lse - stats[0][0, 5:6]
    lane = lax.broadcasted_iota(jnp.int32, (1, BLK), 1)
    here = jnp.zeros((1, BLK), jnp.float32)
    for i in range(9):
        here = jnp.where(lane == i, flags[i].astype(jnp.float32), here)
    pay[0:1] = row_lse
    pay[1:2] = col_lse
    pay[2:3] = here


def block_of(arrays, spot):
    return arrays[spot[0]] if spot[1] is None else arrays[spot[0]].at[spot[1]]


def tscores_kernel(passages, queries, out):
    for i in range(out.shape[0]):
        out[i] = scores_of(passages[...], queries[i])


def tscores_of(passages, queries):
    out = jax.ShapeDtypeStruct((queries.shape[0], BLK, BLK), jnp.float32)
    return call(tscores_kernel, "tscores", out, passages, queries)


def grad_kernel(names, passage_side, at, scores_at, has_total, sizes, *refs):
    n = len(names)
    flags, positives = refs[:2]
    messages, refs = refs[2:7], refs[7:]
    others, refs = refs[: sizes[0]], refs[sizes[0] :]
    scores, refs = refs[: sizes[1]], refs[sizes[1] :]
    if not scores:
        own, refs = refs[0], refs[1:]
    if has_total:
        earlier, refs = refs[0], refs[1:]
    out, total, out_sem = refs
    own_lse = column_of(messages[0][0, 1:2] if passage_side else messages[0][0, 0:1])
    lane = lax.broadcasted_iota(jnp.int32, (1, BLK), 1)
    sent = []
    for i, name in enumerate(names):
        message, which = MESSAGE[name]
        pay = messages[message].at[which]
        other = block_of(others, at[i])
        s = block_of(scores, scores_at[i])[...] if scores else scores_of(own[...], other[...])
        weight = jnp.exp(s - own_lse) + jnp.exp(s - (pay[0:1] if passage_side else pay[1:2]))
        if name == "own":
            if passage_side:
                hit = lax.broadcasted_iota(jnp.int32, s.shape, 0) == positives[...]
            else:
                hit = lax.broadcasted_iota(jnp.int32, s.shape, 1) == chosen_of(positives)
            weight = LOGIT * jnp.where(hit, weight - 2.0, weight)
        else:
            if passage_side:
                lanes = jnp.where(lane == PLACE[BACK[name]], pay[2:3], 0.0)
                here = jnp.broadcast_to(jnp.sum(lanes, axis=1, keepdims=True), lane.shape) > 0.5
            else:
                here = flags[PLACE[name]] > 0
            weight = jnp.where(here, LOGIT * weight, 0.0)
        weight = weight.astype(jnp.bfloat16)
        last = i == n - 1
        step = WIDTH // 4 if last else WIDTH
        for start in range(0, WIDTH, step):
            span = slice(start, start + step)
            part = jnp.dot(weight, other[:, span], preferred_element_type=jnp.float32)
            if i > 0:
                total[:, span] += part
            else:
                total[:, span] = earlier[:, span] + part if has_total else part
            if last:
                copy = pltpu.make_async_copy(total.at[:, span], out.at[:, span], out_sem.at[start // step])
                copy.start()
                sent.append(copy)
    for copy in sent:
        copy.wait()


def grad(names, passage_side, flags, positives, messages, others, at, scores=(), scores_at=(), own=None, earlier=None):
    operands = [flags, positives, *messages, *others, *scores]
    operands += [] if scores else [own]
    operands += [] if earlier is None else [earlier]
    sizes = (len(others), len(scores))
    return pl.pallas_call(
        functools.partial(grad_kernel, names, passage_side, at, scores_at, earlier is not None, sizes),
        in_specs=[SMEM] + [VMEM] * (len(operands) - 1),
        out_specs=HBM,
        out_shape=jax.ShapeDtypeStruct((BLK, WIDTH), jnp.float32),
        scratch_shapes=[pltpu.VMEM((BLK, WIDTH), jnp.float32), pltpu.SemaphoreType.DMA((4,))],
        compiler_params=LIMIT,
        cost_estimate=FREE,
        name="grad_" + ("p_" if passage_side else "q_") + names[0],
    )(*operands)


def body(queries, passages, positives, pair_blocks, negative_pair_count):
    blocks = lax.axis_size(AXES)
    sign = 1 - 2 * lax.axis_index("cores")
    offsets = jnp.array([SLOTS[name] for name in NAMES], jnp.int32)
    targets = (lax.axis_index(AXES) + sign * offsets) % blocks
    used = jnp.arange(pair_blocks.shape[1], dtype=jnp.int32) < negative_pair_count[0]
    listed = jnp.any((pair_blocks == targets[:, None]) & used[None, :], axis=1)
    flags = (listed | (offsets == 0)).astype(jnp.int32)

    v = dict(flags=flags, pos=positives, q=queries, p=passages)

    def fence():
        keys = sorted(v)
        v.update(zip(keys, lax.optimization_barrier(tuple(v[key] for key in keys))))

    def stat(g):
        v["s%d" % g], v["st%d" % g] = stats_of(
            g, v["flags"], v["pos"], v["q"], [v["p_" + name] for name in GROUPS[g]]
        )

    def group_of(what):
        return [v["%s%d" % (what, g)] for g in range(5)]

    v["p_own"] = v.pop("p")
    v["p_s0"], v["q_s0"] = swap(v["p_own"]), swap(v["q"])
    v["p_a"], v["p_sb"] = split(v["p_own"], -1, 1), split(v["p_s0"], -1, 1)
    stat(0)
    fence()
    p_r2, p_r4 = split(v["p_a"], -1, 1), split(v["p_sb"], -1, 1)
    v["p_sa"], v["p_b"] = swap(v["p_a"]), swap(v["p_sb"])
    stat(1)
    stat(2)
    v["x1"], v["x2"] = swap(v["st1"]), swap(v["st2"])
    v["q0"] = pair(v["q"], v["q_s0"])
    q1 = split(after(v["q0"], v["st1"]), -1, 1)
    v["p_r2"], v["p_r4"] = p_r2, p_r4
    fence()
    v["p_s2"], v["p_r3"] = swap(v["p_r2"]), swap(v["p_r4"])
    stat(3)
    stat(4)
    x3, x4 = swap(v["st3"]), swap(v["st4"])
    near = call(near_kernel, "near", small(4), v["st1"], v["x1"], v["st2"], v["x2"], v["st3"], x3, x4)
    v["one"] = split(near, 1, -1)
    v["two"] = split(v["one"], 1, -1)
    v["t0"] = tscores_of(v["p_own"], v["q0"])
    v["q1"] = q1
    fence()
    v["q3"] = split(v["q1"], -1, 1)
    v["q2"] = swap(v["q1"])
    mine, theirs = call(home_kernel, "home", [small()] * 2, v["st0"], v["one"], v["two"])
    line = jax.ShapeDtypeStruct((1, BLK), jnp.float32)
    pay, query_loss, passage_loss = call(
        lse_kernel, "lse", [small(), line, line], v["flags"], *group_of("st"), mine, swap(theirs), first=SMEM
    )
    m0 = pair(pay, swap(pay))
    m1 = split(m0, 1, -1)
    m3 = split(m1, 1, -1)
    messages = [m0, m1, swap(m1), m3, swap(m3)]
    query_grad = grad(
        NAMES, False, v["flags"], v["pos"], messages, [v["p_" + name] for name in NAMES],
        [(i, None) for i in range(9)], group_of("s"), [SPOT[name] for name in NAMES],
    )
    early, late = ("own", "s0", "a", "sb", "sa", "b"), ("r2", "s2", "r3")
    spots = [(i // 2, i % 2) for i in range(6)]
    scores = [v["t0"], tscores_of(v["p_own"], v["q1"]), tscores_of(v["p_own"], v["q2"])]
    total = grad(
        early, True, v["flags"], v["pos"], messages, [v["q0"], v["q1"], v["q2"]], spots, scores, spots
    )
    q4 = swap(after(v["q3"], query_grad))
    passage_grad = grad(
        late, True, v["flags"], v["pos"], messages, [v["q3"], q4], [(0, 0), (1, 0), (1, 1)],
        own=v["p_own"], earlier=total,
    )
    return (query_loss, passage_loss, query_grad, passage_grad)


def solution(mesh):
    spec = P(AXES, None)
    return jax.shard_map(
        body,
        mesh=mesh,
        in_specs=(spec, spec, spec, spec, P(AXES)),
        out_specs=(spec, spec, spec, spec),
        check_vma=False,
    )
```

profile of v0, /device:TPU:0, one launch (start us, length us, event | category | flops | bytes accessed | tf_op | source)
XLA Modules:
  0.0 142.6 jit_solution(14834387101168367551)
XLA Ops:
  0.7 8.8 %collective-permute-start = (bf16[512,1024]{1,0:T(8,128)(2,1)}, bf16[512,1024]{1,0:T(8,128)(2,1)S(1)}, u32[]{:S(2)}, u32[]{:S(2)}) collective-permute-start(bf16[512,1024]{1,0:T(8,128)(2,1)} %refs_9_), channel_id=1, source_target_pairs={{0,126},{1,3},{2,0},{3,5},{4,2},{5,7},{6,4},{7,9},{8,6},{9,11},{10... | collective-permute-start | bytes 3145736 | tf_op jit(solution)/shard_map/ppermute | solution.py:36
  9.6 2.8 %collective-permute-start.2 = (bf16[512,1024]{1,0:T(8,128)(2,1)S(1)}, bf16[512,1024]{1,0:T(8,128)(2,1)S(1)}, u32[]{:S(2)}, u32[]{:S(2)}) collective-permute-start(bf16[512,1024]{1,0:T(8,128)(2,1)S(1)} %collective-permute-done.1.refs_1_.refs_8_), channel_id=1, source_target_pairs={{0,126},{1,3},{2,0},{3,5},{4,2},{5,7},{6,4},{7,9},{8,6},{9,11},{10... | collective-permute-start | bytes 3145736 | tf_op jit(solution)/shard_map/ppermute | solution.py:36
  18.2 2.9 %stats0.1 = (f32[2,512,512]{2,1,0:T(8,128)S(1)}, f32[2,8,512]{2,1,0:T(8,128)S(1)}) custom-call(s32[9]{0:T(128)S(1)} %or_convert_fusion.flags.refs_0_, s32[1,512]{1,0:T(1,128)S(1)} %copy-done.4, bf16[512,1024]{1,0:T(8,128)(2,1)S(1)} %copy-done, bf16[512,1024]{1,0:T(8,128)(2,1)S(1)} %copy-done.2, bf16[512,1024]{1,0:T(8,128)(2,1)S(1)} %collective-permute-done.1.refs_1_.refs_8_), custom_call_target="tpu_custom_call" | custom-call | tf_op jit(solution)/shard_map/stats0/pallas_call | solution.py:53
  22.2 11.1 %collective-permute-done.2.refs_0_.refs_11_ = bf16[512,1024]{1,0:T(8,128)(2,1)S(1)} collective-permute-done((bf16[512,1024]{1,0:T(8,128)(2,1)S(1)}, bf16[512,1024]{1,0:T(8,128)(2,1)S(1)}, u32[]{:S(2)}, u32[]{:S(2)}) %collective-permute-start.2) | collective-permute-done | bytes 1048608 | tf_op jit(solution)/shard_map/ppermute | solution.py:36
  33.8 7.9 %collective-permute-start.5 = (bf16[512,1024]{1,0:T(8,128)(2,1)S(1)}, bf16[512,1024]{1,0:T(8,128)(2,1)S(1)}, u32[]{:S(2)}, u32[]{:S(2)}) collective-permute-start(bf16[512,1024]{1,0:T(8,128)(2,1)S(1)} %collective-permute-done.refs_0_.refs_9_), channel_id=1, source_target_pairs={{0,126},{1,3},{2,0},{3,5},{4,2},{5,7},{6,4},{7,9},{8,6},{9,11},{10... | collective-permute-start | bytes 3145736 | tf_op jit(solution)/shard_map/ppermute | solution.py:36
  41.8 1.4 pair.2.queries.refs_7_
  43.2 2.7 %stats1.1 = (f32[2,512,512]{2,1,0:T(8,128)S(1)}, f32[2,8,512]{2,1,0:T(8,128)S(1)}) custom-call(s32[9]{0:T(128)S(1)} %or_convert_fusion.flags.refs_0_, s32[1,512]{1,0:T(1,128)S(1)} %copy-done.4, bf16[512,1024]{1,0:T(8,128)(2,1)S(1)} %copy-done.1, bf16[512,1024]{1,0:T(8,128)(2,1)S(1)} %collective-permute-done.refs_0_.refs_9_, ...), custom_call_target="tpu_custom_call" | custom-call | tf_op jit(solution)/shard_map/stats1/pallas_call | solution.py:53
  46.6 2.7 %stats2.1 = (f32[2,512,512]{2,1,0:T(8,128)S(1)}, f32[2,8,512]{2,1,0:T(8,128)S(1)}) custom-call(s32[9]{0:T(128)S(1)} %or_convert_fusion.flags.refs_0_, s32[1,512]{1,0:T(1,128)S(1)} %copy-done.4, bf16[512,1024]{1,0:T(8,128)(2,1)S(1)} %copy-done.1, bf16[512,1024]{1,0:T(8,128)(2,1)S(1)} %collective-permute-done.2.refs_0_.refs_11_, ...), custom_call_target="tpu_custom_call" | custom-call | tf_op jit(solution)/shard_map/stats2/pallas_call | solution.py:53
  49.8 4.2 %collective-permute-done.5.refs_0_.refs_13_ = bf16[512,1024]{1,0:T(8,128)(2,1)S(1)} collective-permute-done((bf16[512,1024]{1,0:T(8,128)(2,1)S(1)}, bf16[512,1024]{1,0:T(8,128)(2,1)S(1)}, u32[]{:S(2)}, u32[]{:S(2)}) %collective-permute-start.5) | collective-permute-done | bytes 1048608 | tf_op jit(solution)/shard_map/ppermute | solution.py:36
  54.1 11.2 %collective-permute-done.6 = bf16[512,1024]{1,0:T(8,128)(2,1)S(1)} collective-permute-done((bf16[512,1024]{1,0:T(8,128)(2,1)S(1)}, bf16[512,1024]{1,0:T(8,128)(2,1)S(1)}, u32[]{:S(2)}, u32[]{:S(2)}) %collective-permute-start.6) | collective-permute-done | bytes 1048608 | tf_op jit(solution)/shard_map/ppermute | solution.py:36
  65.9 2.1 %collective-permute-done.10.refs_1_.refs_14_ = bf16[512,1024]{1,0:T(8,128)(2,1)S(1)} collective-permute-done((bf16[512,1024]{1,0:T(8,128)(2,1)S(1)}, bf16[512,1024]{1,0:T(8,128)(2,1)S(1)}, u32[]{:S(2)}, u32[]{:S(2)}) %collective-permute-start.10) | collective-permute-done | bytes 1048608 | tf_op jit(solution)/shard_map/ppermute | solution.py:41
  68.0 2.7 %stats3.1 = (f32[2,512,512]{2,1,0:T(8,128)S(1)}, f32[2,8,512]{2,1,0:T(8,128)S(1)}) custom-call(s32[9]{0:T(128)S(1)} %or_convert_fusion.flags.refs_0_, s32[1,512]{1,0:T(1,128)S(1)} %copy-done.4, bf16[512,1024]{1,0:T(8,128)(2,1)S(1)} %copy-done.1, bf16[512,1024]{1,0:T(8,128)(2,1)S(1)} %collective-permute-done.5.refs_0_.refs_13_, ...), custom_call_target="tpu_custom_call" | custom-call | tf_op jit(solution)/shard_map/stats3/pallas_call | solution.py:53
  71.1 1.7 %stats4.1 = (f32[1,512,512]{2,1,0:T(8,128)S(1)}, f32[1,8,512]{2,1,0:T(8,128)S(1)}) custom-call(s32[9]{0:T(128)S(1)} %or_convert_fusion.flags.refs_0_, s32[1,512]{1,0:T(1,128)S(1)} %copy-done.4, bf16[512,1024]{1,0:T(8,128)(2,1)S(1)} %copy-done.1, bf16[512,1024]{1,0:T(8,128)(2,1)S(1)} %collective-permute-done.12.refs_0_.refs_15_), custom_call_target="tpu_custom_call" | custom-call | tf_op jit(solution)/shard_map/stats4/pallas_call | solution.py:53
  74.2 10.9 %collective-permute-done.14.one = f32[4,8,512]{2,1,0:T(8,128)S(1)} collective-permute-done((f32[4,8,512]{2,1,0:T(8,128)S(1)}, f32[4,8,512]{2,1,0:T(8,128)S(1)}, u32[]{:S(2)}, u32[]{:S(2)}) %collective-permute-start.14) | collective-permute-done | bytes 65568 | tf_op jit(solution)/shard_map/ppermute | solution.py:36
  86.4 8.4 %collective-permute-done.16.two = f32[4,8,512]{2,1,0:T(8,128)S(1)} collective-permute-done((f32[4,8,512]{2,1,0:T(8,128)S(1)}, f32[4,8,512]{2,1,0:T(8,128)S(1)}, u32[]{:S(2)}, u32[]{:S(2)}) %collective-permute-start.16) | collective-permute-done | bytes 65568 | tf_op jit(solution)/shard_map/ppermute | solution.py:36
  94.8 1.6 %collective-permute-start.23 = (bf16[2,512,1024]{2,1,0:T(8,128)(2,1)S(1)}, bf16[2,512,1024]{2,1,0:T(8,128)(2,1)S(1)}, u32[]{:S(2)}, u32[]{:S(2)}) collective-permute-start(bf16[2,512,1024]{2,1,0:T(8,128)(2,1)S(1)} %collective-permute-done.15.queries.refs_8_), channel_id=1, source_target_pairs={{0,126},{1,3},{2,0},{3,5},{4,2},{5,7},{6,4},{7,9},{8,6},{9,11},{10... | collective-permute-start | bytes 6291464 | tf_op jit(solution)/shard_map/ppermute | solution.py:36
  100.5 9.3 %collective-permute-done.19.refs_3_ = f32[2,8,512]{2,1,0:T(8,128)S(1)} collective-permute-done((f32[2,8,512]{2,1,0:T(8,128)S(1)}, f32[2,8,512]{2,1,0:T(8,128)S(1)}, u32[]{:S(2)}, u32[]{:S(2)}) %collective-permute-start.19) | collective-permute-done | bytes 32800 | tf_op jit(solution)/shard_map/ppermute | solution.py:36
  109.8 3.1 %collective-permute-start.20 = (f32[2,8,512]{2,1,0:T(8,128)S(1)}, f32[2,8,512]{2,1,0:T(8,128)S(1)}, u32[]{:S(2)}, u32[]{:S(2)}) collective-permute-start(f32[2,8,512]{2,1,0:T(8,128)S(1)} %collective-permute-done.19.refs_3_), channel_id=1, source_target_pairs={{0,1},{1,0},{2,3},{3,2},{4,5},{5,4},{6,7},{7,6},{8,9},{9,8},{10,11... | collective-permute-start | bytes 98312 | tf_op jit(solution)/shard_map/ppermute | solution.py:41
  112.9 6.7 %collective-permute-done.21.refs_5_ = f32[2,8,512]{2,1,0:T(8,128)S(1)} collective-permute-done((f32[2,8,512]{2,1,0:T(8,128)S(1)}, f32[2,8,512]{2,1,0:T(8,128)S(1)}, u32[]{:S(2)}, u32[]{:S(2)}) %collective-permute-start.21) | collective-permute-done | bytes 32800 | tf_op jit(solution)/shard_map/ppermute | solution.py:36
  120.7 7.2 %grad_q_own.1 = f32[512,1024]{1,0:T(8,128)} custom-call(s32[9]{0:T(128)S(1)} %or_convert_fusion.flags.refs_0_, s32[1,512]{1,0:T(1,128)S(1)} %copy-done.5, f32[2,8,512]{2,1,0:T(8,128)S(1)} %pair.3.refs_2_, f32[2,8,512]{2,1,0:T(8,128)S(1)} %collective-permute-done.19.refs_3_, f32[2,8,512]{2,1,0:T(8,128)S(1)} %collective-permute-done.20.refs_4_, ...), custom_call_target="tpu_custom_call" | custom-call | tf_op jit(solution)/shard_map/grad_q_own/pallas_call | solution.py:237
  128.5 1.3 tscores.4.refs_11_
  129.8 1.3 tscores.5.refs_12_
  131.1 5.7 %grad_p_own.1.refs_10_ = f32[512,1024]{1,0:T(8,128)S(1)} custom-call(s32[9]{0:T(128)S(1)} %or_convert_fusion.flags.refs_0_, s32[1,512]{1,0:T(1,128)S(1)} %copy-done.5, f32[2,8,512]{2,1,0:T(8,128)S(1)} %pair.3.refs_2_, f32[2,8,512]{2,1,0:T(8,128)S(1)} %collective-permute-done.19.refs_3_, f32[2,8,512]{2,1,0:T(8,128)S(1)} %collective-permute-done.20.refs_4_, ...), custom_call_target="tpu_custom_call" | custom-call | tf_op jit(solution)/shard_map/grad_p_own/pallas_call | solution.py:237
  136.7 5.7 %grad_p_r2.1 = f32[512,1024]{1,0:T(8,128)} custom-call(s32[9]{0:T(128)S(1)} %or_convert_fusion.flags.refs_0_, s32[1,512]{1,0:T(1,128)S(1)} %copy-done.5, f32[2,8,512]{2,1,0:T(8,128)S(1)} %pair.3.refs_2_, f32[2,8,512]{2,1,0:T(8,128)S(1)} %collective-permute-done.19.refs_3_, f32[2,8,512]{2,1,0:T(8,128)S(1)} %collective-permute-done.20.refs_4_, ...), custom_call_target="tpu_custom_call" | custom-call | tf_op jit(solution)/shard_map/grad_p_r2/pallas_call | solution.py:237
  (60 shorter events, 17.6 us)
Async XLA Ops:
  0.6 8.9 %collective-permute-start.1 = (bf16[512,1024]{1,0:T(8,128)(2,1)}, bf16[512,1024]{1,0:T(8,128)(2,1)S(1)}, u32[]{:S(2)}, u32[]{:S(2)}) collective-permute-start(bf16[512,1024]{1,0:T(8,128)(2,1)} %refs_9_), channel_id=1, source_target_pairs={{0,1},{1,0},{2,3},{3,2},{4,5},{5,4},{6,7},{7,6},{8,9},{9,8},{10,11... | collective-permute-start | bytes 3145736 | tf_op jit(solution)/shard_map/ppermute | solution.py:41
  0.7 21.5 %collective-permute-start = (bf16[512,1024]{1,0:T(8,128)(2,1)}, bf16[512,1024]{1,0:T(8,128)(2,1)S(1)}, u32[]{:S(2)}, u32[]{:S(2)}) collective-permute-start(bf16[512,1024]{1,0:T(8,128)(2,1)} %refs_9_), channel_id=1, source_target_pairs={{0,126},{1,3},{2,0},{3,5},{4,2},{5,7},{6,4},{7,9},{8,6},{9,11},{10... | collective-permute-start | bytes 3145736 | tf_op jit(solution)/shard_map/ppermute | solution.py:36
  9.6 11.6 %collective-permute-start.3 = (bf16[512,1024]{1,0:T(8,128)(2,1)}, bf16[512,1024]{1,0:T(8,128)(2,1)}, u32[]{:S(2)}, u32[]{:S(2)}) collective-permute-start(bf16[512,1024]{1,0:T(8,128)(2,1)} %queries.5), channel_id=1, source_target_pairs={{0,1},{1,0},{2,3},{3,2},{4,5},{5,4},{6,7},{7,6},{8,9},{9,8},{10,11... | collective-permute-start | bytes 3145736 | tf_op jit(solution)/shard_map/ppermute | solution.py:41
  9.6 23.8 %collective-permute-start.2 = (bf16[512,1024]{1,0:T(8,128)(2,1)S(1)}, bf16[512,1024]{1,0:T(8,128)(2,1)S(1)}, u32[]{:S(2)}, u32[]{:S(2)}) collective-permute-start(bf16[512,1024]{1,0:T(8,128)(2,1)S(1)} %collective-permute-done.1.refs_1_.refs_8_), channel_id=1, source_target_pairs={{0,126},{1,3},{2,0},{3,5},{4,2},{5,7},{6,4},{7,9},{8,6},{9,11},{10... | collective-permute-start | bytes 3145736 | tf_op jit(solution)/shard_map/ppermute | solution.py:36
  33.3 9.8 %collective-permute-start.7 = (bf16[512,1024]{1,0:T(8,128)(2,1)S(1)}, bf16[512,1024]{1,0:T(8,128)(2,1)S(1)}, u32[]{:S(2)}, u32[]{:S(2)}) collective-permute-start(bf16[512,1024]{1,0:T(8,128)(2,1)S(1)} %collective-permute-done.refs_0_.refs_9_), channel_id=1, source_target_pairs={{0,1},{1,0},{2,3},{3,2},{4,5},{5,4},{6,7},{7,6},{8,9},{9,8},{10,11... | collective-permute-start | bytes 3145736 | tf_op jit(solution)/shard_map/ppermute | solution.py:41
  33.3 13.3 %collective-permute-start.4 = (bf16[512,1024]{1,0:T(8,128)(2,1)S(1)}, bf16[512,1024]{1,0:T(8,128)(2,1)S(1)}, u32[]{:S(2)}, u32[]{:S(2)}) collective-permute-start(bf16[512,1024]{1,0:T(8,128)(2,1)S(1)} %collective-permute-done.2.refs_0_.refs_11_), channel_id=1, source_target_pairs={{0,1},{1,0},{2,3},{3,2},{4,5},{5,4},{6,7},{7,6},{8,9},{9,8},{10,11... | collective-permute-start | bytes 3145736 | tf_op jit(solution)/shard_map/ppermute | solution.py:41
  33.8 20.2 %collective-permute-start.5 = (bf16[512,1024]{1,0:T(8,128)(2,1)S(1)}, bf16[512,1024]{1,0:T(8,128)(2,1)S(1)}, u32[]{:S(2)}, u32[]{:S(2)}) collective-permute-start(bf16[512,1024]{1,0:T(8,128)(2,1)S(1)} %collective-permute-done.refs_0_.refs_9_), channel_id=1, source_target_pairs={{0,126},{1,3},{2,0},{3,5},{4,2},{5,7},{6,4},{7,9},{8,6},{9,11},{10... | collective-permute-start | bytes 3145736 | tf_op jit(solution)/shard_map/ppermute | solution.py:36
  41.7 23.6 %collective-permute-start.6 = (bf16[512,1024]{1,0:T(8,128)(2,1)S(1)}, bf16[512,1024]{1,0:T(8,128)(2,1)S(1)}, u32[]{:S(2)}, u32[]{:S(2)}) collective-permute-start(bf16[512,1024]{1,0:T(8,128)(2,1)S(1)} %collective-permute-done.2.refs_0_.refs_11_), channel_id=1, source_target_pairs={{0,126},{1,3},{2,0},{3,5},{4,2},{5,7},{6,4},{7,9},{8,6},{9,11},{10... | collective-permute-start | bytes 3145736 | tf_op jit(solution)/shard_map/ppermute | solution.py:36
  45.8 49.0 %collective-permute-start.15 = (bf16[2,512,1024]{2,1,0:T(8,128)(2,1)S(1)}, bf16[2,512,1024]{2,1,0:T(8,128)(2,1)S(1)}, u32[]{:S(2)}, u32[]{:S(2)}) collective-permute-start(bf16[2,512,1024]{2,1,0:T(8,128)(2,1)S(1)} %pair.2.queries.refs_7_), channel_id=1, source_target_pairs={{0,126},{1,3},{2,0},{3,5},{4,2},{5,7},{6,4},{7,9},{8,6},{9,11},{10... | collective-permute-start | bytes 6291464 | tf_op jit(solution)/shard_map/ppermute | solution.py:36
  49.3 16.0 %collective-permute-start.9 = (f32[2,8,512]{2,1,0:T(8,128)S(1)}, f32[2,8,512]{2,1,0:T(8,128)S(1)}, u32[]{:S(2)}, u32[]{:S(2)}) collective-permute-start(f32[2,8,512]{2,1,0:T(8,128)S(1)} %get-tuple-element.121.st2.refs_2_), channel_id=1, source_target_pairs={{0,1},{1,0},{2,3},{3,2},{4,5},{5,4},{6,7},{7,6},{8,9},{9,8},{10,11... | collective-permute-start | bytes 98312 | tf_op jit(solution)/shard_map/ppermute | solution.py:41
  49.3 16.0 %collective-permute-start.8 = (f32[2,8,512]{2,1,0:T(8,128)S(1)}, f32[2,8,512]{2,1,0:T(8,128)S(1)}, u32[]{:S(2)}, u32[]{:S(2)}) collective-permute-start(f32[2,8,512]{2,1,0:T(8,128)S(1)} %get-tuple-element.120.st1.refs_1_), channel_id=1, source_target_pairs={{0,1},{1,0},{2,3},{3,2},{4,5},{5,4},{6,7},{7,6},{8,9},{9,8},{10,11... | collective-permute-start | bytes 98312 | tf_op jit(solution)/shard_map/ppermute | solution.py:41
  65.3 2.7 %collective-permute-start.10 = (bf16[512,1024]{1,0:T(8,128)(2,1)S(1)}, bf16[512,1024]{1,0:T(8,128)(2,1)S(1)}, u32[]{:S(2)}, u32[]{:S(2)}) collective-permute-start(bf16[512,1024]{1,0:T(8,128)(2,1)S(1)} %collective-permute-done.5.refs_0_.refs_13_), channel_id=1, source_target_pairs={{0,1},{1,0},{2,3},{3,2},{4,5},{5,4},{6,7},{7,6},{8,9},{9,8},{10,11... | collective-permute-start | bytes 3145736 | tf_op jit(solution)/shard_map/ppermute | solution.py:41
  65.4 5.7 %collective-permute-start.12 = (bf16[512,1024]{1,0:T(8,128)(2,1)S(1)}, bf16[512,1024]{1,0:T(8,128)(2,1)S(1)}, u32[]{:S(2)}, u32[]{:S(2)}) collective-permute-start(bf16[512,1024]{1,0:T(8,128)(2,1)S(1)} %collective-permute-done.6), channel_id=1, source_target_pairs={{0,1},{1,0},{2,3},{3,2},{4,5},{5,4},{6,7},{7,6},{8,9},{9,8},{10,11... | collective-permute-start | bytes 3145736 | tf_op jit(solution)/shard_map/ppermute | solution.py:41
  70.7 3.4 %collective-permute-start.11 = (f32[2,8,512]{2,1,0:T(8,128)S(1)}, f32[2,8,512]{2,1,0:T(8,128)S(1)}, u32[]{:S(2)}, u32[]{:S(2)}) collective-permute-start(f32[2,8,512]{2,1,0:T(8,128)S(1)} %get-tuple-element.122.st3.refs_3_), channel_id=1, source_target_pairs={{0,1},{1,0},{2,3},{3,2},{4,5},{5,4},{6,7},{7,6},{8,9},{9,8},{10,11... | collective-permute-start | bytes 98312 | tf_op jit(solution)/shard_map/ppermute | solution.py:41
  72.8 1.3 collective-permute-start.13
  74.1 11.0 %collective-permute-start.14 = (f32[4,8,512]{2,1,0:T(8,128)S(1)}, f32[4,8,512]{2,1,0:T(8,128)S(1)}, u32[]{:S(2)}, u32[]{:S(2)}) collective-permute-start(f32[4,8,512]{2,1,0:T(8,128)S(1)} %near.1), channel_id=1, source_target_pairs={{0,2},{1,127},{2,4},{3,1},{4,6},{5,3},{6,8},{7,5},{8,10},{9,7},{10... | collective-permute-start | bytes 196616 | tf_op jit(solution)/shard_map/ppermute | solution.py:36
  85.1 9.7 %collective-permute-start.16 = (f32[4,8,512]{2,1,0:T(8,128)S(1)}, f32[4,8,512]{2,1,0:T(8,128)S(1)}, u32[]{:S(2)}, u32[]{:S(2)}) collective-permute-start(f32[4,8,512]{2,1,0:T(8,128)S(1)} %collective-permute-done.14.one), channel_id=1, source_target_pairs={{0,2},{1,127},{2,4},{3,1},{4,6},{5,3},{6,8},{7,5},{8,10},{9,7},{10... | collective-permute-start | bytes 196616 | tf_op jit(solution)/shard_map/ppermute | solution.py:36
  94.8 33.2 %collective-permute-start.23 = (bf16[2,512,1024]{2,1,0:T(8,128)(2,1)S(1)}, bf16[2,512,1024]{2,1,0:T(8,128)(2,1)S(1)}, u32[]{:S(2)}, u32[]{:S(2)}) collective-permute-start(bf16[2,512,1024]{2,1,0:T(8,128)(2,1)S(1)} %collective-permute-done.15.queries.refs_8_), channel_id=1, source_target_pairs={{0,126},{1,3},{2,0},{3,5},{4,2},{5,7},{6,4},{7,9},{8,6},{9,11},{10... | collective-permute-start | bytes 6291464 | tf_op jit(solution)/shard_map/ppermute | solution.py:36
  96.4 1.3 collective-permute-start.17
  100.0 9.8 %collective-permute-start.19 = (f32[2,8,512]{2,1,0:T(8,128)S(1)}, f32[2,8,512]{2,1,0:T(8,128)S(1)}, u32[]{:S(2)}, u32[]{:S(2)}) collective-permute-start(f32[2,8,512]{2,1,0:T(8,128)S(1)} %pair.3.refs_2_), channel_id=1, source_target_pairs={{0,2},{1,127},{2,4},{3,1},{4,6},{5,3},{6,8},{7,5},{8,10},{9,7},{10... | collective-permute-start | bytes 98312 | tf_op jit(solution)/shard_map/ppermute | solution.py:36
  109.8 9.8 %collective-permute-start.21 = (f32[2,8,512]{2,1,0:T(8,128)S(1)}, f32[2,8,512]{2,1,0:T(8,128)S(1)}, u32[]{:S(2)}, u32[]{:S(2)}) collective-permute-start(f32[2,8,512]{2,1,0:T(8,128)S(1)} %collective-permute-done.19.refs_3_), channel_id=1, source_target_pairs={{0,2},{1,127},{2,4},{3,1},{4,6},{5,3},{6,8},{7,5},{8,10},{9,7},{10... | collective-permute-start | bytes 98312 | tf_op jit(solution)/shard_map/ppermute | solution.py:36
  109.8 10.3 %collective-permute-start.20 = (f32[2,8,512]{2,1,0:T(8,128)S(1)}, f32[2,8,512]{2,1,0:T(8,128)S(1)}, u32[]{:S(2)}, u32[]{:S(2)}) collective-permute-start(f32[2,8,512]{2,1,0:T(8,128)S(1)} %collective-permute-done.19.refs_3_), channel_id=1, source_target_pairs={{0,1},{1,0},{2,3},{3,2},{4,5},{5,4},{6,7},{7,6},{8,9},{9,8},{10,11... | collective-permute-start | bytes 98312 | tf_op jit(solution)/shard_map/ppermute | solution.py:41
  119.5 10.2 %collective-permute-start.25 = (bf16[2,512,1024]{2,1,0:T(8,128)(2,1)S(1)}, bf16[2,512,1024]{2,1,0:T(8,128)(2,1)S(1)}, u32[]{:S(2)}, u32[]{:S(2)}) collective-permute-start(bf16[2,512,1024]{2,1,0:T(8,128)(2,1)S(1)} %collective-permute-done.15.queries.refs_8_), channel_id=1, source_target_pairs={{0,1},{1,0},{2,3},{3,2},{4,5},{5,4},{6,7},{7,6},{8,9},{9,8},{10,11... | collective-permute-start | bytes 6291464 | tf_op jit(solution)/shard_map/ppermute | solution.py:41
  128.0 8.7 %collective-permute-start.24 = (bf16[2,512,1024]{2,1,0:T(8,128)(2,1)S(1)}, bf16[2,512,1024]{2,1,0:T(8,128)(2,1)S(1)}, u32[]{:S(2)}, u32[]{:S(2)}) collective-permute-start(bf16[2,512,1024]{2,1,0:T(8,128)(2,1)S(1)} %collective-permute-done.23.refs_7_), channel_id=1, source_target_pairs={{0,1},{1,0},{2,3},{3,2},{4,5},{5,4},{6,7},{7,6},{8,9},{9,8},{10,11... | collective-permute-start | bytes 6291464 | tf_op jit(solution)/shard_map/ppermute | solution.py:41
  (8 other events, 95.5 us)
where the time goes:
time: 144 us; the launch traced here: 143 us
  waiting for transfers between devices  68.8 us (48%)
  Pallas kernels  37.7 us (26%)
  starting transfers between devices  29.3 us (20%)
  local copies, waits for them, and re-layouts  3.14 us (2%)
  other arithmetic  2.08 us (1%)
  between operations  1.63 us (1%)
    ppermute x10, waiting for transfers between devices, split(): return lax.ppermute(value, AXES, pairs)  62.9 us
    ppermute x10, starting transfers between devices, split(): return lax.ppermute(value, AXES, pairs)  22.4 us
    pallas_call x13, Pallas kernels, call(): pl.pallas_call(kernel, in_specs=[first] + [VMEM] * (len(operands) - 1), o...  19.1 us
    pallas_call x3, Pallas kernels, grad(): pl.pallas_call(functools.partial(grad_kernel, names, passage_side, at, sc...  18.6 us
    ppermute x16, starting transfers between devices, swap(): return lax.ppermute(value, AXES, [(i, i ^ 1) for i in range(n)])  6.84 us
    ppermute x16, waiting for transfers between devices, swap(): return lax.ppermute(value, AXES, [(i, i ^ 1) for i in range(n)])  5.9 us
    unnamed x12, local copies, waits for them, and re-layouts  3.14 us
  transfers between devices with their start and end apart: 26, of which 13 were waited for; matrix products, arithmetic and copies ran while one was open for 1% of the time, Pallas kernels for 22%

commit v1 on v0

--- a/solution.py
+++ b/solution.py
@@ -135,37 +135,34 @@
     out[2:3], out[3:4] = merged(parts, 2)
 
 
-def near_kernel(st1, peer1, st2, peer2, st3, peer3, peer4, out):
+def lse_q_kernel(flags, *refs):
+    stats, (pay, loss) = refs[:5], refs[5:]
+    top, total = merged([stats[SPOT[name][0]].at[SPOT[name][1]] for name in NAMES], 0)
+    lse = top + jnp.log(total)
+    lane = lax.broadcasted_iota(jnp.int32, (1, BLK), 1)
+    here = jnp.zeros((1, BLK), jnp.float32)
+    for i in range(9):
+        here = jnp.where(lane == i, flags[i].astype(jnp.float32), here)
+    pay[0:1] = lse
+    pay[1:2] = here
+    loss[...] = lse - stats[0][0, 4:5]
+
+
+def near_kernel(st1, peer1, st2, peer2, st3, peer3, peer4, pay, peer_pay, out):
     merge_into(out.at[0], st1.at[0], peer1.at[1])
     merge_into(out.at[1], st2.at[0], peer2.at[1])
     merge_into(out.at[2], st3.at[0], peer3.at[1])
     out[3] = peer4[0]
-
-
-def home_kernel(st0, one, two, mine, theirs):
-    merge_into(mine, st0.at[0], one.at[0], two.at[2])
-    merge_into(theirs, st0.at[1], one.at[1], two.at[3])
-
-
-def lse_kernel(flags, *refs):
-    stats, mine, peer, pay, query_loss, passage_loss = refs[:5], *refs[5:]
-    top, total = merged([stats[SPOT[name][0]].at[SPOT[name][1]] for name in NAMES], 0)
-    row_lse = top + jnp.log(total)
-    top, total = merged([mine, peer], 2)
-    col_lse = top + jnp.log(total)
-    query_loss[...] = row_lse - stats[0][0, 4:5]
-    passage_loss[...] = col_lse - stats[0][0, 5:6]
-    lane = lax.broadcasted_iota(jnp.int32, (1, BLK), 1)
-    here = jnp.zeros((1, BLK), jnp.float32)
-    for i in range(9):
-        here = jnp.where(lane == i, flags[i].astype(jnp.float32), here)
-    pay[0:1] = row_lse
-    pay[1:2] = col_lse
-    pay[2:3] = here
-
-
-def block_of(arrays, spot):
-    return arrays[spot[0]] if spot[1] is None else arrays[spot[0]].at[spot[1]]
+    out[4] = pay[...]
+    out[5] = peer_pay[...]
+
+
+def lse_p_kernel(st0, peer0, one, one_peer, two, two_peer, pay, loss):
+    parts = [st0.at[0], peer0.at[1], one.at[0], one_peer.at[1], two.at[2], two_peer.at[3]]
+    top, total = merged(parts, 2)
+    lse = top + jnp.log(total)
+    pay[0:1] = lse
+    loss[...] = lse - st0[0, 5:6]
 
 
 def tscores_kernel(passages, queries, out):
@@ -178,72 +175,96 @@
     return call(tscores_kernel, "tscores", out, passages, queries)
 
 
-def grad_kernel(names, passage_side, at, scores_at, has_total, sizes, *refs):
-    n = len(names)
-    flags, positives = refs[:2]
-    messages, refs = refs[2:7], refs[7:]
-    others, refs = refs[: sizes[0]], refs[sizes[0] :]
-    scores, refs = refs[: sizes[1]], refs[sizes[1] :]
-    if not scores:
-        own, refs = refs[0], refs[1:]
-    if has_total:
-        earlier, refs = refs[0], refs[1:]
-    out, total, out_sem = refs
-    own_lse = column_of(messages[0][0, 1:2] if passage_side else messages[0][0, 0:1])
+def parts_kernel(steps, earlier, final, n_arrays, *refs):
+    flags, positives, own_rows, own_columns, refs = *refs[:4], refs[4:]
+    from_q, from_p, refs = refs[:5], refs[5:10], refs[10:]
+    arrays, refs = refs[:n_arrays], refs[n_arrays:]
+    sides = sorted(earlier)
+    outs, scratch = refs[: len(sides)], refs[len(sides) :]
+    totals, sems = {}, {}
+    for side, out in zip(sides, outs):
+        if final[side]:
+            totals[side], sems[side], *scratch = scratch
+        else:
+            totals[side] = out
     lane = lax.broadcasted_iota(jnp.int32, (1, BLK), 1)
+    own_lse = {side: column_of((own_rows if side == "q" else own_columns)[0:1]) for side in sides}
+    left = {side: sum(step[0] == side for step in steps) for side in sides}
+    begun = set()
     sent = []
-    for i, name in enumerate(names):
+    for side, name, block, score in steps:
         message, which = MESSAGE[name]
-        pay = messages[message].at[which]
-        other = block_of(others, at[i])
-        s = block_of(scores, scores_at[i])[...] if scores else scores_of(own[...], other[...])
-        weight = jnp.exp(s - own_lse) + jnp.exp(s - (pay[0:1] if passage_side else pay[1:2]))
+        pay = from_q[message].at[4 + which] if side == "p" else from_p[message].at[which]
+        other = arrays[block[0]] if block[1] is None else arrays[block[0]].at[block[1]]
+        if score[1] is None:
+            s = scores_of(arrays[score[0]][...], other[...])
+        else:
+            s = arrays[score[0]][score[1]]
+        weight = jnp.exp(s - own_lse[side]) + jnp.exp(s - pay[0:1])
         if name == "own":
-            if passage_side:
+            if side == "p":
                 hit = lax.broadcasted_iota(jnp.int32, s.shape, 0) == positives[...]
             else:
                 hit = lax.broadcasted_iota(jnp.int32, s.shape, 1) == chosen_of(positives)
             weight = LOGIT * jnp.where(hit, weight - 2.0, weight)
         else:
-            if passage_side:
-                lanes = jnp.where(lane == PLACE[BACK[name]], pay[2:3], 0.0)
+            if side == "p":
+                lanes = jnp.where(lane == PLACE[BACK[name]], pay[1:2], 0.0)
                 here = jnp.broadcast_to(jnp.sum(lanes, axis=1, keepdims=True), lane.shape) > 0.5
             else:
                 here = flags[PLACE[name]] > 0
             weight = jnp.where(here, LOGIT * weight, 0.0)
         weight = weight.astype(jnp.bfloat16)
-        last = i == n - 1
-        step = WIDTH // 4 if last else WIDTH
+        left[side] -= 1
+        total = totals[side]
+        out = left[side] == 0 and final[side]
+        step = WIDTH // 4 if out else WIDTH
         for start in range(0, WIDTH, step):
             span = slice(start, start + step)
             part = jnp.dot(weight, other[:, span], preferred_element_type=jnp.float32)
-            if i > 0:
+            if side in begun:
                 total[:, span] += part
+            elif earlier[side] is None:
+                total[:, span] = part
             else:
-                total[:, span] = earlier[:, span] + part if has_total else part
-            if last:
-                copy = pltpu.make_async_copy(total.at[:, span], out.at[:, span], out_sem.at[start // step])
+                total[:, span] = arrays[earlier[side]][:, span] + part
+            if out:
+                sem = sems[side].at[start // step]
+                copy = pltpu.make_async_copy(total.at[:, span], outs[sides.index(side)].at[:, span], sem)
                 copy.start()
                 sent.append(copy)
+        begun.add(side)
     for copy in sent:
         copy.wait()
 
 
-def grad(names, passage_side, flags, positives, messages, others, at, scores=(), scores_at=(), own=None, earlier=None):
-    operands = [flags, positives, *messages, *others, *scores]
-    operands += [] if scores else [own]
-    operands += [] if earlier is None else [earlier]
-    sizes = (len(others), len(scores))
+def parts(name, common, from_p, steps, earlier, final=()):
+    arrays = []
+
+    def at(spot):
+        for i, array in enumerate(arrays):
+            if array is spot[0]:
+                return i, spot[1]
+        arrays.append(spot[0])
+        return len(arrays) - 1, spot[1]
+
+    plan = [(side, slot, at(block), at(scores)) for side, slot, block, scores in steps]
+    sides = sorted(earlier)
+    begin = {side: None if earlier[side] is None else at((earlier[side], None))[0] for side in sides}
+    scratch = []
+    for side in sides:
+        scratch += [pltpu.VMEM((BLK, WIDTH), jnp.float32), pltpu.SemaphoreType.DMA((4,))] * (side in final)
+    last = {side: side in final for side in sides}
     return pl.pallas_call(
-        functools.partial(grad_kernel, names, passage_side, at, scores_at, earlier is not None, sizes),
-        in_specs=[SMEM] + [VMEM] * (len(operands) - 1),
-        out_specs=HBM,
-        out_shape=jax.ShapeDtypeStruct((BLK, WIDTH), jnp.float32),
-        scratch_shapes=[pltpu.VMEM((BLK, WIDTH), jnp.float32), pltpu.SemaphoreType.DMA((4,))],
+        functools.partial(parts_kernel, plan, begin, last, len(arrays)),
+        in_specs=[SMEM] + [VMEM] * (13 + len(arrays)),
+        out_specs=[HBM if last[side] else VMEM for side in sides],
+        out_shape=[jax.ShapeDtypeStruct((BLK, WIDTH), jnp.float32)] * len(sides),
+        scratch_shapes=scratch,
         compiler_params=LIMIT,
         cost_estimate=FREE,
-        name="grad_" + ("p_" if passage_side else "q_") + names[0],
-    )(*operands)
+        name=name,
+    )(*common, *from_p, *arrays)
 
 
 def body(queries, passages, positives, pair_blocks, negative_pair_count):
@@ -271,54 +292,83 @@
 
     v["p_own"] = v.pop("p")
     v["p_s0"], v["q_s0"] = swap(v["p_own"]), swap(v["q"])
-    v["p_a"], v["p_sb"] = split(v["p_own"], -1, 1), split(v["p_s0"], -1, 1)
+    p_sb = split(v["p_s0"], -1, 1)
+    v["p_a"] = split(v["p_own"], -1, 1)
     stat(0)
     fence()
-    p_r2, p_r4 = split(v["p_a"], -1, 1), split(v["p_sb"], -1, 1)
-    v["p_sa"], v["p_b"] = swap(v["p_a"]), swap(v["p_sb"])
+    p_r2, p_sa = split(v["p_a"], -1, 1), swap(v["p_a"])
+    v["p_sb"] = p_sb
+    fence()
+    p_r4, p_b = split(v["p_sb"], -1, 1), swap(v["p_sb"])
+    v["q0"] = pair(v["q"], v["q_s0"])
+    v["p_r2"], v["p_sa"] = p_r2, p_sa
+    fence()
     stat(1)
+    q1 = split(after(v["q0"], v["st1"]), -1, 1)
+    v["p_r4"], v["p_b"] = p_r4, p_b
+    fence()
+    v["p_s2"], v["p_r3"] = swap(v["p_r2"]), swap(v["p_r4"])
     stat(2)
-    v["x1"], v["x2"] = swap(v["st1"]), swap(v["st2"])
-    v["q0"] = pair(v["q"], v["q_s0"])
-    q1 = split(after(v["q0"], v["st1"]), -1, 1)
-    v["p_r2"], v["p_r4"] = p_r2, p_r4
-    fence()
-    v["p_s2"], v["p_r3"] = swap(v["p_r2"]), swap(v["p_r4"])
     stat(3)
     stat(4)
-    x3, x4 = swap(v["st3"]), swap(v["st4"])
-    near = call(near_kernel, "near", small(4), v["st1"], v["x1"], v["st2"], v["x2"], v["st3"], x3, x4)
+    line = jax.ShapeDtypeStruct((1, BLK), jnp.float32)
+    q_pay, query_loss = call(lse_q_kernel, "lse_q", [small(), line], v["flags"], *group_of("st"), first=SMEM)
+    x0, x1, x2, x3, x4 = (swap(stats) for stats in group_of("st"))
+    near = call(
+        near_kernel, "near", small(6), v["st1"], x1, v["st2"], x2, v["st3"], x3, x4, q_pay, swap(q_pay)
+    )
     v["one"] = split(near, 1, -1)
     v["two"] = split(v["one"], 1, -1)
+    v["one_peer"] = swap(v["one"])
+    v["x0"], v["near"], v["q_pay"] = x0, near, q_pay
     v["t0"] = tscores_of(v["p_own"], v["q0"])
     v["q1"] = q1
     fence()
     v["q3"] = split(v["q1"], -1, 1)
     v["q2"] = swap(v["q1"])
-    mine, theirs = call(home_kernel, "home", [small()] * 2, v["st0"], v["one"], v["two"])
-    line = jax.ShapeDtypeStruct((1, BLK), jnp.float32)
-    pay, query_loss, passage_loss = call(
-        lse_kernel, "lse", [small(), line, line], v["flags"], *group_of("st"), mine, swap(theirs), first=SMEM
-    )
-    m0 = pair(pay, swap(pay))
+    two_peer = swap(v["two"])
+    p_pay, passage_loss = call(
+        lse_p_kernel, "lse_p", [small(), line], v["st0"], v["x0"], v["one"], v["one_peer"], v["two"], two_peer
+    )
+    m0 = pair(p_pay, swap(p_pay))
+
+    common = (v["flags"], v["pos"], v["q_pay"], p_pay, v["near"], v["one"], v["one_peer"], v["two"], two_peer)
+    places = dict(
+        own=("q0", 0), s0=("q0", 1), a=("q1", 0), sb=("q1", 1), sa=("q2", 0), b=("q2", 1), r2=("q3", 0),
+        s2=("q4", 0), r3=("q4", 1),
+    )
+
+    def steps_of(side, *names):
+        steps = []
+        for name in names:
+            if side == "q":
+                g, k = SPOT[name]
+                steps.append(("q", name, (v["p_" + name], None), (v["s%d" % g], k)))
+            else:
+                array, k = places[name]
+                scores = (v["t0"], k) if array == "q0" else (v["p_own"], None)
+                steps.append(("p", name, (v[array], k), scores))
+        return steps
+
+    hold = lax.optimization_barrier
     m1 = split(m0, 1, -1)
+    steps = steps_of("q", "own", "s0") + steps_of("p", "own", "s0", "sa", "b")
+    p_total, q_total = parts("part0", common, [m0] * 5, steps, dict(p=None, q=None))
+    m1, q_total, p_total = hold((m1, q_total, p_total))
     m3 = split(m1, 1, -1)
-    messages = [m0, m1, swap(m1), m3, swap(m3)]
-    query_grad = grad(
-        NAMES, False, v["flags"], v["pos"], messages, [v["p_" + name] for name in NAMES],
-        [(i, None) for i in range(9)], group_of("s"), [SPOT[name] for name in NAMES],
-    )
-    early, late = ("own", "s0", "a", "sb", "sa", "b"), ("r2", "s2", "r3")
-    spots = [(i // 2, i % 2) for i in range(6)]
-    scores = [v["t0"], tscores_of(v["p_own"], v["q1"]), tscores_of(v["p_own"], v["q2"])]
-    total = grad(
-        early, True, v["flags"], v["pos"], messages, [v["q0"], v["q1"], v["q2"]], spots, scores, spots
-    )
-    q4 = swap(after(v["q3"], query_grad))
-    passage_grad = grad(
-        late, True, v["flags"], v["pos"], messages, [v["q3"], q4], [(0, 0), (1, 0), (1, 1)],
-        own=v["p_own"], earlier=total,
-    )
+    m2 = swap(m1)
+    steps = steps_of("q", "sa", "b") + steps_of("p", "a", "sb")
+    p_total, q_total = parts("part1", common, [m0, m1, m0, m0, m0], steps, dict(p=p_total, q=q_total))
+    m2, m3, q_total, p_total = hold((m2, m3, q_total, p_total))
+    m4 = swap(m3)
+    m4, v["q3"] = hold((m4, v["q3"]))
+    v["q4"] = swap(v["q3"])
+    messages = [m0, m1, m2, m3, m4]
+    (query_grad,) = parts(
+        "part2", common, messages, steps_of("q", "a", "sb", "s2", "r3", "r2"), dict(q=q_total), "q"
+    )
+    v["q4"], p_total, _ = hold((v["q4"], p_total, query_grad))
+    (passage_grad,) = parts("part3", common, messages, steps_of("p", "r2", "s2", "r3"), dict(p=p_total), "p")
     return (query_loss, passage_loss, query_grad, passage_grad)
 
 

time: 144 us -> 132 us (0.917)
  waiting for transfers between devices: 68.8 us -> 37.2 us
  starting transfers between devices: 29.3 us -> 50 us
    ppermute x10, waiting for transfers between devices: 62.9 us -> 33.7 us  [split(): return lax.ppermute(value, AXES, pairs)]
    ppermute x10, starting transfers between devices: 22.4 us -> 39.6 us  [split(): return lax.ppermute(value, AXES, pairs)]
    ppermute x16 -> x19, starting transfers between devices: 6.84 us -> 10.3 us  [swap(): return lax.ppermute(value, AXES, [(i, i ^ 1) for i in range(n)])]
    pallas_call x13 -> x11, Pallas kernels: 19.1 us -> 15.9 us  [call(): pl.pallas_call(kernel, in_specs=[first] + [VMEM] * (len(operands) - 1), o...]
    pallas_call x3 -> x4, Pallas kernels: 18.6 us -> 21.3 us  [parts(): pl.pallas_call(functools.partial(parts_kernel, plan, begin, last, len(arr...]
    ppermute x16 -> x19, waiting for transfers between devices: 5.9 us -> 3.45 us  [swap(): return lax.ppermute(value, AXES, [(i, i ^ 1) for i in range(n)])]
  transfers between devices with their start and end apart: 26 -> 29, of which waited for: 13 -> 13; matrix products, arithmetic and copies ran while one was open for 1% -> 2% of each run, Pallas kernels for 22% -> 24%
where the time goes in v1:
time: 132 us; the launch traced here: 131 us
  starting transfers between devices  50 us (38%)
  waiting for transfers between devices  37.2 us (28%)
  Pallas kernels  37.1 us (28%)
  local copies, waits for them, and re-layouts  3.14 us (2%)
  other arithmetic  2.08 us (2%)
  between operations  1.62 us (1%)
    ppermute x10, starting transfers between devices, split(): return lax.ppermute(value, AXES, pairs)  39.6 us
    ppermute x10, waiting for transfers between devices, split(): return lax.ppermute(value, AXES, pairs)  33.7 us
    pallas_call x4, Pallas kernels, parts(): pl.pallas_call(functools.partial(parts_kernel, plan, begin, last, len(arr...  21.3 us
    pallas_call x11, Pallas kernels, call(): pl.pallas_call(kernel, in_specs=[first] + [VMEM] * (len(operands) - 1), o...  15.9 us
    ppermute x19, starting transfers between devices, swap(): return lax.ppermute(value, AXES, [(i, i ^ 1) for i in range(n)])  10.3 us
    ppermute x19, waiting for transfers between devices, swap(): return lax.ppermute(value, AXES, [(i, i ^ 1) for i in range(n)])  3.45 us
    unnamed x12, local copies, waits for them, and re-layouts  3.14 us
  transfers between devices with their start and end apart: 29, of which 13 were waited for; matrix products, arithmetic and copies ran while one was open for 2% of the time, Pallas kernels for 24%

profile of v1, /device:TPU:0, one launch (start us, length us, event | category | flops | bytes accessed | tf_op | source)
XLA Modules:
  0.0 131.1 jit_solution(11766066960872422347)
XLA Ops:
  0.7 8.8 %collective-permute-start = (bf16[512,1024]{1,0:T(8,128)(2,1)}, bf16[512,1024]{1,0:T(8,128)(2,1)S(1)}, u32[]{:S(2)}, u32[]{:S(2)}) collective-permute-start(bf16[512,1024]{1,0:T(8,128)(2,1)} %refs_15_), channel_id=1, source_target_pairs={{0,126},{1,3},{2,0},{3,5},{4,2},{5,7},{6,4},{7,9},{8,6},{9,11},{10... | collective-permute-start | bytes 3145736 | tf_op jit(solution)/shard_map/ppermute | solution.py:36
  16.9 2.9 %stats0.1 = (f32[2,512,512]{2,1,0:T(8,128)S(1)}, f32[2,8,512]{2,1,0:T(8,128)S(1)}) custom-call(s32[9]{0:T(128)S(1)} %or_convert_fusion.flags.refs_0_, s32[1,512]{1,0:T(1,128)S(1)} %copy-done.4, bf16[512,1024]{1,0:T(8,128)(2,1)S(1)} %copy-done, bf16[512,1024]{1,0:T(8,128)(2,1)S(1)} %copy-done.2, bf16[512,1024]{1,0:T(8,128)(2,1)S(1)} %collective-permute-done.1.refs_1_.refs_16_), custom_call_target="tpu_custom_call" | custom-call | tf_op jit(solution)/shard_map/stats0/pallas_call | solution.py:53
  19.8 2.4 %collective-permute-done.refs_0_.refs_14_ = bf16[512,1024]{1,0:T(8,128)(2,1)S(1)} collective-permute-done((bf16[512,1024]{1,0:T(8,128)(2,1)}, bf16[512,1024]{1,0:T(8,128)(2,1)S(1)}, u32[]{:S(2)}, u32[]{:S(2)}) %collective-permute-start) | collective-permute-done | bytes 1048608 | tf_op jit(solution)/shard_map/ppermute | solution.py:36
  22.2 7.8 %collective-permute-start.4 = (bf16[512,1024]{1,0:T(8,128)(2,1)S(1)}, bf16[512,1024]{1,0:T(8,128)(2,1)S(1)}, u32[]{:S(2)}, u32[]{:S(2)}) collective-permute-start(bf16[512,1024]{1,0:T(8,128)(2,1)S(1)} %collective-permute-done.refs_0_.refs_14_), channel_id=1, source_target_pairs={{0,126},{1,3},{2,0},{3,5},{4,2},{5,7},{6,4},{7,9},{8,6},{9,11},{10... | collective-permute-start | bytes 3145736 | tf_op jit(solution)/shard_map/ppermute | solution.py:36
  30.0 3.3 %collective-permute-done.3.refs_0_.refs_16_ = bf16[512,1024]{1,0:T(8,128)(2,1)S(1)} collective-permute-done((bf16[512,1024]{1,0:T(8,128)(2,1)S(1)}, bf16[512,1024]{1,0:T(8,128)(2,1)S(1)}, u32[]{:S(2)}, u32[]{:S(2)}) %collective-permute-start.3) | collective-permute-done | bytes 1048608 | tf_op jit(solution)/shard_map/ppermute | solution.py:36
  33.3 7.9 %collective-permute-start.7 = (bf16[512,1024]{1,0:T(8,128)(2,1)S(1)}, bf16[512,1024]{1,0:T(8,128)(2,1)S(1)}, u32[]{:S(2)}, u32[]{:S(2)}) collective-permute-start(bf16[512,1024]{1,0:T(8,128)(2,1)S(1)} %collective-permute-done.3.refs_0_.refs_16_), channel_id=1, source_target_pairs={{0,126},{1,3},{2,0},{3,5},{4,2},{5,7},{6,4},{7,9},{8,6},{9,11},{10... | collective-permute-start | bytes 3145736 | tf_op jit(solution)/shard_map/ppermute | solution.py:36
  41.4 3.2 %collective-permute-done.4.refs_0_.refs_22_ = bf16[512,1024]{1,0:T(8,128)(2,1)S(1)} collective-permute-done((bf16[512,1024]{1,0:T(8,128)(2,1)S(1)}, bf16[512,1024]{1,0:T(8,128)(2,1)S(1)}, u32[]{:S(2)}, u32[]{:S(2)}) %collective-permute-start.4) | collective-permute-done | bytes 1048608 | tf_op jit(solution)/shard_map/ppermute | solution.py:36
  44.6 2.7 %stats1.1 = (f32[2,512,512]{2,1,0:T(8,128)S(1)}, f32[2,8,512]{2,1,0:T(8,128)S(1)}) custom-call(s32[9]{0:T(128)S(1)} %or_convert_fusion.flags.refs_0_, s32[1,512]{1,0:T(1,128)S(1)} %copy-done.4, bf16[512,1024]{1,0:T(8,128)(2,1)S(1)} %copy-done.1, bf16[512,1024]{1,0:T(8,128)(2,1)S(1)} %collective-permute-done.refs_0_.refs_14_, ...), custom_call_target="tpu_custom_call" | custom-call | tf_op jit(solution)/shard_map/stats1/pallas_call | solution.py:53
  47.2 8.0 %collective-permute-start.17 = (bf16[2,512,1024]{2,1,0:T(8,128)(2,1)S(1)}, bf16[2,512,1024]{2,1,0:T(8,128)(2,1)S(1)}, u32[]{:S(2)}, u32[]{:S(2)}) collective-permute-start(bf16[2,512,1024]{2,1,0:T(8,128)(2,1)S(1)} %pair.2.queries.refs_17_), channel_id=1, source_target_pairs={{0,126},{1,3},{2,0},{3,5},{4,2},{5,7},{6,4},{7,9},{8,6},{9,11},{10... | collective-permute-start | bytes 6291464 | tf_op jit(solution)/shard_map/ppermute | solution.py:36
  56.3 2.7 %stats2.1 = (f32[2,512,512]{2,1,0:T(8,128)S(1)}, f32[2,8,512]{2,1,0:T(8,128)S(1)}) custom-call(s32[9]{0:T(128)S(1)} %or_convert_fusion.flags.refs_0_, s32[1,512]{1,0:T(1,128)S(1)} %copy-done.4, bf16[512,1024]{1,0:T(8,128)(2,1)S(1)} %copy-done.1, bf16[512,1024]{1,0:T(8,128)(2,1)S(1)} %collective-permute-done.3.refs_0_.refs_16_, ...), custom_call_target="tpu_custom_call" | custom-call | tf_op jit(solution)/shard_map/stats2/pallas_call | solution.py:53
  59.5 2.7 %stats3.1 = (f32[2,512,512]{2,1,0:T(8,128)S(1)}, f32[2,8,512]{2,1,0:T(8,128)S(1)}) custom-call(s32[9]{0:T(128)S(1)} %or_convert_fusion.flags.refs_0_, s32[1,512]{1,0:T(1,128)S(1)} %copy-done.4, bf16[512,1024]{1,0:T(8,128)(2,1)S(1)} %copy-done.1, bf16[512,1024]{1,0:T(8,128)(2,1)S(1)} %collective-permute-done.4.refs_0_.refs_22_, ...), custom_call_target="tpu_custom_call" | custom-call | tf_op jit(solution)/shard_map/stats3/pallas_call | solution.py:53
  62.5 1.7 %stats4.1 = (f32[1,512,512]{2,1,0:T(8,128)S(1)}, f32[1,8,512]{2,1,0:T(8,128)S(1)}) custom-call(s32[9]{0:T(128)S(1)} %or_convert_fusion.flags.refs_0_, s32[1,512]{1,0:T(1,128)S(1)} %copy-done.4, bf16[512,1024]{1,0:T(8,128)(2,1)S(1)} %copy-done.1, bf16[512,1024]{1,0:T(8,128)(2,1)S(1)} %collective-permute-done.9.refs_0_.refs_20_), custom_call_target="tpu_custom_call" | custom-call | tf_op jit(solution)/shard_map/stats4/pallas_call | solution.py:53
  67.2 11.6 %collective-permute-done.15.one.refs_5_ = f32[6,8,512]{2,1,0:T(8,128)S(1)} collective-permute-done((f32[6,8,512]{2,1,0:T(8,128)S(1)}, f32[6,8,512]{2,1,0:T(8,128)S(1)}, u32[]{:S(2)}, u32[]{:S(2)}) %collective-permute-start.15) | collective-permute-done | bytes 98336 | tf_op jit(solution)/shard_map/ppermute | solution.py:36
  78.8 6.5 %collective-permute-start.19 = (f32[2,8,512]{2,1,0:T(8,128)S(1)}, f32[2,8,512]{2,1,0:T(8,128)S(1)}, u32[]{:S(2)}, u32[]{:S(2)}) collective-permute-start(f32[2,8,512]{2,1,0:T(8,128)S(1)} %get-tuple-element.167.refs_0_.st0), channel_id=1, source_target_pairs={{0,1},{1,0},{2,3},{3,2},{4,5},{5,4},{6,7},{7,6},{8,9},{9,8},{10,11... | collective-permute-start | bytes 98312 | tf_op jit(solution)/shard_map/ppermute | solution.py:41
  86.6 2.2 %collective-permute-done.18.two.refs_7_ = f32[6,8,512]{2,1,0:T(8,128)S(1)} collective-permute-done((f32[6,8,512]{2,1,0:T(8,128)S(1)}, f32[6,8,512]{2,1,0:T(8,128)S(1)}, u32[]{:S(2)}, u32[]{:S(2)}) %collective-permute-start.18) | collective-permute-done | bytes 98336 | tf_op jit(solution)/shard_map/ppermute | solution.py:36
  88.8 5.6 %collective-permute-start.27 = (bf16[2,512,1024]{2,1,0:T(8,128)(2,1)S(1)}, bf16[2,512,1024]{2,1,0:T(8,128)(2,1)S(1)}, u32[]{:S(2)}, u32[]{:S(2)}) collective-permute-start(bf16[2,512,1024]{2,1,0:T(8,128)(2,1)S(1)} %collective-permute-done.17.refs_18_), channel_id=1, source_target_pairs={{0,126},{1,3},{2,0},{3,5},{4,2},{5,7},{6,4},{7,9},{8,6},{9,11},{10... | collective-permute-start | bytes 6291464 | tf_op jit(solution)/shard_map/ppermute | solution.py:36
  97.6 6.0 %part0.1 = (f32[512,1024]{1,0:T(8,128)S(1)}, f32[512,1024]{1,0:T(8,128)S(1)}) custom-call(s32[9]{0:T(128)S(1)} %or_convert_fusion.flags.refs_0_, s32[1,512]{1,0:T(1,128)S(1)} %copy-done.5, f32[8,512]{1,0:T(8,128)S(1)} %get-tuple-element.175.pay.refs_2_, f32[8,512]{1,0:T(8,128)S(1)} %get-tuple-element.176.mine.refs_3_, f32[6,8,512]{2,1,0:T(8,128)S(1)} %near.1.refs_4_, ...), custom_call_target="tpu_custom_call" | custom-call | tf_op jit(solution)/shard_map/part0/pallas_call | solution.py:258
  103.6 3.7 %collective-permute-done.22.refs_10_ = f32[2,8,512]{2,1,0:T(8,128)S(1)} collective-permute-done((f32[2,8,512]{2,1,0:T(8,128)S(1)}, f32[2,8,512]{2,1,0:T(8,128)S(1)}, u32[]{:S(2)}, u32[]{:S(2)}) %collective-permute-start.22) | collective-permute-done | bytes 32800 | tf_op jit(solution)/shard_map/ppermute | solution.py:36
  107.3 4.7 %part1.1 = (f32[512,1024]{1,0:T(8,128)S(1)}, f32[512,1024]{1,0:T(8,128)S(1)}) custom-call(s32[9]{0:T(128)S(1)} %or_convert_fusion.flags.refs_0_, s32[1,512]{1,0:T(1,128)S(1)} %copy-done.5, f32[8,512]{1,0:T(8,128)S(1)} %get-tuple-element.175.pay.refs_2_, f32[8,512]{1,0:T(8,128)S(1)} %get-tuple-element.176.mine.refs_3_, f32[6,8,512]{2,1,0:T(8,128)S(1)} %near.1.refs_4_, ...), custom_call_target="tpu_custom_call" | custom-call | tf_op jit(solution)/shard_map/part1/pallas_call | solution.py:258
  112.0 5.0 %collective-permute-done.25.refs_12_ = f32[2,8,512]{2,1,0:T(8,128)S(1)} collective-permute-done((f32[2,8,512]{2,1,0:T(8,128)S(1)}, f32[2,8,512]{2,1,0:T(8,128)S(1)}, u32[]{:S(2)}, u32[]{:S(2)}) %collective-permute-start.25) | collective-permute-done | bytes 32800 | tf_op jit(solution)/shard_map/ppermute | solution.py:36
  117.1 1.6 %collective-permute-done.27.refs_14_ = bf16[2,512,1024]{2,1,0:T(8,128)(2,1)S(1)} collective-permute-done((bf16[2,512,1024]{2,1,0:T(8,128)(2,1)S(1)}, bf16[2,512,1024]{2,1,0:T(8,128)(2,1)S(1)}, u32[]{:S(2)}, u32[]{:S(2)}) %collective-permute-start.27) | collective-permute-done | bytes 2097184 | tf_op jit(solution)/shard_map/ppermute | solution.py:36
  118.7 1.7 %collective-permute-start.28 = (bf16[2,512,1024]{2,1,0:T(8,128)(2,1)S(1)}, bf16[2,512,1024]{2,1,0:T(8,128)(2,1)S(1)}, u32[]{:S(2)}, u32[]{:S(2)}) collective-permute-start(bf16[2,512,1024]{2,1,0:T(8,128)(2,1)S(1)} %collective-permute-done.27.refs_14_), channel_id=1, source_target_pairs={{0,1},{1,0},{2,3},{3,2},{4,5},{5,4},{6,7},{7,6},{8,9},{9,8},{10,11... | collective-permute-start | bytes 6291464 | tf_op jit(solution)/shard_map/ppermute | solution.py:41
  120.4 4.9 %part2.1 = f32[512,1024]{1,0:T(8,128)} custom-call(s32[9]{0:T(128)S(1)} %or_convert_fusion.flags.refs_0_, s32[1,512]{1,0:T(1,128)S(1)} %copy-done.5, f32[8,512]{1,0:T(8,128)S(1)} %get-tuple-element.175.pay.refs_2_, f32[8,512]{1,0:T(8,128)S(1)} %get-tuple-element.176.mine.refs_3_, f32[6,8,512]{2,1,0:T(8,128)S(1)} %near.1.refs_4_, ...), custom_call_target="tpu_custom_call" | custom-call | tf_op jit(solution)/shard_map/part2/pallas_call | solution.py:258
  125.3 5.7 %part3.1 = f32[512,1024]{1,0:T(8,128)} custom-call(s32[9]{0:T(128)S(1)} %or_convert_fusion.flags.refs_0_, s32[1,512]{1,0:T(1,128)S(1)} %copy-done.5, f32[8,512]{1,0:T(8,128)S(1)} %get-tuple-element.175.pay.refs_2_, f32[8,512]{1,0:T(8,128)S(1)} %get-tuple-element.176.mine.refs_3_, f32[6,8,512]{2,1,0:T(8,128)S(1)} %near.1.refs_4_, ...), custom_call_target="tpu_custom_call" | custom-call | tf_op jit(solution)/shard_map/part3/pallas_call | solution.py:258
  (65 shorter events, 16.2 us)
Async XLA Ops:
  0.6 10.3 %collective-permute-start.1 = (bf16[512,1024]{1,0:T(8,128)(2,1)}, bf16[512,1024]{1,0:T(8,128)(2,1)S(1)}, u32[]{:S(2)}, u32[]{:S(2)}) collective-permute-start(bf16[512,1024]{1,0:T(8,128)(2,1)} %refs_15_), channel_id=1, source_target_pairs={{0,1},{1,0},{2,3},{3,2},{4,5},{5,4},{6,7},{7,6},{8,9},{9,8},{10,11... | collective-permute-start | bytes 3145736 | tf_op jit(solution)/shard_map/ppermute | solution.py:41
  0.7 21.5 %collective-permute-start = (bf16[512,1024]{1,0:T(8,128)(2,1)}, bf16[512,1024]{1,0:T(8,128)(2,1)S(1)}, u32[]{:S(2)}, u32[]{:S(2)}) collective-permute-start(bf16[512,1024]{1,0:T(8,128)(2,1)} %refs_15_), channel_id=1, source_target_pairs={{0,126},{1,3},{2,0},{3,5},{4,2},{5,7},{6,4},{7,9},{8,6},{9,11},{10... | collective-permute-start | bytes 3145736 | tf_op jit(solution)/shard_map/ppermute | solution.py:36
  9.6 12.6 %collective-permute-start.2 = (bf16[512,1024]{1,0:T(8,128)(2,1)}, bf16[512,1024]{1,0:T(8,128)(2,1)S(1)}, u32[]{:S(2)}, u32[]{:S(2)}) collective-permute-start(bf16[512,1024]{1,0:T(8,128)(2,1)} %queries.5), channel_id=1, source_target_pairs={{0,1},{1,0},{2,3},{3,2},{4,5},{5,4},{6,7},{7,6},{8,9},{9,8},{10,11... | collective-permute-start | bytes 3145736 | tf_op jit(solution)/shard_map/ppermute | solution.py:41
  10.9 22.4 %collective-permute-start.3 = (bf16[512,1024]{1,0:T(8,128)(2,1)S(1)}, bf16[512,1024]{1,0:T(8,128)(2,1)S(1)}, u32[]{:S(2)}, u32[]{:S(2)}) collective-permute-start(bf16[512,1024]{1,0:T(8,128)(2,1)S(1)} %collective-permute-done.1.refs_1_.refs_16_), channel_id=1, source_target_pairs={{0,126},{1,3},{2,0},{3,5},{4,2},{5,7},{6,4},{7,9},{8,6},{9,11},{10... | collective-permute-start | bytes 3145736 | tf_op jit(solution)/shard_map/ppermute | solution.py:36
  22.2 22.4 %collective-permute-start.4 = (bf16[512,1024]{1,0:T(8,128)(2,1)S(1)}, bf16[512,1024]{1,0:T(8,128)(2,1)S(1)}, u32[]{:S(2)}, u32[]{:S(2)}) collective-permute-start(bf16[512,1024]{1,0:T(8,128)(2,1)S(1)} %collective-permute-done.refs_0_.refs_14_), channel_id=1, source_target_pairs={{0,126},{1,3},{2,0},{3,5},{4,2},{5,7},{6,4},{7,9},{8,6},{9,11},{10... | collective-permute-start | bytes 3145736 | tf_op jit(solution)/shard_map/ppermute | solution.py:36
  30.0 14.6 %collective-permute-start.5 = (bf16[512,1024]{1,0:T(8,128)(2,1)S(1)}, bf16[512,1024]{1,0:T(8,128)(2,1)S(1)}, u32[]{:S(2)}, u32[]{:S(2)}) collective-permute-start(bf16[512,1024]{1,0:T(8,128)(2,1)S(1)} %collective-permute-done.refs_0_.refs_14_), channel_id=1, source_target_pairs={{0,1},{1,0},{2,3},{3,2},{4,5},{5,4},{6,7},{7,6},{8,9},{9,8},{10,11... | collective-permute-start | bytes 3145736 | tf_op jit(solution)/shard_map/ppermute | solution.py:41
  33.3 21.9 %collective-permute-start.6 = (bf16[512,1024]{1,0:T(8,128)(2,1)S(1)}, bf16[512,1024]{1,0:T(8,128)(2,1)S(1)}, u32[]{:S(2)}, u32[]{:S(2)}) collective-permute-start(bf16[512,1024]{1,0:T(8,128)(2,1)S(1)} %collective-permute-done.3.refs_0_.refs_16_), channel_id=1, source_target_pairs={{0,1},{1,0},{2,3},{3,2},{4,5},{5,4},{6,7},{7,6},{8,9},{9,8},{10,11... | collective-permute-start | bytes 3145736 | tf_op jit(solution)/shard_map/ppermute | solution.py:41
  33.3 22.5 %collective-permute-start.7 = (bf16[512,1024]{1,0:T(8,128)(2,1)S(1)}, bf16[512,1024]{1,0:T(8,128)(2,1)S(1)}, u32[]{:S(2)}, u32[]{:S(2)}) collective-permute-start(bf16[512,1024]{1,0:T(8,128)(2,1)S(1)} %collective-permute-done.3.refs_0_.refs_16_), channel_id=1, source_target_pairs={{0,126},{1,3},{2,0},{3,5},{4,2},{5,7},{6,4},{7,9},{8,6},{9,11},{10... | collective-permute-start | bytes 3145736 | tf_op jit(solution)/shard_map/ppermute | solution.py:36
  47.2 39.4 %collective-permute-start.17 = (bf16[2,512,1024]{2,1,0:T(8,128)(2,1)S(1)}, bf16[2,512,1024]{2,1,0:T(8,128)(2,1)S(1)}, u32[]{:S(2)}, u32[]{:S(2)}) collective-permute-start(bf16[2,512,1024]{2,1,0:T(8,128)(2,1)S(1)} %pair.2.queries.refs_17_), channel_id=1, source_target_pairs={{0,126},{1,3},{2,0},{3,5},{4,2},{5,7},{6,4},{7,9},{8,6},{9,11},{10... | collective-permute-start | bytes 6291464 | tf_op jit(solution)/shard_map/ppermute | solution.py:36
  55.8 3.7 %collective-permute-start.8 = (bf16[512,1024]{1,0:T(8,128)(2,1)S(1)}, bf16[512,1024]{1,0:T(8,128)(2,1)S(1)}, u32[]{:S(2)}, u32[]{:S(2)}) collective-permute-start(bf16[512,1024]{1,0:T(8,128)(2,1)S(1)} %collective-permute-done.4.refs_0_.refs_22_), channel_id=1, source_target_pairs={{0,1},{1,0},{2,3},{3,2},{4,5},{5,4},{6,7},{7,6},{8,9},{9,8},{10,11... | collective-permute-start | bytes 3145736 | tf_op jit(solution)/shard_map/ppermute | solution.py:41
  55.8 6.7 %collective-permute-start.9 = (bf16[512,1024]{1,0:T(8,128)(2,1)S(1)}, bf16[512,1024]{1,0:T(8,128)(2,1)S(1)}, u32[]{:S(2)}, u32[]{:S(2)}) collective-permute-start(bf16[512,1024]{1,0:T(8,128)(2,1)S(1)} %collective-permute-done.7), channel_id=1, source_target_pairs={{0,1},{1,0},{2,3},{3,2},{4,5},{5,4},{6,7},{7,6},{8,9},{9,8},{10,11... | collective-permute-start | bytes 3145736 | tf_op jit(solution)/shard_map/ppermute | solution.py:41
  59.0 6.9 %collective-permute-start.11 = (f32[2,8,512]{2,1,0:T(8,128)S(1)}, f32[2,8,512]{2,1,0:T(8,128)S(1)}, u32[]{:S(2)}, u32[]{:S(2)}) collective-permute-start(f32[2,8,512]{2,1,0:T(8,128)S(1)} %get-tuple-element.149.refs_2_.st2), channel_id=1, source_target_pairs={{0,1},{1,0},{2,3},{3,2},{4,5},{5,4},{6,7},{7,6},{8,9},{9,8},{10,11... | collective-permute-start | bytes 98312 | tf_op jit(solution)/shard_map/ppermute | solution.py:41
  59.0 6.9 %collective-permute-start.10 = (f32[2,8,512]{2,1,0:T(8,128)S(1)}, f32[2,8,512]{2,1,0:T(8,128)S(1)}, u32[]{:S(2)}, u32[]{:S(2)}) collective-permute-start(f32[2,8,512]{2,1,0:T(8,128)S(1)} %get-tuple-element.144.refs_1_.st1), channel_id=1, source_target_pairs={{0,1},{1,0},{2,3},{3,2},{4,5},{5,4},{6,7},{7,6},{8,9},{9,8},{10,11... | collective-permute-start | bytes 98312 | tf_op jit(solution)/shard_map/ppermute | solution.py:41
  62.2 4.8 %collective-permute-start.12 = (f32[2,8,512]{2,1,0:T(8,128)S(1)}, f32[2,8,512]{2,1,0:T(8,128)S(1)}, u32[]{:S(2)}, u32[]{:S(2)}) collective-permute-start(f32[2,8,512]{2,1,0:T(8,128)S(1)} %get-tuple-element.151.refs_3_.st3), channel_id=1, source_target_pairs={{0,1},{1,0},{2,3},{3,2},{4,5},{5,4},{6,7},{7,6},{8,9},{9,8},{10,11... | collective-permute-start | bytes 98312 | tf_op jit(solution)/shard_map/ppermute | solution.py:41
  67.1 11.7 %collective-permute-start.15 = (f32[6,8,512]{2,1,0:T(8,128)S(1)}, f32[6,8,512]{2,1,0:T(8,128)S(1)}, u32[]{:S(2)}, u32[]{:S(2)}) collective-permute-start(f32[6,8,512]{2,1,0:T(8,128)S(1)} %near.1.refs_4_), channel_id=1, source_target_pairs={{0,2},{1,127},{2,4},{3,1},{4,6},{5,3},{6,8},{7,5},{8,10},{9,7},{10... | collective-permute-start | bytes 294920 | tf_op jit(solution)/shard_map/ppermute | solution.py:36
  78.8 7.8 %collective-permute-start.16 = (f32[6,8,512]{2,1,0:T(8,128)S(1)}, f32[6,8,512]{2,1,0:T(8,128)S(1)}, u32[]{:S(2)}, u32[]{:S(2)}) collective-permute-start(f32[6,8,512]{2,1,0:T(8,128)S(1)} %collective-permute-done.15.one.refs_5_), channel_id=1, source_target_pairs={{0,1},{1,0},{2,3},{3,2},{4,5},{5,4},{6,7},{7,6},{8,9},{9,8},{10,11... | collective-permute-start | bytes 294920 | tf_op jit(solution)/shard_map/ppermute | solution.py:41
  78.8 10.0 %collective-permute-start.18 = (f32[6,8,512]{2,1,0:T(8,128)S(1)}, f32[6,8,512]{2,1,0:T(8,128)S(1)}, u32[]{:S(2)}, u32[]{:S(2)}) collective-permute-start(f32[6,8,512]{2,1,0:T(8,128)S(1)} %collective-permute-done.15.one.refs_5_), channel_id=1, source_target_pairs={{0,2},{1,127},{2,4},{3,1},{4,6},{5,3},{6,8},{7,5},{8,10},{9,7},{10... | collective-permute-start | bytes 294920 | tf_op jit(solution)/shard_map/ppermute | solution.py:36
  78.8 7.8 %collective-permute-start.19 = (f32[2,8,512]{2,1,0:T(8,128)S(1)}, f32[2,8,512]{2,1,0:T(8,128)S(1)}, u32[]{:S(2)}, u32[]{:S(2)}) collective-permute-start(f32[2,8,512]{2,1,0:T(8,128)S(1)} %get-tuple-element.167.refs_0_.st0), channel_id=1, source_target_pairs={{0,1},{1,0},{2,3},{3,2},{4,5},{5,4},{6,7},{7,6},{8,9},{9,8},{10,11... | collective-permute-start | bytes 98312 | tf_op jit(solution)/shard_map/ppermute | solution.py:41
  88.8 8.7 %collective-permute-start.23 = (bf16[2,512,1024]{2,1,0:T(8,128)(2,1)S(1)}, bf16[2,512,1024]{2,1,0:T(8,128)(2,1)S(1)}, u32[]{:S(2)}, u32[]{:S(2)}) collective-permute-start(bf16[2,512,1024]{2,1,0:T(8,128)(2,1)S(1)} %collective-permute-done.17.refs_18_), channel_id=1, source_target_pairs={{0,1},{1,0},{2,3},{3,2},{4,5},{5,4},{6,7},{7,6},{8,9},{9,8},{10,11... | collective-permute-start | bytes 6291464 | tf_op jit(solution)/shard_map/ppermute | solution.py:41
  88.8 29.9 %collective-permute-start.27 = (bf16[2,512,1024]{2,1,0:T(8,128)(2,1)S(1)}, bf16[2,512,1024]{2,1,0:T(8,128)(2,1)S(1)}, u32[]{:S(2)}, u32[]{:S(2)}) collective-permute-start(bf16[2,512,1024]{2,1,0:T(8,128)(2,1)S(1)} %collective-permute-done.17.refs_18_), channel_id=1, source_target_pairs={{0,126},{1,3},{2,0},{3,5},{4,2},{5,7},{6,4},{7,9},{8,6},{9,11},{10... | collective-permute-start | bytes 6291464 | tf_op jit(solution)/shard_map/ppermute | solution.py:36
  97.5 9.8 %collective-permute-start.22 = (f32[2,8,512]{2,1,0:T(8,128)S(1)}, f32[2,8,512]{2,1,0:T(8,128)S(1)}, u32[]{:S(2)}, u32[]{:S(2)}) collective-permute-start(f32[2,8,512]{2,1,0:T(8,128)S(1)} %pair.3.refs_9_.refs_10_.refs_11_.refs_12_.refs_13_), channel_id=1, source_target_pairs={{0,2},{1,127},{2,4},{3,1},{4,6},{5,3},{6,8},{7,5},{8,10},{9,7},{10... | collective-permute-start | bytes 98312 | tf_op jit(solution)/shard_map/ppermute | solution.py:36
  107.3 4.7 %collective-permute-start.24 = (f32[2,8,512]{2,1,0:T(8,128)S(1)}, f32[2,8,512]{2,1,0:T(8,128)S(1)}, u32[]{:S(2)}, u32[]{:S(2)}) collective-permute-start(f32[2,8,512]{2,1,0:T(8,128)S(1)} %collective-permute-done.22.refs_10_), channel_id=1, source_target_pairs={{0,1},{1,0},{2,3},{3,2},{4,5},{5,4},{6,7},{7,6},{8,9},{9,8},{10,11... | collective-permute-start | bytes 98312 | tf_op jit(solution)/shard_map/ppermute | solution.py:41
  107.3 9.8 %collective-permute-start.25 = (f32[2,8,512]{2,1,0:T(8,128)S(1)}, f32[2,8,512]{2,1,0:T(8,128)S(1)}, u32[]{:S(2)}, u32[]{:S(2)}) collective-permute-start(f32[2,8,512]{2,1,0:T(8,128)S(1)} %collective-permute-done.22.refs_10_), channel_id=1, source_target_pairs={{0,2},{1,127},{2,4},{3,1},{4,6},{5,3},{6,8},{7,5},{8,10},{9,7},{10... | collective-permute-start | bytes 98312 | tf_op jit(solution)/shard_map/ppermute | solution.py:36
  118.7 6.5 %collective-permute-start.28 = (bf16[2,512,1024]{2,1,0:T(8,128)(2,1)S(1)}, bf16[2,512,1024]{2,1,0:T(8,128)(2,1)S(1)}, u32[]{:S(2)}, u32[]{:S(2)}) collective-permute-start(bf16[2,512,1024]{2,1,0:T(8,128)(2,1)S(1)} %collective-permute-done.27.refs_14_), channel_id=1, source_target_pairs={{0,1},{1,0},{2,3},{3,2},{4,5},{5,4},{6,7},{7,6},{8,9},{9,8},{10,11... | collective-permute-start | bytes 6291464 | tf_op jit(solution)/shard_map/ppermute | solution.py:41
  (11 other events, 90.8 us)

commit v2 on v1

--- a/solution.py
+++ b/solution.py
@@ -13,14 +13,14 @@
 BLK = 512
 WIDTH = 1024
 MIB = 1 << 20
-SLOTS = dict(own=0, s0=1, a=2, sa=-1, sb=3, b=-2, r2=4, s2=-3, r3=-4)
+SLOTS = dict(own=0, s0=1, a=-2, sa=3, sb=-1, b=2, r2=-4, r4=-3, s4=4)
 NAMES = tuple(SLOTS)
-GROUPS = (("own", "s0"), ("a", "sa"), ("sb", "b"), ("r2", "s2"), ("r3",))
+GROUPS = (("own", "s0"), ("a", "sa"), ("sb", "b"), ("r2", "r4"), ("s4",))
 PLACE = {name: i for i, name in enumerate(NAMES)}
 SPOT = {name: (g, i) for g, names in enumerate(GROUPS) for i, name in enumerate(names)}
-BACK = dict(own="own", s0="s0", a="b", b="a", r2="r3", r3="r2", sa="sa", sb="sb", s2="s2")
+BACK = dict(own="own", s0="s0", a="b", b="a", r2="s4", s4="r2", sa="sa", sb="sb", r4="r4")
 MESSAGE = dict(
-    own=(0, 0), s0=(0, 1), b=(1, 0), sa=(1, 1), sb=(2, 0), a=(2, 1), r3=(3, 0), s2=(3, 1), r2=(4, 1)
+    own=(0, 0), s0=(0, 1), b=(1, 0), sa=(1, 1), sb=(2, 0), a=(2, 1), s4=(3, 0), r4=(4, 0), r2=(4, 1)
 )
 
 VMEM = pl.BlockSpec(memory_space=pltpu.VMEM)
@@ -148,11 +148,11 @@
     loss[...] = lse - stats[0][0, 4:5]
 
 
-def near_kernel(st1, peer1, st2, peer2, st3, peer3, peer4, pay, peer_pay, out):
+def near_kernel(st1, peer1, st2, peer2, st3, peer4, pay, peer_pay, out):
     merge_into(out.at[0], st1.at[0], peer1.at[1])
     merge_into(out.at[1], st2.at[0], peer2.at[1])
-    merge_into(out.at[2], st3.at[0], peer3.at[1])
-    out[3] = peer4[0]
+    out[2] = st3[0]
+    merge_into(out.at[3], st3.at[1], peer4.at[0])
     out[4] = pay[...]
     out[5] = peer_pay[...]
 
@@ -292,39 +292,40 @@
 
     v["p_own"] = v.pop("p")
     v["p_s0"], v["q_s0"] = swap(v["p_own"]), swap(v["q"])
-    p_sb = split(v["p_s0"], -1, 1)
-    v["p_a"] = split(v["p_own"], -1, 1)
+    p_sb = split(v["p_s0"], 1, -1)
+    v["p_a"] = split(v["p_own"], 1, -1)
     stat(0)
     fence()
-    p_r2, p_sa = split(v["p_a"], -1, 1), swap(v["p_a"])
+    p_r2, p_sa = split(v["p_a"], 1, -1), swap(v["p_a"])
     v["p_sb"] = p_sb
     fence()
-    p_r4, p_b = split(v["p_sb"], -1, 1), swap(v["p_sb"])
+    p_r4, p_b = split(v["p_sb"], 1, -1), swap(v["p_sb"])
     v["q0"] = pair(v["q"], v["q_s0"])
     v["p_r2"], v["p_sa"] = p_r2, p_sa
     fence()
     stat(1)
-    q1 = split(after(v["q0"], v["st1"]), -1, 1)
-    v["p_r4"], v["p_b"] = p_r4, p_b
-    fence()
-    v["p_s2"], v["p_r3"] = swap(v["p_r2"]), swap(v["p_r4"])
+    q1 = split(after(v["q0"], v["st1"]), 1, -1)
+    v["p_b"] = p_b
     stat(2)
+    v["p_r4"] = p_r4
+    fence()
+    v["p_s4"] = swap(v["p_r4"])
     stat(3)
     stat(4)
     line = jax.ShapeDtypeStruct((1, BLK), jnp.float32)
     q_pay, query_loss = call(lse_q_kernel, "lse_q", [small(), line], v["flags"], *group_of("st"), first=SMEM)
-    x0, x1, x2, x3, x4 = (swap(stats) for stats in group_of("st"))
+    x0, x1, x2, x4 = (swap(v[stats]) for stats in ("st0", "st1", "st2", "st4"))
     near = call(
-        near_kernel, "near", small(6), v["st1"], x1, v["st2"], x2, v["st3"], x3, x4, q_pay, swap(q_pay)
-    )
-    v["one"] = split(near, 1, -1)
-    v["two"] = split(v["one"], 1, -1)
+        near_kernel, "near", small(6), v["st1"], x1, v["st2"], x2, v["st3"], x4, q_pay, swap(q_pay)
+    )
+    v["one"] = split(near, -1, 1)
+    v["two"] = split(v["one"], -1, 1)
     v["one_peer"] = swap(v["one"])
     v["x0"], v["near"], v["q_pay"] = x0, near, q_pay
     v["t0"] = tscores_of(v["p_own"], v["q0"])
     v["q1"] = q1
     fence()
-    v["q3"] = split(v["q1"], -1, 1)
+    v["q3"] = split(v["q1"], 1, -1)
     v["q2"] = swap(v["q1"])
     two_peer = swap(v["two"])
     p_pay, passage_loss = call(
@@ -335,7 +336,7 @@
     common = (v["flags"], v["pos"], v["q_pay"], p_pay, v["near"], v["one"], v["one_peer"], v["two"], two_peer)
     places = dict(
         own=("q0", 0), s0=("q0", 1), a=("q1", 0), sb=("q1", 1), sa=("q2", 0), b=("q2", 1), r2=("q3", 0),
-        s2=("q4", 0), r3=("q4", 1),
+        r4=("q3", 1), s4=("q4", 1),
     )
 
     def steps_of(side, *names):
@@ -351,11 +352,11 @@
         return steps
 
     hold = lax.optimization_barrier
-    m1 = split(m0, 1, -1)
+    m1 = split(m0, -1, 1)
     steps = steps_of("q", "own", "s0") + steps_of("p", "own", "s0", "sa", "b")
     p_total, q_total = parts("part0", common, [m0] * 5, steps, dict(p=None, q=None))
     m1, q_total, p_total = hold((m1, q_total, p_total))
-    m3 = split(m1, 1, -1)
+    m3 = split(m1, -1, 1)
     m2 = swap(m1)
     steps = steps_of("q", "sa", "b") + steps_of("p", "a", "sb")
     p_total, q_total = parts("part1", common, [m0, m1, m0, m0, m0], steps, dict(p=p_total, q=q_total))
@@ -365,10 +366,10 @@
     v["q4"] = swap(v["q3"])
     messages = [m0, m1, m2, m3, m4]
     (query_grad,) = parts(
-        "part2", common, messages, steps_of("q", "a", "sb", "s2", "r3", "r2"), dict(q=q_total), "q"
+        "part2", common, messages, steps_of("q", "a", "sb", "s4", "r4", "r2"), dict(q=q_total), "q"
     )
     v["q4"], p_total, _ = hold((v["q4"], p_total, query_grad))
-    (passage_grad,) = parts("part3", common, messages, steps_of("p", "r2", "s2", "r3"), dict(p=p_total), "p")
+    (passage_grad,) = parts("part3", common, messages, steps_of("p", "r2", "r4", "s4"), dict(p=p_total), "p")
     return (query_loss, passage_loss, query_grad, passage_grad)
 
 

time: 132 us -> 129 us (0.977)
  starting transfers between devices: 50 us -> 47.7 us
  waiting for transfers between devices: 37.2 us -> 35.6 us
    ppermute x10, starting transfers between devices: 39.6 us -> 22.4 us  [split(): return lax.ppermute(value, AXES, pairs)]
    ppermute x19 -> x17, starting transfers between devices: 10.3 us -> 25.3 us  [swap(): return lax.ppermute(value, AXES, [(i, i ^ 1) for i in range(n)])]
    ppermute x19 -> x17, waiting for transfers between devices: 3.45 us -> 2.65 us  [swap(): return lax.ppermute(value, AXES, [(i, i ^ 1) for i in range(n)])]
  transfers between devices with their start and end apart: 29 -> 27, of which waited for: 13 -> 11; matrix products, arithmetic and copies ran while one was open for 2% -> 2% of each run, Pallas kernels for 24% -> 25%
where the time goes in v2:
time: 129 us; the launch traced here: 127 us
  starting transfers between devices  47.7 us (37%)
  Pallas kernels  37.2 us (29%)
  waiting for transfers between devices  35.6 us (28%)
  local copies, waits for them, and re-layouts  3.14 us (2%)
  other arithmetic  2.08 us (2%)
  between operations  1.64 us (1%)
    ppermute x10, waiting for transfers between devices, split(): return lax.ppermute(value, AXES, pairs)  32.9 us
    ppermute x17, starting transfers between devices, swap(): return lax.ppermute(value, AXES, [(i, i ^ 1) for i in range(n)])  25.3 us
    ppermute x10, starting transfers between devices, split(): return lax.ppermute(value, AXES, pairs)  22.4 us
    pallas_call x4, Pallas kernels, parts(): pl.pallas_call(functools.partial(parts_kernel, plan, begin, last, len(arr...  21.3 us
    pallas_call x11, Pallas kernels, call(): pl.pallas_call(kernel, in_specs=[first] + [VMEM] * (len(operands) - 1), o...  15.9 us
    unnamed x12, local copies, waits for them, and re-layouts  3.14 us
    ppermute x17, waiting for transfers between devices, swap(): return lax.ppermute(value, AXES, [(i, i ^ 1) for i in range(n)])  2.65 us
  transfers between devices with their start and end apart: 27, of which 11 were waited for; matrix products, arithmetic and copies ran while one was open for 2% of the time, Pallas kernels for 25%

profile of v2, /device:TPU:0, one launch (start us, length us, event | category | flops | bytes accessed | tf_op | source)
XLA Modules:
  0.0 127.2 jit_solution(15722601512675583159)
XLA Ops:
  0.7 2.1 %collective-permute-start = (bf16[512,1024]{1,0:T(8,128)(2,1)}, bf16[512,1024]{1,0:T(8,128)(2,1)S(1)}, u32[]{:S(2)}, u32[]{:S(2)}) collective-permute-start(bf16[512,1024]{1,0:T(8,128)(2,1)} %refs_15_), channel_id=1, source_target_pairs={{0,2},{1,127},{2,4},{3,1},{4,6},{5,3},{6,8},{7,5},{8,10},{9,7},{10... | collective-permute-start | bytes 3145736 | tf_op jit(solution)/shard_map/ppermute | solution.py:36
  2.8 6.9 %collective-permute-start.2 = (bf16[512,1024]{1,0:T(8,128)(2,1)}, bf16[512,1024]{1,0:T(8,128)(2,1)S(1)}, u32[]{:S(2)}, u32[]{:S(2)}) collective-permute-start(bf16[512,1024]{1,0:T(8,128)(2,1)} %queries.5), channel_id=1, source_target_pairs={{0,1},{1,0},{2,3},{3,2},{4,5},{5,4},{6,7},{7,6},{8,9},{9,8},{10,11... | collective-permute-start | bytes 3145736 | tf_op jit(solution)/shard_map/ppermute | solution.py:41
  15.7 2.9 %stats0.1 = (f32[2,512,512]{2,1,0:T(8,128)S(1)}, f32[2,8,512]{2,1,0:T(8,128)S(1)}) custom-call(s32[9]{0:T(128)S(1)} %or_convert_fusion.flags.refs_0_, s32[1,512]{1,0:T(1,128)S(1)} %copy-done.4, bf16[512,1024]{1,0:T(8,128)(2,1)S(1)} %copy-done, bf16[512,1024]{1,0:T(8,128)(2,1)S(1)} %copy-done.2, bf16[512,1024]{1,0:T(8,128)(2,1)S(1)} %collective-permute-done.1.refs_1_.refs_16_), custom_call_target="tpu_custom_call" | custom-call | tf_op jit(solution)/shard_map/stats0/pallas_call | solution.py:53
  18.6 3.9 %collective-permute-done.refs_0_.refs_14_ = bf16[512,1024]{1,0:T(8,128)(2,1)S(1)} collective-permute-done((bf16[512,1024]{1,0:T(8,128)(2,1)}, bf16[512,1024]{1,0:T(8,128)(2,1)S(1)}, u32[]{:S(2)}, u32[]{:S(2)}) %collective-permute-start) | collective-permute-done | bytes 1048608 | tf_op jit(solution)/shard_map/ppermute | solution.py:36
  22.6 6.4 %collective-permute-start.5 = (bf16[512,1024]{1,0:T(8,128)(2,1)S(1)}, bf16[512,1024]{1,0:T(8,128)(2,1)S(1)}, u32[]{:S(2)}, u32[]{:S(2)}) collective-permute-start(bf16[512,1024]{1,0:T(8,128)(2,1)S(1)} %collective-permute-done.refs_0_.refs_14_), channel_id=1, source_target_pairs={{0,1},{1,0},{2,3},{3,2},{4,5},{5,4},{6,7},{7,6},{8,9},{9,8},{10,11... | collective-permute-start | bytes 3145736 | tf_op jit(solution)/shard_map/ppermute | solution.py:41
  29.0 4.8 %collective-permute-done.3.refs_0_.refs_16_ = bf16[512,1024]{1,0:T(8,128)(2,1)S(1)} collective-permute-done((bf16[512,1024]{1,0:T(8,128)(2,1)S(1)}, bf16[512,1024]{1,0:T(8,128)(2,1)S(1)}, u32[]{:S(2)}, u32[]{:S(2)}) %collective-permute-start.3) | collective-permute-done | bytes 1048608 | tf_op jit(solution)/shard_map/ppermute | solution.py:36
  33.9 11.1 %collective-permute-done.4.refs_0_.refs_22_ = bf16[512,1024]{1,0:T(8,128)(2,1)S(1)} collective-permute-done((bf16[512,1024]{1,0:T(8,128)(2,1)S(1)}, bf16[512,1024]{1,0:T(8,128)(2,1)S(1)}, u32[]{:S(2)}, u32[]{:S(2)}) %collective-permute-start.4) | collective-permute-done | bytes 1048608 | tf_op jit(solution)/shard_map/ppermute | solution.py:36
  45.0 2.7 %stats1.1 = (f32[2,512,512]{2,1,0:T(8,128)S(1)}, f32[2,8,512]{2,1,0:T(8,128)S(1)}) custom-call(s32[9]{0:T(128)S(1)} %or_convert_fusion.flags.refs_0_, s32[1,512]{1,0:T(1,128)S(1)} %copy-done.4, bf16[512,1024]{1,0:T(8,128)(2,1)S(1)} %copy-done.1, bf16[512,1024]{1,0:T(8,128)(2,1)S(1)} %collective-permute-done.refs_0_.refs_14_, ...), custom_call_target="tpu_custom_call" | custom-call | tf_op jit(solution)/shard_map/stats1/pallas_call | solution.py:53
  47.8 2.7 %stats2.1 = (f32[2,512,512]{2,1,0:T(8,128)S(1)}, f32[2,8,512]{2,1,0:T(8,128)S(1)}) custom-call(s32[9]{0:T(128)S(1)} %or_convert_fusion.flags.refs_0_, s32[1,512]{1,0:T(1,128)S(1)} %copy-done.4, bf16[512,1024]{1,0:T(8,128)(2,1)S(1)} %copy-done.1, bf16[512,1024]{1,0:T(8,128)(2,1)S(1)} %collective-permute-done.3.refs_0_.refs_16_, ...), custom_call_target="tpu_custom_call" | custom-call | tf_op jit(solution)/shard_map/stats2/pallas_call | solution.py:53
  50.4 5.8 %collective-permute-done.7.refs_1_.refs_20_ = bf16[512,1024]{1,0:T(8,128)(2,1)S(1)} collective-permute-done((bf16[512,1024]{1,0:T(8,128)(2,1)S(1)}, bf16[512,1024]{1,0:T(8,128)(2,1)S(1)}, u32[]{:S(2)}, u32[]{:S(2)}) %collective-permute-start.7) | collective-permute-done | bytes 1048608 | tf_op jit(solution)/shard_map/ppermute | solution.py:36
  57.4 2.7 %stats3.1 = (f32[2,512,512]{2,1,0:T(8,128)S(1)}, f32[2,8,512]{2,1,0:T(8,128)S(1)}) custom-call(s32[9]{0:T(128)S(1)} %or_convert_fusion.flags.refs_0_, s32[1,512]{1,0:T(1,128)S(1)} %copy-done.4, bf16[512,1024]{1,0:T(8,128)(2,1)S(1)} %copy-done.1, bf16[512,1024]{1,0:T(8,128)(2,1)S(1)} %collective-permute-done.4.refs_0_.refs_22_, ...), custom_call_target="tpu_custom_call" | custom-call | tf_op jit(solution)/shard_map/stats3/pallas_call | solution.py:53
  60.1 1.8 %stats4.1 = (f32[1,512,512]{2,1,0:T(8,128)S(1)}, f32[1,8,512]{2,1,0:T(8,128)S(1)}) custom-call(s32[9]{0:T(128)S(1)} %or_convert_fusion.flags.refs_0_, s32[1,512]{1,0:T(1,128)S(1)} %copy-done.4, bf16[512,1024]{1,0:T(8,128)(2,1)S(1)} %copy-done.1, bf16[512,1024]{1,0:T(8,128)(2,1)S(1)} %collective-permute-done.8.refs_0_.refs_18_), custom_call_target="tpu_custom_call" | custom-call | tf_op jit(solution)/shard_map/stats4/pallas_call | solution.py:53
  64.4 6.1 %collective-permute-start.13 = (f32[6,8,512]{2,1,0:T(8,128)S(1)}, f32[6,8,512]{2,1,0:T(8,128)S(1)}, u32[]{:S(2)}, u32[]{:S(2)}) collective-permute-start(f32[6,8,512]{2,1,0:T(8,128)S(1)} %near.1.refs_4_), channel_id=1, source_target_pairs={{0,126},{1,3},{2,0},{3,5},{4,2},{5,7},{6,4},{7,9},{8,6},{9,11},{10... | collective-permute-start | bytes 294920 | tf_op jit(solution)/shard_map/ppermute | solution.py:36
  70.5 3.3 %collective-permute-done.13.one.refs_5_ = f32[6,8,512]{2,1,0:T(8,128)S(1)} collective-permute-done((f32[6,8,512]{2,1,0:T(8,128)S(1)}, f32[6,8,512]{2,1,0:T(8,128)S(1)}, u32[]{:S(2)}, u32[]{:S(2)}) %collective-permute-start.13) | collective-permute-done | bytes 98336 | tf_op jit(solution)/shard_map/ppermute | solution.py:36
  73.8 1.3 %collective-permute-start.14 = (f32[6,8,512]{2,1,0:T(8,128)S(1)}, f32[6,8,512]{2,1,0:T(8,128)S(1)}, u32[]{:S(2)}, u32[]{:S(2)}) collective-permute-start(f32[6,8,512]{2,1,0:T(8,128)S(1)} %collective-permute-done.13.one.refs_5_), channel_id=1, source_target_pairs={{0,1},{1,0},{2,3},{3,2},{4,5},{5,4},{6,7},{7,6},{8,9},{9,8},{10,11... | collective-permute-start | bytes 294920 | tf_op jit(solution)/shard_map/ppermute | solution.py:41
  75.1 6.6 %collective-permute-start.16 = (f32[6,8,512]{2,1,0:T(8,128)S(1)}, f32[6,8,512]{2,1,0:T(8,128)S(1)}, u32[]{:S(2)}, u32[]{:S(2)}) collective-permute-start(f32[6,8,512]{2,1,0:T(8,128)S(1)} %collective-permute-done.13.one.refs_5_), channel_id=1, source_target_pairs={{0,126},{1,3},{2,0},{3,5},{4,2},{5,7},{6,4},{7,9},{8,6},{9,11},{10... | collective-permute-start | bytes 294920 | tf_op jit(solution)/shard_map/ppermute | solution.py:36
  84.0 7.9 %collective-permute-start.18 = (f32[6,8,512]{2,1,0:T(8,128)S(1)}, f32[6,8,512]{2,1,0:T(8,128)S(1)}, u32[]{:S(2)}, u32[]{:S(2)}) collective-permute-start(f32[6,8,512]{2,1,0:T(8,128)S(1)} %collective-permute-done.16.two.refs_7_), channel_id=1, source_target_pairs={{0,1},{1,0},{2,3},{3,2},{4,5},{5,4},{6,7},{7,6},{8,9},{9,8},{10,11... | collective-permute-start | bytes 294920 | tf_op jit(solution)/shard_map/ppermute | solution.py:41
  94.7 3.1 %collective-permute-start.20 = (f32[2,8,512]{2,1,0:T(8,128)S(1)}, f32[2,8,512]{2,1,0:T(8,128)S(1)}, u32[]{:S(2)}, u32[]{:S(2)}) collective-permute-start(f32[2,8,512]{2,1,0:T(8,128)S(1)} %pair.3.refs_9_.refs_10_.refs_11_.refs_12_.refs_13_), channel_id=1, source_target_pairs={{0,126},{1,3},{2,0},{3,5},{4,2},{5,7},{6,4},{7,9},{8,6},{9,11},{10... | collective-permute-start | bytes 98312 | tf_op jit(solution)/shard_map/ppermute | solution.py:36
  97.9 6.0 %part0.1 = (f32[512,1024]{1,0:T(8,128)S(1)}, f32[512,1024]{1,0:T(8,128)S(1)}) custom-call(s32[9]{0:T(128)S(1)} %or_convert_fusion.flags.refs_0_, s32[1,512]{1,0:T(1,128)S(1)} %copy-done.5, f32[8,512]{1,0:T(8,128)S(1)} %get-tuple-element.179.pay.refs_2_, f32[8,512]{1,0:T(8,128)S(1)} %get-tuple-element.180.mine.refs_3_, f32[6,8,512]{2,1,0:T(8,128)S(1)} %near.1.refs_4_, ...), custom_call_target="tpu_custom_call" | custom-call | tf_op jit(solution)/shard_map/part0/pallas_call | solution.py:258
  104.0 4.4 %collective-permute-start.23 = (f32[2,8,512]{2,1,0:T(8,128)S(1)}, f32[2,8,512]{2,1,0:T(8,128)S(1)}, u32[]{:S(2)}, u32[]{:S(2)}) collective-permute-start(f32[2,8,512]{2,1,0:T(8,128)S(1)} %collective-permute-done.20.refs_10_), channel_id=1, source_target_pairs={{0,126},{1,3},{2,0},{3,5},{4,2},{5,7},{6,4},{7,9},{8,6},{9,11},{10... | collective-permute-start | bytes 98312 | tf_op jit(solution)/shard_map/ppermute | solution.py:36
  108.3 4.7 %part1.1 = (f32[512,1024]{1,0:T(8,128)S(1)}, f32[512,1024]{1,0:T(8,128)S(1)}) custom-call(s32[9]{0:T(128)S(1)} %or_convert_fusion.flags.refs_0_, s32[1,512]{1,0:T(1,128)S(1)} %copy-done.5, f32[8,512]{1,0:T(8,128)S(1)} %get-tuple-element.179.pay.refs_2_, f32[8,512]{1,0:T(8,128)S(1)} %get-tuple-element.180.mine.refs_3_, f32[6,8,512]{2,1,0:T(8,128)S(1)} %near.1.refs_4_, ...), custom_call_target="tpu_custom_call" | custom-call | tf_op jit(solution)/shard_map/part1/pallas_call | solution.py:258
  113.3 3.1 %collective-permute-done.25.refs_14_ = bf16[2,512,1024]{2,1,0:T(8,128)(2,1)S(1)} collective-permute-done((bf16[2,512,1024]{2,1,0:T(8,128)(2,1)S(1)}, bf16[2,512,1024]{2,1,0:T(8,128)(2,1)S(1)}, u32[]{:S(2)}, u32[]{:S(2)}) %collective-permute-start.25) | collective-permute-done | bytes 2097184 | tf_op jit(solution)/shard_map/ppermute | solution.py:36
  116.5 4.9 %part2.1 = f32[512,1024]{1,0:T(8,128)} custom-call(s32[9]{0:T(128)S(1)} %or_convert_fusion.flags.refs_0_, s32[1,512]{1,0:T(1,128)S(1)} %copy-done.5, f32[8,512]{1,0:T(8,128)S(1)} %get-tuple-element.179.pay.refs_2_, f32[8,512]{1,0:T(8,128)S(1)} %get-tuple-element.180.mine.refs_3_, f32[6,8,512]{2,1,0:T(8,128)S(1)} %near.1.refs_4_, ...), custom_call_target="tpu_custom_call" | custom-call | tf_op jit(solution)/shard_map/part2/pallas_call | solution.py:258
  121.4 5.7 %part3.1 = f32[512,1024]{1,0:T(8,128)} custom-call(s32[9]{0:T(128)S(1)} %or_convert_fusion.flags.refs_0_, s32[1,512]{1,0:T(1,128)S(1)} %copy-done.5, f32[8,512]{1,0:T(8,128)S(1)} %get-tuple-element.179.pay.refs_2_, f32[8,512]{1,0:T(8,128)S(1)} %get-tuple-element.180.mine.refs_3_, f32[6,8,512]{2,1,0:T(8,128)S(1)} %near.1.refs_4_, ...), custom_call_target="tpu_custom_call" | custom-call | tf_op jit(solution)/shard_map/part3/pallas_call | solution.py:258
  (61 shorter events, 14.8 us)
Async XLA Ops:
  0.6 11.2 %collective-permute-start.1 = (bf16[512,1024]{1,0:T(8,128)(2,1)}, bf16[512,1024]{1,0:T(8,128)(2,1)S(1)}, u32[]{:S(2)}, u32[]{:S(2)}) collective-permute-start(bf16[512,1024]{1,0:T(8,128)(2,1)} %refs_15_), channel_id=1, source_target_pairs={{0,1},{1,0},{2,3},{3,2},{4,5},{5,4},{6,7},{7,6},{8,9},{9,8},{10,11... | collective-permute-start | bytes 3145736 | tf_op jit(solution)/shard_map/ppermute | solution.py:41
  0.7 21.8 %collective-permute-start = (bf16[512,1024]{1,0:T(8,128)(2,1)}, bf16[512,1024]{1,0:T(8,128)(2,1)S(1)}, u32[]{:S(2)}, u32[]{:S(2)}) collective-permute-start(bf16[512,1024]{1,0:T(8,128)(2,1)} %refs_15_), channel_id=1, source_target_pairs={{0,2},{1,127},{2,4},{3,1},{4,6},{5,3},{6,8},{7,5},{8,10},{9,7},{10... | collective-permute-start | bytes 3145736 | tf_op jit(solution)/shard_map/ppermute | solution.py:36
  2.8 19.8 %collective-permute-start.2 = (bf16[512,1024]{1,0:T(8,128)(2,1)}, bf16[512,1024]{1,0:T(8,128)(2,1)S(1)}, u32[]{:S(2)}, u32[]{:S(2)}) collective-permute-start(bf16[512,1024]{1,0:T(8,128)(2,1)} %queries.5), channel_id=1, source_target_pairs={{0,1},{1,0},{2,3},{3,2},{4,5},{5,4},{6,7},{7,6},{8,9},{9,8},{10,11... | collective-permute-start | bytes 3145736 | tf_op jit(solution)/shard_map/ppermute | solution.py:41
  11.8 22.0 %collective-permute-start.3 = (bf16[512,1024]{1,0:T(8,128)(2,1)S(1)}, bf16[512,1024]{1,0:T(8,128)(2,1)S(1)}, u32[]{:S(2)}, u32[]{:S(2)}) collective-permute-start(bf16[512,1024]{1,0:T(8,128)(2,1)S(1)} %collective-permute-done.1.refs_1_.refs_16_), channel_id=1, source_target_pairs={{0,2},{1,127},{2,4},{3,1},{4,6},{5,3},{6,8},{7,5},{8,10},{9,7},{10... | collective-permute-start | bytes 3145736 | tf_op jit(solution)/shard_map/ppermute | solution.py:36
  22.6 22.5 %collective-permute-start.4 = (bf16[512,1024]{1,0:T(8,128)(2,1)S(1)}, bf16[512,1024]{1,0:T(8,128)(2,1)S(1)}, u32[]{:S(2)}, u32[]{:S(2)}) collective-permute-start(bf16[512,1024]{1,0:T(8,128)(2,1)S(1)} %collective-permute-done.refs_0_.refs_14_), channel_id=1, source_target_pairs={{0,2},{1,127},{2,4},{3,1},{4,6},{5,3},{6,8},{7,5},{8,10},{9,7},{10... | collective-permute-start | bytes 3145736 | tf_op jit(solution)/shard_map/ppermute | solution.py:36
  22.6 22.5 %collective-permute-start.5 = (bf16[512,1024]{1,0:T(8,128)(2,1)S(1)}, bf16[512,1024]{1,0:T(8,128)(2,1)S(1)}, u32[]{:S(2)}, u32[]{:S(2)}) collective-permute-start(bf16[512,1024]{1,0:T(8,128)(2,1)S(1)} %collective-permute-done.refs_0_.refs_14_), channel_id=1, source_target_pairs={{0,1},{1,0},{2,3},{3,2},{4,5},{5,4},{6,7},{7,6},{8,9},{9,8},{10,11... | collective-permute-start | bytes 3145736 | tf_op jit(solution)/shard_map/ppermute | solution.py:41
  33.8 14.0 %collective-permute-start.6 = (bf16[512,1024]{1,0:T(8,128)(2,1)S(1)}, bf16[512,1024]{1,0:T(8,128)(2,1)S(1)}, u32[]{:S(2)}, u32[]{:S(2)}) collective-permute-start(bf16[512,1024]{1,0:T(8,128)(2,1)S(1)} %collective-permute-done.3.refs_0_.refs_16_), channel_id=1, source_target_pairs={{0,1},{1,0},{2,3},{3,2},{4,5},{5,4},{6,7},{7,6},{8,9},{9,8},{10,11... | collective-permute-start | bytes 3145736 | tf_op jit(solution)/shard_map/ppermute | solution.py:41
  33.8 22.5 %collective-permute-start.7 = (bf16[512,1024]{1,0:T(8,128)(2,1)S(1)}, bf16[512,1024]{1,0:T(8,128)(2,1)S(1)}, u32[]{:S(2)}, u32[]{:S(2)}) collective-permute-start(bf16[512,1024]{1,0:T(8,128)(2,1)S(1)} %collective-permute-done.3.refs_0_.refs_16_), channel_id=1, source_target_pairs={{0,2},{1,127},{2,4},{3,1},{4,6},{5,3},{6,8},{7,5},{8,10},{9,7},{10... | collective-permute-start | bytes 3145736 | tf_op jit(solution)/shard_map/ppermute | solution.py:36
  47.7 35.3 %collective-permute-start.15 = (bf16[2,512,1024]{2,1,0:T(8,128)(2,1)S(1)}, bf16[2,512,1024]{2,1,0:T(8,128)(2,1)S(1)}, u32[]{:S(2)}, u32[]{:S(2)}) collective-permute-start(bf16[2,512,1024]{2,1,0:T(8,128)(2,1)S(1)} %pair.2.queries.refs_17_), channel_id=1, source_target_pairs={{0,2},{1,127},{2,4},{3,1},{4,6},{5,3},{6,8},{7,5},{8,10},{9,7},{10... | collective-permute-start | bytes 6291464 | tf_op jit(solution)/shard_map/ppermute | solution.py:36
  56.3 3.8 %collective-permute-start.8 = (bf16[512,1024]{1,0:T(8,128)(2,1)S(1)}, bf16[512,1024]{1,0:T(8,128)(2,1)S(1)}, u32[]{:S(2)}, u32[]{:S(2)}) collective-permute-start(bf16[512,1024]{1,0:T(8,128)(2,1)S(1)} %collective-permute-done.7.refs_1_.refs_20_), channel_id=1, source_target_pairs={{0,1},{1,0},{2,3},{3,2},{4,5},{5,4},{6,7},{7,6},{8,9},{9,8},{10,11... | collective-permute-start | bytes 3145736 | tf_op jit(solution)/shard_map/ppermute | solution.py:41
  56.9 6.6 %collective-permute-start.10 = (f32[2,8,512]{2,1,0:T(8,128)S(1)}, f32[2,8,512]{2,1,0:T(8,128)S(1)}, u32[]{:S(2)}, u32[]{:S(2)}) collective-permute-start(f32[2,8,512]{2,1,0:T(8,128)S(1)} %get-tuple-element.149.refs_2_.st2), channel_id=1, source_target_pairs={{0,1},{1,0},{2,3},{3,2},{4,5},{5,4},{6,7},{7,6},{8,9},{9,8},{10,11... | collective-permute-start | bytes 98312 | tf_op jit(solution)/shard_map/ppermute | solution.py:41
  57.0 6.5 %collective-permute-start.9 = (f32[2,8,512]{2,1,0:T(8,128)S(1)}, f32[2,8,512]{2,1,0:T(8,128)S(1)}, u32[]{:S(2)}, u32[]{:S(2)}) collective-permute-start(f32[2,8,512]{2,1,0:T(8,128)S(1)} %get-tuple-element.148.refs_1_.st1), channel_id=1, source_target_pairs={{0,1},{1,0},{2,3},{3,2},{4,5},{5,4},{6,7},{7,6},{8,9},{9,8},{10,11... | collective-permute-start | bytes 98312 | tf_op jit(solution)/shard_map/ppermute | solution.py:41
  64.4 9.4 %collective-permute-start.13 = (f32[6,8,512]{2,1,0:T(8,128)S(1)}, f32[6,8,512]{2,1,0:T(8,128)S(1)}, u32[]{:S(2)}, u32[]{:S(2)}) collective-permute-start(f32[6,8,512]{2,1,0:T(8,128)S(1)} %near.1.refs_4_), channel_id=1, source_target_pairs={{0,126},{1,3},{2,0},{3,5},{4,2},{5,7},{6,4},{7,9},{8,6},{9,11},{10... | collective-permute-start | bytes 294920 | tf_op jit(solution)/shard_map/ppermute | solution.py:36
  73.8 9.2 %collective-permute-start.14 = (f32[6,8,512]{2,1,0:T(8,128)S(1)}, f32[6,8,512]{2,1,0:T(8,128)S(1)}, u32[]{:S(2)}, u32[]{:S(2)}) collective-permute-start(f32[6,8,512]{2,1,0:T(8,128)S(1)} %collective-permute-done.13.one.refs_5_), channel_id=1, source_target_pairs={{0,1},{1,0},{2,3},{3,2},{4,5},{5,4},{6,7},{7,6},{8,9},{9,8},{10,11... | collective-permute-start | bytes 294920 | tf_op jit(solution)/shard_map/ppermute | solution.py:41
  75.1 8.8 %collective-permute-start.16 = (f32[6,8,512]{2,1,0:T(8,128)S(1)}, f32[6,8,512]{2,1,0:T(8,128)S(1)}, u32[]{:S(2)}, u32[]{:S(2)}) collective-permute-start(f32[6,8,512]{2,1,0:T(8,128)S(1)} %collective-permute-done.13.one.refs_5_), channel_id=1, source_target_pairs={{0,126},{1,3},{2,0},{3,5},{4,2},{5,7},{6,4},{7,9},{8,6},{9,11},{10... | collective-permute-start | bytes 294920 | tf_op jit(solution)/shard_map/ppermute | solution.py:36
  81.7 1.3 %collective-permute-start.17 = (f32[2,8,512]{2,1,0:T(8,128)S(1)}, f32[2,8,512]{2,1,0:T(8,128)S(1)}, u32[]{:S(2)}, u32[]{:S(2)}) collective-permute-start(f32[2,8,512]{2,1,0:T(8,128)S(1)} %get-tuple-element.171.refs_0_.st0), channel_id=1, source_target_pairs={{0,1},{1,0},{2,3},{3,2},{4,5},{5,4},{6,7},{7,6},{8,9},{9,8},{10,11... | collective-permute-start | bytes 98312 | tf_op jit(solution)/shard_map/ppermute | solution.py:41
  83.9 13.9 %collective-permute-start.21 = (bf16[2,512,1024]{2,1,0:T(8,128)(2,1)S(1)}, bf16[2,512,1024]{2,1,0:T(8,128)(2,1)S(1)}, u32[]{:S(2)}, u32[]{:S(2)}) collective-permute-start(bf16[2,512,1024]{2,1,0:T(8,128)(2,1)S(1)} %collective-permute-done.15.refs_18_), channel_id=1, source_target_pairs={{0,1},{1,0},{2,3},{3,2},{4,5},{5,4},{6,7},{7,6},{8,9},{9,8},{10,11... | collective-permute-start | bytes 6291464 | tf_op jit(solution)/shard_map/ppermute | solution.py:41
  84.0 32.4 %collective-permute-start.25 = (bf16[2,512,1024]{2,1,0:T(8,128)(2,1)S(1)}, bf16[2,512,1024]{2,1,0:T(8,128)(2,1)S(1)}, u32[]{:S(2)}, u32[]{:S(2)}) collective-permute-start(bf16[2,512,1024]{2,1,0:T(8,128)(2,1)S(1)} %collective-permute-done.15.refs_18_), channel_id=1, source_target_pairs={{0,2},{1,127},{2,4},{3,1},{4,6},{5,3},{6,8},{7,5},{8,10},{9,7},{10... | collective-permute-start | bytes 6291464 | tf_op jit(solution)/shard_map/ppermute | solution.py:36
  84.0 8.9 %collective-permute-start.18 = (f32[6,8,512]{2,1,0:T(8,128)S(1)}, f32[6,8,512]{2,1,0:T(8,128)S(1)}, u32[]{:S(2)}, u32[]{:S(2)}) collective-permute-start(f32[6,8,512]{2,1,0:T(8,128)S(1)} %collective-permute-done.16.two.refs_7_), channel_id=1, source_target_pairs={{0,1},{1,0},{2,3},{3,2},{4,5},{5,4},{6,7},{7,6},{8,9},{9,8},{10,11... | collective-permute-start | bytes 294920 | tf_op jit(solution)/shard_map/ppermute | solution.py:41
  94.7 9.1 %collective-permute-start.20 = (f32[2,8,512]{2,1,0:T(8,128)S(1)}, f32[2,8,512]{2,1,0:T(8,128)S(1)}, u32[]{:S(2)}, u32[]{:S(2)}) collective-permute-start(f32[2,8,512]{2,1,0:T(8,128)S(1)} %pair.3.refs_9_.refs_10_.refs_11_.refs_12_.refs_13_), channel_id=1, source_target_pairs={{0,126},{1,3},{2,0},{3,5},{4,2},{5,7},{6,4},{7,9},{8,6},{9,11},{10... | collective-permute-start | bytes 98312 | tf_op jit(solution)/shard_map/ppermute | solution.py:36
  103.9 9.2 %collective-permute-start.22 = (f32[2,8,512]{2,1,0:T(8,128)S(1)}, f32[2,8,512]{2,1,0:T(8,128)S(1)}, u32[]{:S(2)}, u32[]{:S(2)}) collective-permute-start(f32[2,8,512]{2,1,0:T(8,128)S(1)} %collective-permute-done.20.refs_10_), channel_id=1, source_target_pairs={{0,1},{1,0},{2,3},{3,2},{4,5},{5,4},{6,7},{7,6},{8,9},{9,8},{10,11... | collective-permute-start | bytes 98312 | tf_op jit(solution)/shard_map/ppermute | solution.py:41
  104.0 9.1 %collective-permute-start.23 = (f32[2,8,512]{2,1,0:T(8,128)S(1)}, f32[2,8,512]{2,1,0:T(8,128)S(1)}, u32[]{:S(2)}, u32[]{:S(2)}) collective-permute-start(f32[2,8,512]{2,1,0:T(8,128)S(1)} %collective-permute-done.20.refs_10_), channel_id=1, source_target_pairs={{0,126},{1,3},{2,0},{3,5},{4,2},{5,7},{6,4},{7,9},{8,6},{9,11},{10... | collective-permute-start | bytes 98312 | tf_op jit(solution)/shard_map/ppermute | solution.py:36
  113.1 3.4 %collective-permute-start.24 = (f32[2,8,512]{2,1,0:T(8,128)S(1)}, f32[2,8,512]{2,1,0:T(8,128)S(1)}, u32[]{:S(2)}, u32[]{:S(2)}) collective-permute-start(f32[2,8,512]{2,1,0:T(8,128)S(1)} %collective-permute-done.23.refs_12_), channel_id=1, source_target_pairs={{0,1},{1,0},{2,3},{3,2},{4,5},{5,4},{6,7},{7,6},{8,9},{9,8},{10,11... | collective-permute-start | bytes 98312 | tf_op jit(solution)/shard_map/ppermute | solution.py:41
  116.5 4.9 %collective-permute-start.26 = (bf16[2,512,1024]{2,1,0:T(8,128)(2,1)S(1)}, bf16[2,512,1024]{2,1,0:T(8,128)(2,1)S(1)}, u32[]{:S(2)}, u32[]{:S(2)}) collective-permute-start(bf16[2,512,1024]{2,1,0:T(8,128)(2,1)S(1)} %collective-permute-done.25.refs_14_), channel_id=1, source_target_pairs={{0,1},{1,0},{2,3},{3,2},{4,5},{5,4},{6,7},{7,6},{8,9},{9,8},{10,11... | collective-permute-start | bytes 6291464 | tf_op jit(solution)/shard_map/ppermute | solution.py:41
  (9 other events, 83.8 us)

commit v3 on v2

--- a/solution.py
+++ b/solution.py
@@ -319,7 +319,7 @@
         near_kernel, "near", small(6), v["st1"], x1, v["st2"], x2, v["st3"], x4, q_pay, swap(q_pay)
     )
     v["one"] = split(near, -1, 1)
-    v["two"] = split(v["one"], -1, 1)
+    v["two"] = split(near, -2, 2)
     v["one_peer"] = swap(v["one"])
     v["x0"], v["near"], v["q_pay"] = x0, near, q_pay
     v["t0"] = tscores_of(v["p_own"], v["q0"])
@@ -365,11 +365,10 @@
     m4, v["q3"] = hold((m4, v["q3"]))
     v["q4"] = swap(v["q3"])
     messages = [m0, m1, m2, m3, m4]
-    (query_grad,) = parts(
-        "part2", common, messages, steps_of("q", "a", "sb", "s4", "r4", "r2"), dict(q=q_total), "q"
-    )
+    steps = steps_of("p", "r2", "r4") + steps_of("q", "a", "sb", "s4", "r4", "r2")
+    p_total, query_grad = parts("part2", common, messages, steps, dict(p=p_total, q=q_total), "q")
     v["q4"], p_total, _ = hold((v["q4"], p_total, query_grad))
-    (passage_grad,) = parts("part3", common, messages, steps_of("p", "r2", "r4", "s4"), dict(p=p_total), "p")
+    (passage_grad,) = parts("part3", common, messages, steps_of("p", "s4"), dict(p=p_total), "p")
     return (query_loss, passage_loss, query_grad, passage_grad)
 
 

time: 129 us -> 127 us (0.984)
  starting transfers between devices: 47.7 us -> 39.9 us
  waiting for transfers between devices: 35.6 us -> 41.4 us
    ppermute x10, starting transfers between devices: 22.4 us -> 15.9 us  [split(): return lax.ppermute(value, AXES, pairs)]
    ppermute x10, waiting for transfers between devices: 32.9 us -> 38.8 us  [split(): return lax.ppermute(value, AXES, pairs)]
  transfers between devices with their start and end apart: 27 -> 27, of which waited for: 11 -> 11; matrix products, arithmetic and copies ran while one was open for 2% -> 2% of each run, Pallas kernels for 25% -> 27%
where the time goes in v3:
time: 127 us; the launch traced here: 125 us
  waiting for transfers between devices  41.4 us (33%)
  starting transfers between devices  39.9 us (31%)
  Pallas kernels  36.9 us (29%)
  local copies, waits for them, and re-layouts  3.14 us (2%)
  other arithmetic  2.08 us (2%)
  between operations  1.65 us (1%)
    ppermute x10, waiting for transfers between devices, split(): return lax.ppermute(value, AXES, pairs)  38.8 us
    ppermute x17, starting transfers between devices, swap(): return lax.ppermute(value, AXES, [(i, i ^ 1) for i in range(n)])  24 us
    pallas_call x4, Pallas kernels, parts(): pl.pallas_call(functools.partial(parts_kernel, plan, begin, last, len(arr...  21.1 us
    ppermute x10, starting transfers between devices, split(): return lax.ppermute(value, AXES, pairs)  15.9 us
    pallas_call x11, Pallas kernels, call(): pl.pallas_call(kernel, in_specs=[first] + [VMEM] * (len(operands) - 1), o...  15.9 us
    unnamed x12, local copies, waits for them, and re-layouts  3.14 us
    ppermute x17, waiting for transfers between devices, swap(): return lax.ppermute(value, AXES, [(i, i ^ 1) for i in range(n)])  2.65 us
  transfers between devices with their start and end apart: 27, of which 11 were waited for; matrix products, arithmetic and copies ran while one was open for 2% of the time, Pallas kernels for 27%

profile of v3, /device:TPU:0, one launch (start us, length us, event | category | flops | bytes accessed | tf_op | source)
XLA Modules:
  0.0 125.2 jit_solution(15771061984980619907)
XLA Ops:
  0.7 2.1 %collective-permute-start = (bf16[512,1024]{1,0:T(8,128)(2,1)}, bf16[512,1024]{1,0:T(8,128)(2,1)S(1)}, u32[]{:S(2)}, u32[]{:S(2)}) collective-permute-start(bf16[512,1024]{1,0:T(8,128)(2,1)} %refs_15_.1), channel_id=1, source_target_pairs={{0,2},{1,127},{2,4},{3,1},{4,6},{5,3},{6,8},{7,5},{8,10},{9,7},{10... | collective-permute-start | bytes 3145736 | tf_op jit(solution)/shard_map/ppermute | solution.py:36
  2.8 6.9 %collective-permute-start.2 = (bf16[512,1024]{1,0:T(8,128)(2,1)}, bf16[512,1024]{1,0:T(8,128)(2,1)S(1)}, u32[]{:S(2)}, u32[]{:S(2)}) collective-permute-start(bf16[512,1024]{1,0:T(8,128)(2,1)} %queries.5), channel_id=1, source_target_pairs={{0,1},{1,0},{2,3},{3,2},{4,5},{5,4},{6,7},{7,6},{8,9},{9,8},{10,11... | collective-permute-start | bytes 3145736 | tf_op jit(solution)/shard_map/ppermute | solution.py:41
  15.7 2.9 %stats0.1 = (f32[2,512,512]{2,1,0:T(8,128)S(1)}, f32[2,8,512]{2,1,0:T(8,128)S(1)}) custom-call(s32[9]{0:T(128)S(1)} %or_convert_fusion.flags.refs_0_, s32[1,512]{1,0:T(1,128)S(1)} %copy-done.4, bf16[512,1024]{1,0:T(8,128)(2,1)S(1)} %copy-done.2, bf16[512,1024]{1,0:T(8,128)(2,1)S(1)} %copy-done, bf16[512,1024]{1,0:T(8,128)(2,1)S(1)} %collective-permute-done.1.refs_1_.refs_16_), custom_call_target="tpu_custom_call" | custom-call | tf_op jit(solution)/shard_map/stats0/pallas_call | solution.py:53
  18.6 3.9 %collective-permute-done.refs_0_.refs_16_ = bf16[512,1024]{1,0:T(8,128)(2,1)S(1)} collective-permute-done((bf16[512,1024]{1,0:T(8,128)(2,1)}, bf16[512,1024]{1,0:T(8,128)(2,1)S(1)}, u32[]{:S(2)}, u32[]{:S(2)}) %collective-permute-start) | collective-permute-done | bytes 1048608 | tf_op jit(solution)/shard_map/ppermute | solution.py:36
  22.6 6.4 %collective-permute-start.5 = (bf16[512,1024]{1,0:T(8,128)(2,1)S(1)}, bf16[512,1024]{1,0:T(8,128)(2,1)S(1)}, u32[]{:S(2)}, u32[]{:S(2)}) collective-permute-start(bf16[512,1024]{1,0:T(8,128)(2,1)S(1)} %collective-permute-done.refs_0_.refs_16_), channel_id=1, source_target_pairs={{0,1},{1,0},{2,3},{3,2},{4,5},{5,4},{6,7},{7,6},{8,9},{9,8},{10,11... | collective-permute-start | bytes 3145736 | tf_op jit(solution)/shard_map/ppermute | solution.py:41
  29.0 4.8 %collective-permute-done.3.refs_0_.refs_18_ = bf16[512,1024]{1,0:T(8,128)(2,1)S(1)} collective-permute-done((bf16[512,1024]{1,0:T(8,128)(2,1)S(1)}, bf16[512,1024]{1,0:T(8,128)(2,1)S(1)}, u32[]{:S(2)}, u32[]{:S(2)}) %collective-permute-start.3) | collective-permute-done | bytes 1048608 | tf_op jit(solution)/shard_map/ppermute | solution.py:36
  33.9 11.1 %collective-permute-done.4.refs_0_.refs_24_ = bf16[512,1024]{1,0:T(8,128)(2,1)S(1)} collective-permute-done((bf16[512,1024]{1,0:T(8,128)(2,1)S(1)}, bf16[512,1024]{1,0:T(8,128)(2,1)S(1)}, u32[]{:S(2)}, u32[]{:S(2)}) %collective-permute-start.4) | collective-permute-done | bytes 1048608 | tf_op jit(solution)/shard_map/ppermute | solution.py:36
  45.0 2.7 %stats1.1 = (f32[2,512,512]{2,1,0:T(8,128)S(1)}, f32[2,8,512]{2,1,0:T(8,128)S(1)}) custom-call(s32[9]{0:T(128)S(1)} %or_convert_fusion.flags.refs_0_, s32[1,512]{1,0:T(1,128)S(1)} %copy-done.4, bf16[512,1024]{1,0:T(8,128)(2,1)S(1)} %copy-done.3, bf16[512,1024]{1,0:T(8,128)(2,1)S(1)} %collective-permute-done.refs_0_.refs_16_, ...), custom_call_target="tpu_custom_call" | custom-call | tf_op jit(solution)/shard_map/stats1/pallas_call | solution.py:53
  47.8 2.7 %stats2.1 = (f32[2,512,512]{2,1,0:T(8,128)S(1)}, f32[2,8,512]{2,1,0:T(8,128)S(1)}) custom-call(s32[9]{0:T(128)S(1)} %or_convert_fusion.flags.refs_0_, s32[1,512]{1,0:T(1,128)S(1)} %copy-done.4, bf16[512,1024]{1,0:T(8,128)(2,1)S(1)} %copy-done.3, bf16[512,1024]{1,0:T(8,128)(2,1)S(1)} %collective-permute-done.3.refs_0_.refs_18_, ...), custom_call_target="tpu_custom_call" | custom-call | tf_op jit(solution)/shard_map/stats2/pallas_call | solution.py:53
  50.4 5.8 %collective-permute-done.7.refs_1_.refs_22_ = bf16[512,1024]{1,0:T(8,128)(2,1)S(1)} collective-permute-done((bf16[512,1024]{1,0:T(8,128)(2,1)S(1)}, bf16[512,1024]{1,0:T(8,128)(2,1)S(1)}, u32[]{:S(2)}, u32[]{:S(2)}) %collective-permute-start.7) | collective-permute-done | bytes 1048608 | tf_op jit(solution)/shard_map/ppermute | solution.py:36
  57.4 2.7 %stats3.1 = (f32[2,512,512]{2,1,0:T(8,128)S(1)}, f32[2,8,512]{2,1,0:T(8,128)S(1)}) custom-call(s32[9]{0:T(128)S(1)} %or_convert_fusion.flags.refs_0_, s32[1,512]{1,0:T(1,128)S(1)} %copy-done.4, bf16[512,1024]{1,0:T(8,128)(2,1)S(1)} %copy-done.3, bf16[512,1024]{1,0:T(8,128)(2,1)S(1)} %collective-permute-done.4.refs_0_.refs_24_, ...), custom_call_target="tpu_custom_call" | custom-call | tf_op jit(solution)/shard_map/stats3/pallas_call | solution.py:53
  60.1 1.8 %stats4.1 = (f32[1,512,512]{2,1,0:T(8,128)S(1)}, f32[1,8,512]{2,1,0:T(8,128)S(1)}) custom-call(s32[9]{0:T(128)S(1)} %or_convert_fusion.flags.refs_0_, s32[1,512]{1,0:T(1,128)S(1)} %copy-done.4, bf16[512,1024]{1,0:T(8,128)(2,1)S(1)} %copy-done.3, bf16[512,1024]{1,0:T(8,128)(2,1)S(1)} %collective-permute-done.8.refs_0_.refs_20_), custom_call_target="tpu_custom_call" | custom-call | tf_op jit(solution)/shard_map/stats4/pallas_call | solution.py:53
  64.4 6.1 %collective-permute-start.13 = (f32[6,8,512]{2,1,0:T(8,128)S(1)}, f32[6,8,512]{2,1,0:T(8,128)S(1)}, u32[]{:S(2)}, u32[]{:S(2)}) collective-permute-start(f32[6,8,512]{2,1,0:T(8,128)S(1)} %near.1.refs_4_), channel_id=1, source_target_pairs={{0,126},{1,3},{2,0},{3,5},{4,2},{5,7},{6,4},{7,9},{8,6},{9,11},{10... | collective-permute-start | bytes 294920 | tf_op jit(solution)/shard_map/ppermute | solution.py:36
  70.5 3.2 %collective-permute-done.13.one.refs_5_ = f32[6,8,512]{2,1,0:T(8,128)S(1)} collective-permute-done((f32[6,8,512]{2,1,0:T(8,128)S(1)}, f32[6,8,512]{2,1,0:T(8,128)S(1)}, u32[]{:S(2)}, u32[]{:S(2)}) %collective-permute-start.13) | collective-permute-done | bytes 98336 | tf_op jit(solution)/shard_map/ppermute | solution.py:36
  73.8 2.1 %collective-permute-start.14 = (f32[6,8,512]{2,1,0:T(8,128)S(1)}, f32[6,8,512]{2,1,0:T(8,128)S(1)}, u32[]{:S(2)}, u32[]{:S(2)}) collective-permute-start(f32[6,8,512]{2,1,0:T(8,128)S(1)} %collective-permute-done.13.one.refs_5_), channel_id=1, source_target_pairs={{0,1},{1,0},{2,3},{3,2},{4,5},{5,4},{6,7},{7,6},{8,9},{9,8},{10,11... | collective-permute-start | bytes 294920 | tf_op jit(solution)/shard_map/ppermute | solution.py:41
  77.2 5.2 %collective-permute-done.15.refs_18_ = bf16[2,512,1024]{2,1,0:T(8,128)(2,1)S(1)} collective-permute-done((bf16[2,512,1024]{2,1,0:T(8,128)(2,1)S(1)}, bf16[2,512,1024]{2,1,0:T(8,128)(2,1)S(1)}, u32[]{:S(2)}, u32[]{:S(2)}) %collective-permute-start.15) | collective-permute-done | bytes 2097184 | tf_op jit(solution)/shard_map/ppermute | solution.py:36
  82.5 6.0 %collective-permute-start.18 = (f32[6,8,512]{2,1,0:T(8,128)S(1)}, f32[6,8,512]{2,1,0:T(8,128)S(1)}, u32[]{:S(2)}, u32[]{:S(2)}) collective-permute-start(f32[6,8,512]{2,1,0:T(8,128)S(1)} %collective-permute-done.16.two.refs_7_), channel_id=1, source_target_pairs={{0,1},{1,0},{2,3},{3,2},{4,5},{5,4},{6,7},{7,6},{8,9},{9,8},{10,11... | collective-permute-start | bytes 294920 | tf_op jit(solution)/shard_map/ppermute | solution.py:41
  91.2 3.2 %collective-permute-start.20 = (f32[2,8,512]{2,1,0:T(8,128)S(1)}, f32[2,8,512]{2,1,0:T(8,128)S(1)}, u32[]{:S(2)}, u32[]{:S(2)}) collective-permute-start(f32[2,8,512]{2,1,0:T(8,128)S(1)} %pair.3.refs_9_.refs_10_.refs_11_.refs_12_.refs_13_), channel_id=1, source_target_pairs={{0,126},{1,3},{2,0},{3,5},{4,2},{5,7},{6,4},{7,9},{8,6},{9,11},{10... | collective-permute-start | bytes 98312 | tf_op jit(solution)/shard_map/ppermute | solution.py:36
  94.4 6.0 %part0.1 = (f32[512,1024]{1,0:T(8,128)S(1)}, f32[512,1024]{1,0:T(8,128)S(1)}) custom-call(s32[9]{0:T(128)S(1)} %or_convert_fusion.flags.refs_0_, s32[1,512]{1,0:T(1,128)S(1)} %copy-done.5, f32[8,512]{1,0:T(8,128)S(1)} %get-tuple-element.181.pay.refs_2_, f32[8,512]{1,0:T(8,128)S(1)} %get-tuple-element.182.mine.refs_3_, f32[6,8,512]{2,1,0:T(8,128)S(1)} %near.1.refs_4_, ...), custom_call_target="tpu_custom_call" | custom-call | tf_op jit(solution)/shard_map/part0/pallas_call | solution.py:258
  100.5 4.3 %collective-permute-start.23 = (f32[2,8,512]{2,1,0:T(8,128)S(1)}, f32[2,8,512]{2,1,0:T(8,128)S(1)}, u32[]{:S(2)}, u32[]{:S(2)}) collective-permute-start(f32[2,8,512]{2,1,0:T(8,128)S(1)} %collective-permute-done.20.refs_10_), channel_id=1, source_target_pairs={{0,126},{1,3},{2,0},{3,5},{4,2},{5,7},{6,4},{7,9},{8,6},{9,11},{10... | collective-permute-start | bytes 98312 | tf_op jit(solution)/shard_map/ppermute | solution.py:36
  104.8 4.7 %part1.1 = (f32[512,1024]{1,0:T(8,128)S(1)}, f32[512,1024]{1,0:T(8,128)S(1)}) custom-call(s32[9]{0:T(128)S(1)} %or_convert_fusion.flags.refs_0_, s32[1,512]{1,0:T(1,128)S(1)} %copy-done.5, f32[8,512]{1,0:T(8,128)S(1)} %get-tuple-element.181.pay.refs_2_, f32[8,512]{1,0:T(8,128)S(1)} %get-tuple-element.182.mine.refs_3_, f32[6,8,512]{2,1,0:T(8,128)S(1)} %near.1.refs_4_, ...), custom_call_target="tpu_custom_call" | custom-call | tf_op jit(solution)/shard_map/part1/pallas_call | solution.py:258
  109.9 4.7 %collective-permute-done.25.refs_14_ = bf16[2,512,1024]{2,1,0:T(8,128)(2,1)S(1)} collective-permute-done((bf16[2,512,1024]{2,1,0:T(8,128)(2,1)S(1)}, bf16[2,512,1024]{2,1,0:T(8,128)(2,1)S(1)}, u32[]{:S(2)}, u32[]{:S(2)}) %collective-permute-start.25) | collective-permute-done | bytes 2097184 | tf_op jit(solution)/shard_map/ppermute | solution.py:36
  114.6 7.2 %part2.1 = (f32[512,1024]{1,0:T(8,128)S(1)}, f32[512,1024]{1,0:T(8,128)}) custom-call(s32[9]{0:T(128)S(1)} %or_convert_fusion.flags.refs_0_, s32[1,512]{1,0:T(1,128)S(1)} %copy-done.5, f32[8,512]{1,0:T(8,128)S(1)} %get-tuple-element.181.pay.refs_2_, f32[8,512]{1,0:T(8,128)S(1)} %get-tuple-element.182.mine.refs_3_, f32[6,8,512]{2,1,0:T(8,128)S(1)} %near.1.refs_4_, ...), custom_call_target="tpu_custom_call" | custom-call | tf_op jit(solution)/shard_map/part2/pallas_call | solution.py:258
  121.8 3.1 %part3.1 = f32[512,1024]{1,0:T(8,128)} custom-call(s32[9]{0:T(128)S(1)} %or_convert_fusion.flags.refs_0_, s32[1,512]{1,0:T(1,128)S(1)} %copy-done.5, f32[8,512]{1,0:T(8,128)S(1)} %get-tuple-element.181.pay.refs_2_, f32[8,512]{1,0:T(8,128)S(1)} %get-tuple-element.182.mine.refs_3_, f32[6,8,512]{2,1,0:T(8,128)S(1)} %near.1.refs_4_, ...), custom_call_target="tpu_custom_call" | custom-call | tf_op jit(solution)/shard_map/part3/pallas_call | solution.py:258
  (61 shorter events, 13.9 us)
Async XLA Ops:
  0.6 11.2 %collective-permute-start.1 = (bf16[512,1024]{1,0:T(8,128)(2,1)}, bf16[512,1024]{1,0:T(8,128)(2,1)S(1)}, u32[]{:S(2)}, u32[]{:S(2)}) collective-permute-start(bf16[512,1024]{1,0:T(8,128)(2,1)} %refs_15_.1), channel_id=1, source_target_pairs={{0,1},{1,0},{2,3},{3,2},{4,5},{5,4},{6,7},{7,6},{8,9},{9,8},{10,11... | collective-permute-start | bytes 3145736 | tf_op jit(solution)/shard_map/ppermute | solution.py:41
  0.7 21.8 %collective-permute-start = (bf16[512,1024]{1,0:T(8,128)(2,1)}, bf16[512,1024]{1,0:T(8,128)(2,1)S(1)}, u32[]{:S(2)}, u32[]{:S(2)}) collective-permute-start(bf16[512,1024]{1,0:T(8,128)(2,1)} %refs_15_.1), channel_id=1, source_target_pairs={{0,2},{1,127},{2,4},{3,1},{4,6},{5,3},{6,8},{7,5},{8,10},{9,7},{10... | collective-permute-start | bytes 3145736 | tf_op jit(solution)/shard_map/ppermute | solution.py:36
  2.8 19.8 %collective-permute-start.2 = (bf16[512,1024]{1,0:T(8,128)(2,1)}, bf16[512,1024]{1,0:T(8,128)(2,1)S(1)}, u32[]{:S(2)}, u32[]{:S(2)}) collective-permute-start(bf16[512,1024]{1,0:T(8,128)(2,1)} %queries.5), channel_id=1, source_target_pairs={{0,1},{1,0},{2,3},{3,2},{4,5},{5,4},{6,7},{7,6},{8,9},{9,8},{10,11... | collective-permute-start | bytes 3145736 | tf_op jit(solution)/shard_map/ppermute | solution.py:41
  11.8 22.0 %collective-permute-start.3 = (bf16[512,1024]{1,0:T(8,128)(2,1)S(1)}, bf16[512,1024]{1,0:T(8,128)(2,1)S(1)}, u32[]{:S(2)}, u32[]{:S(2)}) collective-permute-start(bf16[512,1024]{1,0:T(8,128)(2,1)S(1)} %collective-permute-done.1.refs_1_.refs_16_), channel_id=1, source_target_pairs={{0,2},{1,127},{2,4},{3,1},{4,6},{5,3},{6,8},{7,5},{8,10},{9,7},{10... | collective-permute-start | bytes 3145736 | tf_op jit(solution)/shard_map/ppermute | solution.py:36
  22.6 22.5 %collective-permute-start.4 = (bf16[512,1024]{1,0:T(8,128)(2,1)S(1)}, bf16[512,1024]{1,0:T(8,128)(2,1)S(1)}, u32[]{:S(2)}, u32[]{:S(2)}) collective-permute-start(bf16[512,1024]{1,0:T(8,128)(2,1)S(1)} %collective-permute-done.refs_0_.refs_16_), channel_id=1, source_target_pairs={{0,2},{1,127},{2,4},{3,1},{4,6},{5,3},{6,8},{7,5},{8,10},{9,7},{10... | collective-permute-start | bytes 3145736 | tf_op jit(solution)/shard_map/ppermute | solution.py:36
  22.6 22.5 %collective-permute-start.5 = (bf16[512,1024]{1,0:T(8,128)(2,1)S(1)}, bf16[512,1024]{1,0:T(8,128)(2,1)S(1)}, u32[]{:S(2)}, u32[]{:S(2)}) collective-permute-start(bf16[512,1024]{1,0:T(8,128)(2,1)S(1)} %collective-permute-done.refs_0_.refs_16_), channel_id=1, source_target_pairs={{0,1},{1,0},{2,3},{3,2},{4,5},{5,4},{6,7},{7,6},{8,9},{9,8},{10,11... | collective-permute-start | bytes 3145736 | tf_op jit(solution)/shard_map/ppermute | solution.py:41
  33.8 14.0 %collective-permute-start.6 = (bf16[512,1024]{1,0:T(8,128)(2,1)S(1)}, bf16[512,1024]{1,0:T(8,128)(2,1)S(1)}, u32[]{:S(2)}, u32[]{:S(2)}) collective-permute-start(bf16[512,1024]{1,0:T(8,128)(2,1)S(1)} %collective-permute-done.3.refs_0_.refs_18_), channel_id=1, source_target_pairs={{0,1},{1,0},{2,3},{3,2},{4,5},{5,4},{6,7},{7,6},{8,9},{9,8},{10,11... | collective-permute-start | bytes 3145736 | tf_op jit(solution)/shard_map/ppermute | solution.py:41
  33.8 22.5 %collective-permute-start.7 = (bf16[512,1024]{1,0:T(8,128)(2,1)S(1)}, bf16[512,1024]{1,0:T(8,128)(2,1)S(1)}, u32[]{:S(2)}, u32[]{:S(2)}) collective-permute-start(bf16[512,1024]{1,0:T(8,128)(2,1)S(1)} %collective-permute-done.3.refs_0_.refs_18_), channel_id=1, source_target_pairs={{0,2},{1,127},{2,4},{3,1},{4,6},{5,3},{6,8},{7,5},{8,10},{9,7},{10... | collective-permute-start | bytes 3145736 | tf_op jit(solution)/shard_map/ppermute | solution.py:36
  47.7 34.7 %collective-permute-start.15 = (bf16[2,512,1024]{2,1,0:T(8,128)(2,1)S(1)}, bf16[2,512,1024]{2,1,0:T(8,128)(2,1)S(1)}, u32[]{:S(2)}, u32[]{:S(2)}) collective-permute-start(bf16[2,512,1024]{2,1,0:T(8,128)(2,1)S(1)} %pair.2.queries.refs_17_), channel_id=1, source_target_pairs={{0,2},{1,127},{2,4},{3,1},{4,6},{5,3},{6,8},{7,5},{8,10},{9,7},{10... | collective-permute-start | bytes 6291464 | tf_op jit(solution)/shard_map/ppermute | solution.py:36
  56.3 3.8 %collective-permute-start.8 = (bf16[512,1024]{1,0:T(8,128)(2,1)S(1)}, bf16[512,1024]{1,0:T(8,128)(2,1)S(1)}, u32[]{:S(2)}, u32[]{:S(2)}) collective-permute-start(bf16[512,1024]{1,0:T(8,128)(2,1)S(1)} %collective-permute-done.7.refs_1_.refs_22_), channel_id=1, source_target_pairs={{0,1},{1,0},{2,3},{3,2},{4,5},{5,4},{6,7},{7,6},{8,9},{9,8},{10,11... | collective-permute-start | bytes 3145736 | tf_op jit(solution)/shard_map/ppermute | solution.py:41
  56.9 6.6 %collective-permute-start.10 = (f32[2,8,512]{2,1,0:T(8,128)S(1)}, f32[2,8,512]{2,1,0:T(8,128)S(1)}, u32[]{:S(2)}, u32[]{:S(2)}) collective-permute-start(f32[2,8,512]{2,1,0:T(8,128)S(1)} %get-tuple-element.151.refs_2_.st2), channel_id=1, source_target_pairs={{0,1},{1,0},{2,3},{3,2},{4,5},{5,4},{6,7},{7,6},{8,9},{9,8},{10,11... | collective-permute-start | bytes 98312 | tf_op jit(solution)/shard_map/ppermute | solution.py:41
  57.0 6.5 %collective-permute-start.9 = (f32[2,8,512]{2,1,0:T(8,128)S(1)}, f32[2,8,512]{2,1,0:T(8,128)S(1)}, u32[]{:S(2)}, u32[]{:S(2)}) collective-permute-start(f32[2,8,512]{2,1,0:T(8,128)S(1)} %get-tuple-element.150.refs_1_.st1), channel_id=1, source_target_pairs={{0,1},{1,0},{2,3},{3,2},{4,5},{5,4},{6,7},{7,6},{8,9},{9,8},{10,11... | collective-permute-start | bytes 98312 | tf_op jit(solution)/shard_map/ppermute | solution.py:41
  64.4 9.4 %collective-permute-start.13 = (f32[6,8,512]{2,1,0:T(8,128)S(1)}, f32[6,8,512]{2,1,0:T(8,128)S(1)}, u32[]{:S(2)}, u32[]{:S(2)}) collective-permute-start(f32[6,8,512]{2,1,0:T(8,128)S(1)} %near.1.refs_4_), channel_id=1, source_target_pairs={{0,126},{1,3},{2,0},{3,5},{4,2},{5,7},{6,4},{7,9},{8,6},{9,11},{10... | collective-permute-start | bytes 294920 | tf_op jit(solution)/shard_map/ppermute | solution.py:36
  70.5 11.8 %collective-permute-start.16 = (f32[6,8,512]{2,1,0:T(8,128)S(1)}, f32[6,8,512]{2,1,0:T(8,128)S(1)}, u32[]{:S(2)}, u32[]{:S(2)}) collective-permute-start(f32[6,8,512]{2,1,0:T(8,128)S(1)} %near.1.refs_4_), channel_id=1, source_target_pairs={{0,124},{1,5},{2,126},{3,7},{4,0},{5,9},{6,2},{7,11},{8,4},{9,13},... | collective-permute-start | bytes 294920 | tf_op jit(solution)/shard_map/ppermute | solution.py:36
  73.8 8.6 %collective-permute-start.14 = (f32[6,8,512]{2,1,0:T(8,128)S(1)}, f32[6,8,512]{2,1,0:T(8,128)S(1)}, u32[]{:S(2)}, u32[]{:S(2)}) collective-permute-start(f32[6,8,512]{2,1,0:T(8,128)S(1)} %collective-permute-done.13.one.refs_5_), channel_id=1, source_target_pairs={{0,1},{1,0},{2,3},{3,2},{4,5},{5,4},{6,7},{7,6},{8,9},{9,8},{10,11... | collective-permute-start | bytes 294920 | tf_op jit(solution)/shard_map/ppermute | solution.py:41
  75.9 1.3 %collective-permute-start.17 = (f32[2,8,512]{2,1,0:T(8,128)S(1)}, f32[2,8,512]{2,1,0:T(8,128)S(1)}, u32[]{:S(2)}, u32[]{:S(2)}) collective-permute-start(f32[2,8,512]{2,1,0:T(8,128)S(1)} %get-tuple-element.173.refs_0_.st0), channel_id=1, source_target_pairs={{0,1},{1,0},{2,3},{3,2},{4,5},{5,4},{6,7},{7,6},{8,9},{9,8},{10,11... | collective-permute-start | bytes 98312 | tf_op jit(solution)/shard_map/ppermute | solution.py:41
  82.4 12.0 %collective-permute-start.21 = (bf16[2,512,1024]{2,1,0:T(8,128)(2,1)S(1)}, bf16[2,512,1024]{2,1,0:T(8,128)(2,1)S(1)}, u32[]{:S(2)}, u32[]{:S(2)}) collective-permute-start(bf16[2,512,1024]{2,1,0:T(8,128)(2,1)S(1)} %collective-permute-done.15.refs_18_), channel_id=1, source_target_pairs={{0,1},{1,0},{2,3},{3,2},{4,5},{5,4},{6,7},{7,6},{8,9},{9,8},{10,11... | collective-permute-start | bytes 6291464 | tf_op jit(solution)/shard_map/ppermute | solution.py:41
  82.4 32.2 %collective-permute-start.25 = (bf16[2,512,1024]{2,1,0:T(8,128)(2,1)S(1)}, bf16[2,512,1024]{2,1,0:T(8,128)(2,1)S(1)}, u32[]{:S(2)}, u32[]{:S(2)}) collective-permute-start(bf16[2,512,1024]{2,1,0:T(8,128)(2,1)S(1)} %collective-permute-done.15.refs_18_), channel_id=1, source_target_pairs={{0,2},{1,127},{2,4},{3,1},{4,6},{5,3},{6,8},{7,5},{8,10},{9,7},{10... | collective-permute-start | bytes 6291464 | tf_op jit(solution)/shard_map/ppermute | solution.py:36
  82.5 6.9 %collective-permute-start.18 = (f32[6,8,512]{2,1,0:T(8,128)S(1)}, f32[6,8,512]{2,1,0:T(8,128)S(1)}, u32[]{:S(2)}, u32[]{:S(2)}) collective-permute-start(f32[6,8,512]{2,1,0:T(8,128)S(1)} %collective-permute-done.16.two.refs_7_), channel_id=1, source_target_pairs={{0,1},{1,0},{2,3},{3,2},{4,5},{5,4},{6,7},{7,6},{8,9},{9,8},{10,11... | collective-permute-start | bytes 294920 | tf_op jit(solution)/shard_map/ppermute | solution.py:41
  91.2 9.2 %collective-permute-start.20 = (f32[2,8,512]{2,1,0:T(8,128)S(1)}, f32[2,8,512]{2,1,0:T(8,128)S(1)}, u32[]{:S(2)}, u32[]{:S(2)}) collective-permute-start(f32[2,8,512]{2,1,0:T(8,128)S(1)} %pair.3.refs_9_.refs_10_.refs_11_.refs_12_.refs_13_), channel_id=1, source_target_pairs={{0,126},{1,3},{2,0},{3,5},{4,2},{5,7},{6,4},{7,9},{8,6},{9,11},{10... | collective-permute-start | bytes 98312 | tf_op jit(solution)/shard_map/ppermute | solution.py:36
  100.4 9.1 %collective-permute-start.22 = (f32[2,8,512]{2,1,0:T(8,128)S(1)}, f32[2,8,512]{2,1,0:T(8,128)S(1)}, u32[]{:S(2)}, u32[]{:S(2)}) collective-permute-start(f32[2,8,512]{2,1,0:T(8,128)S(1)} %collective-permute-done.20.refs_10_), channel_id=1, source_target_pairs={{0,1},{1,0},{2,3},{3,2},{4,5},{5,4},{6,7},{7,6},{8,9},{9,8},{10,11... | collective-permute-start | bytes 98312 | tf_op jit(solution)/shard_map/ppermute | solution.py:41
  100.5 9.0 %collective-permute-start.23 = (f32[2,8,512]{2,1,0:T(8,128)S(1)}, f32[2,8,512]{2,1,0:T(8,128)S(1)}, u32[]{:S(2)}, u32[]{:S(2)}) collective-permute-start(f32[2,8,512]{2,1,0:T(8,128)S(1)} %collective-permute-done.20.refs_10_), channel_id=1, source_target_pairs={{0,126},{1,3},{2,0},{3,5},{4,2},{5,7},{6,4},{7,9},{8,6},{9,11},{10... | collective-permute-start | bytes 98312 | tf_op jit(solution)/shard_map/ppermute | solution.py:36
  109.5 5.1 %collective-permute-start.24 = (f32[2,8,512]{2,1,0:T(8,128)S(1)}, f32[2,8,512]{2,1,0:T(8,128)S(1)}, u32[]{:S(2)}, u32[]{:S(2)}) collective-permute-start(f32[2,8,512]{2,1,0:T(8,128)S(1)} %collective-permute-done.23.refs_12_), channel_id=1, source_target_pairs={{0,1},{1,0},{2,3},{3,2},{4,5},{5,4},{6,7},{7,6},{8,9},{9,8},{10,11... | collective-permute-start | bytes 98312 | tf_op jit(solution)/shard_map/ppermute | solution.py:41
  114.6 7.2 %collective-permute-start.26 = (bf16[2,512,1024]{2,1,0:T(8,128)(2,1)S(1)}, bf16[2,512,1024]{2,1,0:T(8,128)(2,1)S(1)}, u32[]{:S(2)}, u32[]{:S(2)}) collective-permute-start(bf16[2,512,1024]{2,1,0:T(8,128)(2,1)S(1)} %collective-permute-done.25.refs_14_), channel_id=1, source_target_pairs={{0,1},{1,0},{2,3},{3,2},{4,5},{5,4},{6,7},{7,6},{8,9},{9,8},{10,11... | collective-permute-start | bytes 6291464 | tf_op jit(solution)/shard_map/ppermute | solution.py:41
  (9 other events, 74.5 us)

commit v4 on v3

--- a/solution.py
+++ b/solution.py
@@ -323,9 +323,9 @@
     v["one_peer"] = swap(v["one"])
     v["x0"], v["near"], v["q_pay"] = x0, near, q_pay
     v["t0"] = tscores_of(v["p_own"], v["q0"])
-    v["q1"] = q1
-    fence()
-    v["q3"] = split(v["q1"], 1, -1)
+    q3 = split(after(q1, v["one"]), 1, -1)
+    fence()
+    v["q1"], v["q3"] = after(q1, v["two"]), q3
     v["q2"] = swap(v["q1"])
     two_peer = swap(v["two"])
     p_pay, passage_loss = call(
@@ -353,12 +353,12 @@
 
     hold = lax.optimization_barrier
     m1 = split(m0, -1, 1)
-    steps = steps_of("q", "own", "s0") + steps_of("p", "own", "s0", "sa", "b")
+    steps = steps_of("q", "own", "s0") + steps_of("p", "own", "s0", "a", "sb")
     p_total, q_total = parts("part0", common, [m0] * 5, steps, dict(p=None, q=None))
     m1, q_total, p_total = hold((m1, q_total, p_total))
     m3 = split(m1, -1, 1)
     m2 = swap(m1)
-    steps = steps_of("q", "sa", "b") + steps_of("p", "a", "sb")
+    steps = steps_of("q", "sa", "b") + steps_of("p", "sa", "b")
     p_total, q_total = parts("part1", common, [m0, m1, m0, m0, m0], steps, dict(p=p_total, q=q_total))
     m2, m3, q_total, p_total = hold((m2, m3, q_total, p_total))
     m4 = swap(m3)

time: 127 us -> 127 us (level)
  waiting for transfers between devices: 41.4 us -> 53.8 us
  starting transfers between devices: 39.9 us -> 27.9 us
    ppermute x17, starting transfers between devices: 24 us -> 10.7 us  [swap(): return lax.ppermute(value, AXES, [(i, i ^ 1) for i in range(n)])]
    ppermute x10, waiting for transfers between devices: 38.8 us -> 51.2 us  [split(): return lax.ppermute(value, AXES, pairs)]
    ppermute x10, starting transfers between devices: 15.9 us -> 17.2 us  [split(): return lax.ppermute(value, AXES, pairs)]
where the time goes in v4:
time: 127 us; the launch traced here: 126 us
  waiting for transfers between devices  53.8 us (42%)
  Pallas kernels  36.9 us (29%)
  starting transfers between devices  27.9 us (22%)
  local copies, waits for them, and re-layouts  3.14 us (2%)
  other arithmetic  2.08 us (2%)
  between operations  1.63 us (1%)
    ppermute x10, waiting for transfers between devices, split(): return lax.ppermute(value, AXES, pairs)  51.2 us
    pallas_call x4, Pallas kernels, parts(): pl.pallas_call(functools.partial(parts_kernel, plan, begin, last, len(arr...  21.1 us
    ppermute x10, starting transfers between devices, split(): return lax.ppermute(value, AXES, pairs)  17.2 us
    pallas_call x11, Pallas kernels, call(): pl.pallas_call(kernel, in_specs=[first] + [VMEM] * (len(operands) - 1), o...  15.9 us
    ppermute x17, starting transfers between devices, swap(): return lax.ppermute(value, AXES, [(i, i ^ 1) for i in range(n)])  10.7 us
    unnamed x12, local copies, waits for them, and re-layouts  3.14 us
    ppermute x17, waiting for transfers between devices, swap(): return lax.ppermute(value, AXES, [(i, i ^ 1) for i in range(n)])  2.65 us
  transfers between devices with their start and end apart: 27, of which 11 were waited for; matrix products, arithmetic and copies ran while one was open for 2% of the time, Pallas kernels for 27%

profile of v4, /device:TPU:0, one launch (start us, length us, event | category | flops | bytes accessed | tf_op | source)
XLA Modules:
  0.0 125.5 jit_solution(16690208701897521272)
XLA Ops:
  1.2 2.0 %collective-permute-start = (bf16[512,1024]{1,0:T(8,128)(2,1)}, bf16[512,1024]{1,0:T(8,128)(2,1)S(1)}, u32[]{:S(2)}, u32[]{:S(2)}) collective-permute-start(bf16[512,1024]{1,0:T(8,128)(2,1)} %refs_15_.1), channel_id=1, source_target_pairs={{0,2},{1,127},{2,4},{3,1},{4,6},{5,3},{6,8},{7,5},{8,10},{9,7},{10... | collective-permute-start | bytes 3145736 | tf_op jit(solution)/shard_map/ppermute | solution.py:36
  5.3 2.0 %collective-permute-start.3 = (bf16[512,1024]{1,0:T(8,128)(2,1)S(1)}, bf16[512,1024]{1,0:T(8,128)(2,1)S(1)}, u32[]{:S(2)}, u32[]{:S(2)}) collective-permute-start(bf16[512,1024]{1,0:T(8,128)(2,1)S(1)} %collective-permute-done.1.refs_1_.refs_16_), channel_id=1, source_target_pairs={{0,2},{1,127},{2,4},{3,1},{4,6},{5,3},{6,8},{7,5},{8,10},{9,7},{10... | collective-permute-start | bytes 3145736 | tf_op jit(solution)/shard_map/ppermute | solution.py:36
  11.1 2.9 %stats0.1 = (f32[2,512,512]{2,1,0:T(8,128)S(1)}, f32[2,8,512]{2,1,0:T(8,128)S(1)}) custom-call(s32[9]{0:T(128)S(1)} %or_convert_fusion.flags.refs_0_, s32[1,512]{1,0:T(1,128)S(1)} %copy-done.4, bf16[512,1024]{1,0:T(8,128)(2,1)S(1)} %copy-done.2, bf16[512,1024]{1,0:T(8,128)(2,1)S(1)} %copy-done, bf16[512,1024]{1,0:T(8,128)(2,1)S(1)} %collective-permute-done.1.refs_1_.refs_16_), custom_call_target="tpu_custom_call" | custom-call | tf_op jit(solution)/shard_map/stats0/pallas_call | solution.py:53
  14.0 9.0 %collective-permute-done.refs_0_.refs_16_ = bf16[512,1024]{1,0:T(8,128)(2,1)S(1)} collective-permute-done((bf16[512,1024]{1,0:T(8,128)(2,1)}, bf16[512,1024]{1,0:T(8,128)(2,1)S(1)}, u32[]{:S(2)}, u32[]{:S(2)}) %collective-permute-start) | collective-permute-done | bytes 1048608 | tf_op jit(solution)/shard_map/ppermute | solution.py:36
  23.0 11.2 %collective-permute-done.3.refs_0_.refs_18_ = bf16[512,1024]{1,0:T(8,128)(2,1)S(1)} collective-permute-done((bf16[512,1024]{1,0:T(8,128)(2,1)S(1)}, bf16[512,1024]{1,0:T(8,128)(2,1)S(1)}, u32[]{:S(2)}, u32[]{:S(2)}) %collective-permute-start.3) | collective-permute-done | bytes 1048608 | tf_op jit(solution)/shard_map/ppermute | solution.py:36
  34.4 11.1 %collective-permute-done.4.refs_0_.refs_24_ = bf16[512,1024]{1,0:T(8,128)(2,1)S(1)} collective-permute-done((bf16[512,1024]{1,0:T(8,128)(2,1)S(1)}, bf16[512,1024]{1,0:T(8,128)(2,1)S(1)}, u32[]{:S(2)}, u32[]{:S(2)}) %collective-permute-start.4) | collective-permute-done | bytes 1048608 | tf_op jit(solution)/shard_map/ppermute | solution.py:36
  45.4 2.7 %stats1.1 = (f32[2,512,512]{2,1,0:T(8,128)S(1)}, f32[2,8,512]{2,1,0:T(8,128)S(1)}) custom-call(s32[9]{0:T(128)S(1)} %or_convert_fusion.flags.refs_0_, s32[1,512]{1,0:T(1,128)S(1)} %copy-done.4, bf16[512,1024]{1,0:T(8,128)(2,1)S(1)} %copy-done.3, bf16[512,1024]{1,0:T(8,128)(2,1)S(1)} %collective-permute-done.refs_0_.refs_16_, ...), custom_call_target="tpu_custom_call" | custom-call | tf_op jit(solution)/shard_map/stats1/pallas_call | solution.py:53
  48.2 2.7 %stats2.1 = (f32[2,512,512]{2,1,0:T(8,128)S(1)}, f32[2,8,512]{2,1,0:T(8,128)S(1)}) custom-call(s32[9]{0:T(128)S(1)} %or_convert_fusion.flags.refs_0_, s32[1,512]{1,0:T(1,128)S(1)} %copy-done.4, bf16[512,1024]{1,0:T(8,128)(2,1)S(1)} %copy-done.3, bf16[512,1024]{1,0:T(8,128)(2,1)S(1)} %collective-permute-done.3.refs_0_.refs_18_, ...), custom_call_target="tpu_custom_call" | custom-call | tf_op jit(solution)/shard_map/stats2/pallas_call | solution.py:53
  50.8 5.9 %collective-permute-done.7.refs_1_.refs_22_ = bf16[512,1024]{1,0:T(8,128)(2,1)S(1)} collective-permute-done((bf16[512,1024]{1,0:T(8,128)(2,1)S(1)}, bf16[512,1024]{1,0:T(8,128)(2,1)S(1)}, u32[]{:S(2)}, u32[]{:S(2)}) %collective-permute-start.7) | collective-permute-done | bytes 1048608 | tf_op jit(solution)/shard_map/ppermute | solution.py:36
  57.5 2.7 %stats3.1 = (f32[2,512,512]{2,1,0:T(8,128)S(1)}, f32[2,8,512]{2,1,0:T(8,128)S(1)}) custom-call(s32[9]{0:T(128)S(1)} %or_convert_fusion.flags.refs_0_, s32[1,512]{1,0:T(1,128)S(1)} %copy-done.4, bf16[512,1024]{1,0:T(8,128)(2,1)S(1)} %copy-done.3, bf16[512,1024]{1,0:T(8,128)(2,1)S(1)} %collective-permute-done.4.refs_0_.refs_24_, ...), custom_call_target="tpu_custom_call" | custom-call | tf_op jit(solution)/shard_map/stats3/pallas_call | solution.py:53
  60.2 1.8 %stats4.1 = (f32[1,512,512]{2,1,0:T(8,128)S(1)}, f32[1,8,512]{2,1,0:T(8,128)S(1)}) custom-call(s32[9]{0:T(128)S(1)} %or_convert_fusion.flags.refs_0_, s32[1,512]{1,0:T(1,128)S(1)} %copy-done.4, bf16[512,1024]{1,0:T(8,128)(2,1)S(1)} %copy-done.3, bf16[512,1024]{1,0:T(8,128)(2,1)S(1)} %collective-permute-done.8.refs_0_.refs_20_), custom_call_target="tpu_custom_call" | custom-call | tf_op jit(solution)/shard_map/stats4/pallas_call | solution.py:53
  64.5 6.1 %collective-permute-start.13 = (f32[6,8,512]{2,1,0:T(8,128)S(1)}, f32[6,8,512]{2,1,0:T(8,128)S(1)}, u32[]{:S(2)}, u32[]{:S(2)}) collective-permute-start(f32[6,8,512]{2,1,0:T(8,128)S(1)} %near.1.refs_4_), channel_id=1, source_target_pairs={{0,126},{1,3},{2,0},{3,5},{4,2},{5,7},{6,4},{7,9},{8,6},{9,11},{10... | collective-permute-start | bytes 294920 | tf_op jit(solution)/shard_map/ppermute | solution.py:36
  70.7 3.2 %collective-permute-done.13.one.refs_5_ = f32[6,8,512]{2,1,0:T(8,128)S(1)} collective-permute-done((f32[6,8,512]{2,1,0:T(8,128)S(1)}, f32[6,8,512]{2,1,0:T(8,128)S(1)}, u32[]{:S(2)}, u32[]{:S(2)}) %collective-permute-start.13) | collective-permute-done | bytes 98336 | tf_op jit(solution)/shard_map/ppermute | solution.py:36
  73.9 2.1 %collective-permute-start.14 = (f32[6,8,512]{2,1,0:T(8,128)S(1)}, f32[6,8,512]{2,1,0:T(8,128)S(1)}, u32[]{:S(2)}, u32[]{:S(2)}) collective-permute-start(f32[6,8,512]{2,1,0:T(8,128)S(1)} %collective-permute-done.13.one.refs_5_), channel_id=1, source_target_pairs={{0,1},{1,0},{2,3},{3,2},{4,5},{5,4},{6,7},{7,6},{8,9},{9,8},{10,11... | collective-permute-start | bytes 294920 | tf_op jit(solution)/shard_map/ppermute | solution.py:41
  77.3 2.9 %collective-permute-done.15.two.refs_7_ = f32[6,8,512]{2,1,0:T(8,128)S(1)} collective-permute-done((f32[6,8,512]{2,1,0:T(8,128)S(1)}, f32[6,8,512]{2,1,0:T(8,128)S(1)}, u32[]{:S(2)}, u32[]{:S(2)}) %collective-permute-start.15) | collective-permute-done | bytes 98336 | tf_op jit(solution)/shard_map/ppermute | solution.py:36
  80.2 2.6 %collective-permute-done.20.refs_19_ = bf16[2,512,1024]{2,1,0:T(8,128)(2,1)S(1)} collective-permute-done((bf16[2,512,1024]{2,1,0:T(8,128)(2,1)S(1)}, bf16[2,512,1024]{2,1,0:T(8,128)(2,1)S(1)}, u32[]{:S(2)}, u32[]{:S(2)}) %collective-permute-start.20) | collective-permute-done | bytes 2097184 | tf_op jit(solution)/shard_map/ppermute | solution.py:36
  82.8 5.7 %collective-permute-start.17 = (f32[6,8,512]{2,1,0:T(8,128)S(1)}, f32[6,8,512]{2,1,0:T(8,128)S(1)}, u32[]{:S(2)}, u32[]{:S(2)}) collective-permute-start(f32[6,8,512]{2,1,0:T(8,128)S(1)} %collective-permute-done.15.two.refs_7_), channel_id=1, source_target_pairs={{0,1},{1,0},{2,3},{3,2},{4,5},{5,4},{6,7},{7,6},{8,9},{9,8},{10,11... | collective-permute-start | bytes 294920 | tf_op jit(solution)/shard_map/ppermute | solution.py:41
  91.2 3.3 %collective-permute-start.19 = (f32[2,8,512]{2,1,0:T(8,128)S(1)}, f32[2,8,512]{2,1,0:T(8,128)S(1)}, u32[]{:S(2)}, u32[]{:S(2)}) collective-permute-start(f32[2,8,512]{2,1,0:T(8,128)S(1)} %pair.3.refs_9_.refs_10_.refs_11_.refs_12_.refs_13_), channel_id=1, source_target_pairs={{0,126},{1,3},{2,0},{3,5},{4,2},{5,7},{6,4},{7,9},{8,6},{9,11},{10... | collective-permute-start | bytes 98312 | tf_op jit(solution)/shard_map/ppermute | solution.py:36
  94.5 6.0 %part0.1 = (f32[512,1024]{1,0:T(8,128)S(1)}, f32[512,1024]{1,0:T(8,128)S(1)}) custom-call(s32[9]{0:T(128)S(1)} %or_convert_fusion.flags.refs_0_, s32[1,512]{1,0:T(1,128)S(1)} %copy-done.5, f32[8,512]{1,0:T(8,128)S(1)} %get-tuple-element.181.pay.refs_2_, f32[8,512]{1,0:T(8,128)S(1)} %get-tuple-element.182.mine.refs_3_, f32[6,8,512]{2,1,0:T(8,128)S(1)} %near.1.refs_4_, ...), custom_call_target="tpu_custom_call" | custom-call | tf_op jit(solution)/shard_map/part0/pallas_call | solution.py:258
  100.5 3.7 %collective-permute-start.22 = (f32[2,8,512]{2,1,0:T(8,128)S(1)}, f32[2,8,512]{2,1,0:T(8,128)S(1)}, u32[]{:S(2)}, u32[]{:S(2)}) collective-permute-start(f32[2,8,512]{2,1,0:T(8,128)S(1)} %collective-permute-done.19.refs_10_), channel_id=1, source_target_pairs={{0,126},{1,3},{2,0},{3,5},{4,2},{5,7},{6,4},{7,9},{8,6},{9,11},{10... | collective-permute-start | bytes 98312 | tf_op jit(solution)/shard_map/ppermute | solution.py:36
  104.2 4.7 %part1.1 = (f32[512,1024]{1,0:T(8,128)S(1)}, f32[512,1024]{1,0:T(8,128)S(1)}) custom-call(s32[9]{0:T(128)S(1)} %or_convert_fusion.flags.refs_0_, s32[1,512]{1,0:T(1,128)S(1)} %copy-done.5, f32[8,512]{1,0:T(8,128)S(1)} %get-tuple-element.181.pay.refs_2_, f32[8,512]{1,0:T(8,128)S(1)} %get-tuple-element.182.mine.refs_3_, f32[6,8,512]{2,1,0:T(8,128)S(1)} %near.1.refs_4_, ...), custom_call_target="tpu_custom_call" | custom-call | tf_op jit(solution)/shard_map/part1/pallas_call | solution.py:258
  109.6 5.4 %collective-permute-done.25.refs_14_ = bf16[2,512,1024]{2,1,0:T(8,128)(2,1)S(1)} collective-permute-done((bf16[2,512,1024]{2,1,0:T(8,128)(2,1)S(1)}, bf16[2,512,1024]{2,1,0:T(8,128)(2,1)S(1)}, u32[]{:S(2)}, u32[]{:S(2)}) %collective-permute-start.25) | collective-permute-done | bytes 2097184 | tf_op jit(solution)/shard_map/ppermute | solution.py:36
  114.9 7.2 %part2.1 = (f32[512,1024]{1,0:T(8,128)S(1)}, f32[512,1024]{1,0:T(8,128)}) custom-call(s32[9]{0:T(128)S(1)} %or_convert_fusion.flags.refs_0_, s32[1,512]{1,0:T(1,128)S(1)} %copy-done.5, f32[8,512]{1,0:T(8,128)S(1)} %get-tuple-element.181.pay.refs_2_, f32[8,512]{1,0:T(8,128)S(1)} %get-tuple-element.182.mine.refs_3_, f32[6,8,512]{2,1,0:T(8,128)S(1)} %near.1.refs_4_, ...), custom_call_target="tpu_custom_call" | custom-call | tf_op jit(solution)/shard_map/part2/pallas_call | solution.py:258
  122.2 3.1 %part3.1 = f32[512,1024]{1,0:T(8,128)} custom-call(s32[9]{0:T(128)S(1)} %or_convert_fusion.flags.refs_0_, s32[1,512]{1,0:T(1,128)S(1)} %copy-done.5, f32[8,512]{1,0:T(8,128)S(1)} %get-tuple-element.181.pay.refs_2_, f32[8,512]{1,0:T(8,128)S(1)} %get-tuple-element.182.mine.refs_3_, f32[6,8,512]{2,1,0:T(8,128)S(1)} %near.1.refs_4_, ...), custom_call_target="tpu_custom_call" | custom-call | tf_op jit(solution)/shard_map/part3/pallas_call | solution.py:258
  (61 shorter events, 14.1 us)
Async XLA Ops:
  0.6 4.7 %collective-permute-start.1 = (bf16[512,1024]{1,0:T(8,128)(2,1)}, bf16[512,1024]{1,0:T(8,128)(2,1)S(1)}, u32[]{:S(2)}, u32[]{:S(2)}) collective-permute-start(bf16[512,1024]{1,0:T(8,128)(2,1)} %refs_15_.1), channel_id=1, source_target_pairs={{0,1},{1,0},{2,3},{3,2},{4,5},{5,4},{6,7},{7,6},{8,9},{9,8},{10,11... | collective-permute-start | bytes 3145736 | tf_op jit(solution)/shard_map/ppermute | solution.py:41
  0.7 13.3 %collective-permute-start.2 = (bf16[512,1024]{1,0:T(8,128)(2,1)}, bf16[512,1024]{1,0:T(8,128)(2,1)S(1)}, u32[]{:S(2)}, u32[]{:S(2)}) collective-permute-start(bf16[512,1024]{1,0:T(8,128)(2,1)} %queries.5), channel_id=1, source_target_pairs={{0,1},{1,0},{2,3},{3,2},{4,5},{5,4},{6,7},{7,6},{8,9},{9,8},{10,11... | collective-permute-start | bytes 3145736 | tf_op jit(solution)/shard_map/ppermute | solution.py:41
  1.2 21.8 %collective-permute-start = (bf16[512,1024]{1,0:T(8,128)(2,1)}, bf16[512,1024]{1,0:T(8,128)(2,1)S(1)}, u32[]{:S(2)}, u32[]{:S(2)}) collective-permute-start(bf16[512,1024]{1,0:T(8,128)(2,1)} %refs_15_.1), channel_id=1, source_target_pairs={{0,2},{1,127},{2,4},{3,1},{4,6},{5,3},{6,8},{7,5},{8,10},{9,7},{10... | collective-permute-start | bytes 3145736 | tf_op jit(solution)/shard_map/ppermute | solution.py:36
  5.3 28.9 %collective-permute-start.3 = (bf16[512,1024]{1,0:T(8,128)(2,1)S(1)}, bf16[512,1024]{1,0:T(8,128)(2,1)S(1)}, u32[]{:S(2)}, u32[]{:S(2)}) collective-permute-start(bf16[512,1024]{1,0:T(8,128)(2,1)S(1)} %collective-permute-done.1.refs_1_.refs_16_), channel_id=1, source_target_pairs={{0,2},{1,127},{2,4},{3,1},{4,6},{5,3},{6,8},{7,5},{8,10},{9,7},{10... | collective-permute-start | bytes 3145736 | tf_op jit(solution)/shard_map/ppermute | solution.py:36
  23.0 11.4 %collective-permute-start.5 = (bf16[512,1024]{1,0:T(8,128)(2,1)S(1)}, bf16[512,1024]{1,0:T(8,128)(2,1)S(1)}, u32[]{:S(2)}, u32[]{:S(2)}) collective-permute-start(bf16[512,1024]{1,0:T(8,128)(2,1)S(1)} %collective-permute-done.refs_0_.refs_16_), channel_id=1, source_target_pairs={{0,1},{1,0},{2,3},{3,2},{4,5},{5,4},{6,7},{7,6},{8,9},{9,8},{10,11... | collective-permute-start | bytes 3145736 | tf_op jit(solution)/shard_map/ppermute | solution.py:41
  23.0 22.5 %collective-permute-start.4 = (bf16[512,1024]{1,0:T(8,128)(2,1)S(1)}, bf16[512,1024]{1,0:T(8,128)(2,1)S(1)}, u32[]{:S(2)}, u32[]{:S(2)}) collective-permute-start(bf16[512,1024]{1,0:T(8,128)(2,1)S(1)} %collective-permute-done.refs_0_.refs_16_), channel_id=1, source_target_pairs={{0,2},{1,127},{2,4},{3,1},{4,6},{5,3},{6,8},{7,5},{8,10},{9,7},{10... | collective-permute-start | bytes 3145736 | tf_op jit(solution)/shard_map/ppermute | solution.py:36
  34.2 14.0 %collective-permute-start.6 = (bf16[512,1024]{1,0:T(8,128)(2,1)S(1)}, bf16[512,1024]{1,0:T(8,128)(2,1)S(1)}, u32[]{:S(2)}, u32[]{:S(2)}) collective-permute-start(bf16[512,1024]{1,0:T(8,128)(2,1)S(1)} %collective-permute-done.3.refs_0_.refs_18_), channel_id=1, source_target_pairs={{0,1},{1,0},{2,3},{3,2},{4,5},{5,4},{6,7},{7,6},{8,9},{9,8},{10,11... | collective-permute-start | bytes 3145736 | tf_op jit(solution)/shard_map/ppermute | solution.py:41
  34.2 22.5 %collective-permute-start.7 = (bf16[512,1024]{1,0:T(8,128)(2,1)S(1)}, bf16[512,1024]{1,0:T(8,128)(2,1)S(1)}, u32[]{:S(2)}, u32[]{:S(2)}) collective-permute-start(bf16[512,1024]{1,0:T(8,128)(2,1)S(1)} %collective-permute-done.3.refs_0_.refs_18_), channel_id=1, source_target_pairs={{0,2},{1,127},{2,4},{3,1},{4,6},{5,3},{6,8},{7,5},{8,10},{9,7},{10... | collective-permute-start | bytes 3145736 | tf_op jit(solution)/shard_map/ppermute | solution.py:36
  48.1 34.7 %collective-permute-start.20 = (bf16[2,512,1024]{2,1,0:T(8,128)(2,1)S(1)}, bf16[2,512,1024]{2,1,0:T(8,128)(2,1)S(1)}, u32[]{:S(2)}, u32[]{:S(2)}) collective-permute-start(bf16[2,512,1024]{2,1,0:T(8,128)(2,1)S(1)} %pair.2.queries.refs_17_), channel_id=1, source_target_pairs={{0,2},{1,127},{2,4},{3,1},{4,6},{5,3},{6,8},{7,5},{8,10},{9,7},{10... | collective-permute-start | bytes 6291464 | tf_op jit(solution)/shard_map/ppermute | solution.py:36
  56.7 3.5 %collective-permute-start.8 = (bf16[512,1024]{1,0:T(8,128)(2,1)S(1)}, bf16[512,1024]{1,0:T(8,128)(2,1)S(1)}, u32[]{:S(2)}, u32[]{:S(2)}) collective-permute-start(bf16[512,1024]{1,0:T(8,128)(2,1)S(1)} %collective-permute-done.7.refs_1_.refs_22_), channel_id=1, source_target_pairs={{0,1},{1,0},{2,3},{3,2},{4,5},{5,4},{6,7},{7,6},{8,9},{9,8},{10,11... | collective-permute-start | bytes 3145736 | tf_op jit(solution)/shard_map/ppermute | solution.py:41
  57.0 6.6 %collective-permute-start.9 = (f32[2,8,512]{2,1,0:T(8,128)S(1)}, f32[2,8,512]{2,1,0:T(8,128)S(1)}, u32[]{:S(2)}, u32[]{:S(2)}) collective-permute-start(f32[2,8,512]{2,1,0:T(8,128)S(1)} %get-tuple-element.151.refs_1_.st1), channel_id=1, source_target_pairs={{0,1},{1,0},{2,3},{3,2},{4,5},{5,4},{6,7},{7,6},{8,9},{9,8},{10,11... | collective-permute-start | bytes 98312 | tf_op jit(solution)/shard_map/ppermute | solution.py:41
  57.2 6.5 %collective-permute-start.10 = (f32[2,8,512]{2,1,0:T(8,128)S(1)}, f32[2,8,512]{2,1,0:T(8,128)S(1)}, u32[]{:S(2)}, u32[]{:S(2)}) collective-permute-start(f32[2,8,512]{2,1,0:T(8,128)S(1)} %get-tuple-element.152.refs_2_.st2), channel_id=1, source_target_pairs={{0,1},{1,0},{2,3},{3,2},{4,5},{5,4},{6,7},{7,6},{8,9},{9,8},{10,11... | collective-permute-start | bytes 98312 | tf_op jit(solution)/shard_map/ppermute | solution.py:41
  61.9 1.7 %collective-permute-start.11 = (f32[1,8,512]{2,1,0:T(8,128)S(1)}, f32[1,8,512]{2,1,0:T(8,128)S(1)}, u32[]{:S(2)}, u32[]{:S(2)}) collective-permute-start(f32[1,8,512]{2,1,0:T(8,128)S(1)} %get-tuple-element.158.refs_4_), channel_id=1, source_target_pairs={{0,1},{1,0},{2,3},{3,2},{4,5},{5,4},{6,7},{7,6},{8,9},{9,8},{10,11... | collective-permute-start | bytes 49160 | tf_op jit(solution)/shard_map/ppermute | solution.py:41
  64.5 9.4 %collective-permute-start.13 = (f32[6,8,512]{2,1,0:T(8,128)S(1)}, f32[6,8,512]{2,1,0:T(8,128)S(1)}, u32[]{:S(2)}, u32[]{:S(2)}) collective-permute-start(f32[6,8,512]{2,1,0:T(8,128)S(1)} %near.1.refs_4_), channel_id=1, source_target_pairs={{0,126},{1,3},{2,0},{3,5},{4,2},{5,7},{6,4},{7,9},{8,6},{9,11},{10... | collective-permute-start | bytes 294920 | tf_op jit(solution)/shard_map/ppermute | solution.py:36
  70.7 9.5 %collective-permute-start.15 = (f32[6,8,512]{2,1,0:T(8,128)S(1)}, f32[6,8,512]{2,1,0:T(8,128)S(1)}, u32[]{:S(2)}, u32[]{:S(2)}) collective-permute-start(f32[6,8,512]{2,1,0:T(8,128)S(1)} %near.1.refs_4_), channel_id=1, source_target_pairs={{0,124},{1,5},{2,126},{3,7},{4,0},{5,9},{6,2},{7,11},{8,4},{9,13},... | collective-permute-start | bytes 294920 | tf_op jit(solution)/shard_map/ppermute | solution.py:36
  73.9 6.3 %collective-permute-start.14 = (f32[6,8,512]{2,1,0:T(8,128)S(1)}, f32[6,8,512]{2,1,0:T(8,128)S(1)}, u32[]{:S(2)}, u32[]{:S(2)}) collective-permute-start(f32[6,8,512]{2,1,0:T(8,128)S(1)} %collective-permute-done.13.one.refs_5_), channel_id=1, source_target_pairs={{0,1},{1,0},{2,3},{3,2},{4,5},{5,4},{6,7},{7,6},{8,9},{9,8},{10,11... | collective-permute-start | bytes 294920 | tf_op jit(solution)/shard_map/ppermute | solution.py:41
  82.8 21.5 %collective-permute-start.23 = (bf16[2,512,1024]{2,1,0:T(8,128)(2,1)S(1)}, bf16[2,512,1024]{2,1,0:T(8,128)(2,1)S(1)}, u32[]{:S(2)}, u32[]{:S(2)}) collective-permute-start(bf16[2,512,1024]{2,1,0:T(8,128)(2,1)S(1)} %collective-permute-done.20.refs_19_), channel_id=1, source_target_pairs={{0,1},{1,0},{2,3},{3,2},{4,5},{5,4},{6,7},{7,6},{8,9},{9,8},{10,11... | collective-permute-start | bytes 6291464 | tf_op jit(solution)/shard_map/ppermute | solution.py:41
  82.8 32.2 %collective-permute-start.25 = (bf16[2,512,1024]{2,1,0:T(8,128)(2,1)S(1)}, bf16[2,512,1024]{2,1,0:T(8,128)(2,1)S(1)}, u32[]{:S(2)}, u32[]{:S(2)}) collective-permute-start(bf16[2,512,1024]{2,1,0:T(8,128)(2,1)S(1)} %collective-permute-done.20.refs_19_), channel_id=1, source_target_pairs={{0,2},{1,127},{2,4},{3,1},{4,6},{5,3},{6,8},{7,5},{8,10},{9,7},{10... | collective-permute-start | bytes 6291464 | tf_op jit(solution)/shard_map/ppermute | solution.py:36
  82.8 6.6 %collective-permute-start.17 = (f32[6,8,512]{2,1,0:T(8,128)S(1)}, f32[6,8,512]{2,1,0:T(8,128)S(1)}, u32[]{:S(2)}, u32[]{:S(2)}) collective-permute-start(f32[6,8,512]{2,1,0:T(8,128)S(1)} %collective-permute-done.15.two.refs_7_), channel_id=1, source_target_pairs={{0,1},{1,0},{2,3},{3,2},{4,5},{5,4},{6,7},{7,6},{8,9},{9,8},{10,11... | collective-permute-start | bytes 294920 | tf_op jit(solution)/shard_map/ppermute | solution.py:41
  91.2 9.3 %collective-permute-start.19 = (f32[2,8,512]{2,1,0:T(8,128)S(1)}, f32[2,8,512]{2,1,0:T(8,128)S(1)}, u32[]{:S(2)}, u32[]{:S(2)}) collective-permute-start(f32[2,8,512]{2,1,0:T(8,128)S(1)} %pair.3.refs_9_.refs_10_.refs_11_.refs_12_.refs_13_), channel_id=1, source_target_pairs={{0,126},{1,3},{2,0},{3,5},{4,2},{5,7},{6,4},{7,9},{8,6},{9,11},{10... | collective-permute-start | bytes 98312 | tf_op jit(solution)/shard_map/ppermute | solution.py:36
  100.5 8.5 %collective-permute-start.22 = (f32[2,8,512]{2,1,0:T(8,128)S(1)}, f32[2,8,512]{2,1,0:T(8,128)S(1)}, u32[]{:S(2)}, u32[]{:S(2)}) collective-permute-start(f32[2,8,512]{2,1,0:T(8,128)S(1)} %collective-permute-done.19.refs_10_), channel_id=1, source_target_pairs={{0,126},{1,3},{2,0},{3,5},{4,2},{5,7},{6,4},{7,9},{8,6},{9,11},{10... | collective-permute-start | bytes 98312 | tf_op jit(solution)/shard_map/ppermute | solution.py:36
  104.2 4.8 %collective-permute-start.21 = (f32[2,8,512]{2,1,0:T(8,128)S(1)}, f32[2,8,512]{2,1,0:T(8,128)S(1)}, u32[]{:S(2)}, u32[]{:S(2)}) collective-permute-start(f32[2,8,512]{2,1,0:T(8,128)S(1)} %collective-permute-done.19.refs_10_), channel_id=1, source_target_pairs={{0,1},{1,0},{2,3},{3,2},{4,5},{5,4},{6,7},{7,6},{8,9},{9,8},{10,11... | collective-permute-start | bytes 98312 | tf_op jit(solution)/shard_map/ppermute | solution.py:41
  109.0 6.0 %collective-permute-start.24 = (f32[2,8,512]{2,1,0:T(8,128)S(1)}, f32[2,8,512]{2,1,0:T(8,128)S(1)}, u32[]{:S(2)}, u32[]{:S(2)}) collective-permute-start(f32[2,8,512]{2,1,0:T(8,128)S(1)} %collective-permute-done.22.refs_12_), channel_id=1, source_target_pairs={{0,1},{1,0},{2,3},{3,2},{4,5},{5,4},{6,7},{7,6},{8,9},{9,8},{10,11... | collective-permute-start | bytes 98312 | tf_op jit(solution)/shard_map/ppermute | solution.py:41
  114.9 7.2 %collective-permute-start.26 = (bf16[2,512,1024]{2,1,0:T(8,128)(2,1)S(1)}, bf16[2,512,1024]{2,1,0:T(8,128)(2,1)S(1)}, u32[]{:S(2)}, u32[]{:S(2)}) collective-permute-start(bf16[2,512,1024]{2,1,0:T(8,128)(2,1)S(1)} %collective-permute-done.25.refs_14_), channel_id=1, source_target_pairs={{0,1},{1,0},{2,3},{3,2},{4,5},{5,4},{6,7},{7,6},{8,9},{9,8},{10,11... | collective-permute-start | bytes 6291464 | tf_op jit(solution)/shard_map/ppermute | solution.py:41
  (9 other events, 79.2 us)
